TPU v7x, 256 devices: a whole 4x4x8 slice. The times are simulated.
256 devices in a mesh: seq: 32 (over x, z), tensor: 8 (over y, core).
Axes of the slice: x: 4, y: 4, z: 8, core: 2. Of those that a mesh axis runs over, the one named last changes fastest.
Arguments:
- queries: bfloat16 [4608, 3072], P('seq', 'tensor'), may hold values from -60 to 60
- keys: bfloat16 [4608, 3072], P('seq', 'tensor'), may hold values from -60 to 60
- values: bfloat16 [4608, 3072], P('seq', 'tensor'), may hold values from -60 to 60
- out_grad: bfloat16 [4608, 3072], P('seq', 'tensor'), may hold values from -60 to 60
Outputs:
- out_scaled: bfloat16 [4608, 3072], P('seq', 'tensor')
- dq_scaled: bfloat16 [4608, 3072], P('seq', 'tensor')
- dk_scaled: bfloat16 [4608, 3072], P('seq', 'tensor')
- dv_scaled: bfloat16 [4608, 3072], P('seq', 'tensor')
All inputs are finite; a program needn't handle non-finite values. Where the computation divides by a largest or mean magnitude, that divisor is 1e-20 or more.
Results may differ from a plain program's by a relative error of at most 0.019.
The roundings to bfloat16 on the way count: a program that leaves them out, or rounds other values in their place, can miss the bound.
Values may be sent and summed in bfloat16 or wider, within the bound.
No kernel may reach another device: no remote copies, remote signals or barrier semaphores. Data moves between devices by JAX's collectives and lax.ppermute only.
A program may use at most 64 MiB of HBM per device.

v0:
```python
import math

import jax
import jax.numpy as jnp
from jax import lax
from jax.sharding import PartitionSpec as P

HD = 128


TOP = 4.0
LOWEST = -1e30


def local_peak(tensor):
    return jnp.max(jnp.abs(tensor)).astype(jnp.float32)


def to_scaled(tensor, peak):
    return (tensor.astype(jnp.float32) * (TOP / peak)).astype(jnp.bfloat16)


def by_blocks(advance, running, arrays, offset):
    total_rows = arrays[0].shape[0]
    block_rows = total_rows
    while block_rows > 512 and block_rows % 2 == 0:
        block_rows = block_rows // 2
    turn_count = total_rows // block_rows

    def one_turn(number, current):
        first_row = number * block_rows
        sliced = tuple(
            (lax.dynamic_slice_in_dim(member, first_row, block_rows, 0) for member in arrays)
        )
        return advance(current, sliced, offset + first_row)

    return lax.fori_loop(0, turn_count, one_turn, running)


def on_device(queries, keys, values, out_grad):
    query_count = queries.shape[0]
    head_count = queries.shape[1] // HD
    root_dim = math.sqrt(HD)
    peak_q, peak_k, peak_v = lax.pmax(
        (local_peak(queries), local_peak(keys), local_peak(values)), ("seq", "tensor")
    )
    query_cube = to_scaled(queries, peak_q).reshape(query_count, head_count, HD)
    key_cube = to_scaled(keys, peak_k).reshape(query_count, head_count, HD)
    value_cube = to_scaled(values, peak_v).reshape(query_count, head_count, HD)
    score_scale = peak_q * peak_k / (TOP * TOP * root_dim)

    def forward_block(running, sliced, offset):
        row_max, row_total, weighted = running
        key_block, value_block = sliced
        scores = (
            jnp.einsum("qhd,khd->hqk", query_cube, key_block, preferred_element_type=jnp.float32)
            * score_scale
        )
        new_max = jnp.maximum(row_max, jnp.max(scores, axis=2))
        shrink = jnp.exp(row_max - new_max)
        weights = jnp.exp(scores - new_max[:, :, None])
        row_total = row_total * shrink + jnp.sum(weights, axis=2)
        product = jnp.einsum(
            "hqk,khd->hqd",
            weights.astype(jnp.bfloat16),
            value_block,
            preferred_element_type=jnp.float32,
        )
        weighted = weighted * shrink[:, :, None] + product
        return (new_max, row_total, weighted)

    start_state = (
        jnp.full((head_count, query_count), LOWEST, jnp.float32),
        jnp.zeros((head_count, query_count), jnp.float32),
        jnp.zeros((head_count, query_count, HD), jnp.float32),
    )
    whole_keys, whole_values = (
        lax.all_gather(key_cube, "seq", axis=0, tiled=True),
        lax.all_gather(value_cube, "seq", axis=0, tiled=True),
    )
    row_max, row_total, weighted = by_blocks(
        forward_block, start_state, (whole_keys, whole_values), 0
    )
    attended = weighted / row_total[:, :, None] * (peak_v / TOP)
    log_total = row_max + jnp.log(row_total)
    peak_o, peak_g = lax.pmax((jnp.max(jnp.abs(attended)), local_peak(out_grad)), ("seq", "tensor"))
    grad_cube = to_scaled(out_grad, peak_g).reshape(query_count, head_count, HD)
    grad_rows = grad_cube.astype(jnp.float32) * (peak_g / TOP)
    row_delta = jnp.sum(jnp.transpose(grad_rows, (1, 0, 2)) * attended, axis=2)
    all_logs, all_deltas = (
        lax.all_gather(log_total, "seq", axis=1, tiled=True),
        lax.all_gather(row_delta, "seq", axis=1, tiled=True),
    )
    grad_scale = peak_g * peak_v / (TOP * TOP)

    def query_block(running, sliced, offset):
        key_block, value_block = sliced
        scores = (
            jnp.einsum("qhd,khd->hqk", query_cube, key_block, preferred_element_type=jnp.float32)
            * score_scale
        )
        prob_block = jnp.exp(scores - log_total[:, :, None])
        grad_probs = (
            jnp.einsum("qhd,khd->hqk", grad_cube, value_block, preferred_element_type=jnp.float32)
            * grad_scale
        )
        grad_scores = (prob_block * (grad_probs - row_delta[:, :, None])).astype(jnp.bfloat16)
        return running + jnp.einsum(
            "hqk,khd->hqd", grad_scores, key_block, preferred_element_type=jnp.float32
        )

    def key_block_grads(running, sliced, offset):
        grad_k, grad_v = running
        query_rows, grad_block = sliced
        piece_rows = query_rows.shape[0]
        piece_logs = lax.dynamic_slice_in_dim(all_logs, offset, piece_rows, 1)
        piece_deltas = lax.dynamic_slice_in_dim(all_deltas, offset, piece_rows, 1)
        scores = (
            jnp.einsum("qhd,khd->hqk", query_rows, key_cube, preferred_element_type=jnp.float32)
            * score_scale
        )
        prob_block = jnp.exp(scores - piece_logs[:, :, None])
        grad_v = grad_v + jnp.einsum(
            "hqk,qhd->hkd",
            prob_block.astype(jnp.bfloat16),
            grad_block,
            preferred_element_type=jnp.float32,
        )
        grad_probs = (
            jnp.einsum("qhd,khd->hqk", grad_block, value_cube, preferred_element_type=jnp.float32)
            * grad_scale
        )
        grad_scores = (prob_block * (grad_probs - piece_deltas[:, :, None])).astype(jnp.bfloat16)
        grad_k = grad_k + jnp.einsum(
            "hqk,qhd->hkd", grad_scores, query_rows, preferred_element_type=jnp.float32
        )
        return (grad_k, grad_v)

    zero_cube = jnp.zeros((head_count, query_count, HD), jnp.float32)
    grad_q = by_blocks(
        query_block,
        zero_cube,
        (
            lax.all_gather(key_cube, "seq", axis=0, tiled=True),
            lax.all_gather(value_cube, "seq", axis=0, tiled=True),
        ),
        jnp.int32(0),
    )
    grad_k, grad_v = by_blocks(
        key_block_grads,
        (zero_cube, zero_cube),
        (
            lax.all_gather(query_cube, "seq", axis=0, tiled=True),
            lax.all_gather(grad_cube, "seq", axis=0, tiled=True),
        ),
        jnp.int32(0),
    )
    grad_q = grad_q * (peak_k / (TOP * root_dim))
    grad_k = grad_k * (peak_q / (TOP * root_dim))
    grad_v = grad_v * (peak_g / TOP)
    peak_dq, peak_dk, peak_dv = lax.pmax(
        (jnp.max(jnp.abs(grad_q)), jnp.max(jnp.abs(grad_k)), jnp.max(jnp.abs(grad_v))),
        ("seq", "tensor"),
    )

    def flatten(cube, peak):
        flat = jnp.transpose(cube, (1, 0, 2)).reshape(query_count, head_count * HD)
        return (flat * (TOP / peak)).astype(jnp.bfloat16)

    return (
        flatten(attended, peak_o),
        flatten(grad_q, peak_dq),
        flatten(grad_k, peak_dk),
        flatten(grad_v, peak_dv),
    )


def solution(mesh):
    return jax.shard_map(
        on_device,
        mesh=mesh,
        in_specs=(P("seq", "tensor"), P("seq", "tensor"), P("seq", "tensor"), P("seq", "tensor")),
        out_specs=(P("seq", "tensor"), P("seq", "tensor"), P("seq", "tensor"), P("seq", "tensor")),
        check_vma=False,
    )
```

profile of v0, /device:TPU:1, one launch (start us, length us, event | category | flops | bytes accessed | tf_op | source)
XLA Modules:
  0.0 584.3 jit_solution(2246408057598765108)
XLA Ops:
  7.2 1.6 abs_reduce_fusion.6
  8.8 1.6 abs_reduce_fusion.4
  10.4 81.6 %all-reduce.1 = (f32[]{:T(128)}, f32[]{:T(128)}, f32[]{:T(128)}, f32[]{:T(128)}) all-reduce(bf16[]{:T(256)} %get-tuple-element.784, bf16[]{:T(256)} %get-tuple-element.783, bf16[]{:T(256)} %get-tuple-element.782, bf16[]{:T(256)} %get-tuple-element.781), channel_id=1, replica_groups=mesh['seq'=32,'tensor'=8] {'seq','tensor'}, use_global_device_ids=true, to_apply=%region_1.0 | all-reduce | flops 4 | bytes 24 | tf_op jit(solution)/shard_map/pmax | solution.py:44
  92.6 1.6 copy_bitcast_fusion.7
  94.9 1.6 copy_bitcast_fusion.5
  97.3 1.6 copy_bitcast_fusion.6
  99.5 1.6 copy_bitcast_fusion.4
  107.0 60.4 %all-gather.7.cloned.1.call-done = bf16[4608,3,128]{2,0,1:T(8,128)(2,1)} async-done(((bf16[144,3,128]{2,0,1:T(8,128)(2,1)}), bf16[4608,3,128]{2,0,1:T(8,128)(2,1)}) %all-gather.7.cloned.1.call-update) | async-done | bytes 3538960 | tf_op jit(solution)/shard_map/all_gather | solution.py:78
  167.4 80.7 %all-gather.9.cloned.1.call-done = bf16[4608,3,128]{2,0,1:T(8,128)(2,1)} async-done(((bf16[144,3,128]{2,0,1:T(8,128)(2,1)}), bf16[4608,3,128]{2,0,1:T(8,128)(2,1)}) %all-gather.9.cloned.1.call-update) | async-done | bytes 3538960 | tf_op jit(solution)/shard_map/all_gather | solution.py:79
  248.2 49.6 %while.48 = (s32[]{:T(128)}, f32[3,144]{1,0:T(4,128)S(1)}, f32[3,144]{1,0:T(4,128)S(1)}, f32[3,144,128]{2,1,0:T(8,128)S(1)}, bf16[4608,3,128]{2,0,1:T(8,128)(2,1...) while((s32[]{:T(128)}, f32[3,144]{1,0:T(4,128)S(1)}, ...), condition=%wide.region_9.0_spmd.clone, body=%wide.region_6.0_spmd.clone.sunk | while | flops 64615540 | bytes 2516671 | solution.py:37
  299.0 35.6 %all-gather = f32[32,144,3]{1,2,0:T(4,128)S(1)} all-gather(f32[1,144,3]{1,2,0:T(4,128)S(1)} %bitcast.78), channel_id=1, replica_groups=mesh['seq'=32,'tensor'=8] {'seq'}, dimensions={0}, use_global_device_ids=true | all-gather | bytes 57024 | tf_op jit(solution)/shard_map/all_gather | solution.py:91
  334.9 33.8 %all-gather.1 = f32[32,144,3]{1,2,0:T(4,128)S(1)} all-gather(f32[1,144,3]{1,2,0:T(4,128)S(1)} %copy.59), channel_id=1, replica_groups=mesh['seq'=32,'tensor'=8] {'seq'}, dimensions={0}, use_global_device_ids=true | all-gather | bytes 57024 | tf_op jit(solution)/shard_map/all_gather | solution.py:92
  368.9 45.3 %while.49 = (s32[]{:T(128)}, f32[3,144,128]{2,1,0:T(8,128)S(1)}, bf16[4608,3,128]{2,0,1:T(8,128)(2,1)}, bf16[144,3,128]{2,0,1:T(8,128)(2,1)}, f32[]{:T(128)}, /*...) while((s32[]{:T(128)}, f32[3,144,128]{2,1,0:T(8,128)S(1)}, ...), condition=%wide.region_16.0_spmd.clone, body=%wide.region_15.0_spmd.clone.sunk | while | flops 96408576 | bytes 2328648 | solution.py:37
  370.2 1.5 fusion.102
  373.0 1.5 fusion.102
  375.9 1.5 fusion.102
  378.7 1.5 fusion.102
  381.5 1.6 fusion.102
  384.4 1.5 fusion.102
  387.3 1.5 fusion.102
  390.1 1.5 fusion.102
  392.9 1.5 fusion.102
  395.7 1.5 fusion.102
  398.6 1.5 fusion.102
  404.2 1.5 fusion.102
  407.1 1.5 fusion.102
  409.9 1.5 fusion.102
  412.7 1.5 fusion.102
  414.3 64.5 %while.50 = (s32[]{:T(128)}, f32[3,144,128]{2,1,0:T(8,128)S(1)}, f32[3,144,128]{2,1,0:T(8,128)S(1)}, bf16[4608,3,128]{2,0,1:T(8,128)(2,1)}, bf16[144,3,128]{2,0,...) while((s32[]{:T(128)}, f32[3,144,128]{2,1,0:T(8,128)S(1)}, ...), condition=%wide.region_20.0_spmd.clone, body=%wide.region_19.0_spmd.clone.sunk | while | flops 128494080 | bytes 3507161 | solution.py:37
  419.6 1.5 fusion.111
  423.6 1.5 fusion.111
  480.7 91.6 %all-reduce = (f32[]{:T(128)}, f32[]{:T(128)}, f32[]{:T(128)}, f32[]{:T(128)}) all-reduce(f32[]{:T(128)} %get-tuple-element.707, f32[]{:T(128)} %abs_reduce_fusion.3, f32[]{:T(128)} %abs_reduce_fusion.2, f32[]{:T(128)} %abs_reduce_fusion.1), channel_id=1, replica_groups=mesh['seq'=32,'tensor'=8] {'seq','tensor'}, use_global_device_ids=true, to_apply=%region_11.0 | all-reduce | flops 4 | bytes 32 | tf_op jit(solution)/shard_map/pmax | solution.py:86
  (216 shorter events, 139.1 us)
Async XLA Ops:
  7.2 160.3 %all-gather.7.cloned.1.call-start = ((), (), s32[]{:S(2)}) async-start(), calls=%async_computation | async-start | bytes 3649536 | tf_op jit(solution)/shard_map/all_gather | solution.py:78
  94.2 153.9 %all-gather.9.cloned.1.call-start = ((), (), s32[]{:S(2)}) async-start(), calls=%async_computation.1 | async-start | bytes 3649536 | tf_op jit(solution)/shard_map/all_gather | solution.py:79
  96.5 317.7 %all-gather.11.cloned.1.call-start = ((), (), s32[]{:S(2)}) async-start(), calls=%async_computation.2 | async-start | bytes 3649536 | tf_op jit(solution)/shard_map/all_gather | solution.py:153
  98.8 315.4 %all-gather.13.cloned.1.call-start = ((), (), s32[]{:S(2)}) async-start(), calls=%async_computation.3 | async-start | bytes 3649536 | tf_op jit(solution)/shard_map/all_gather | solution.py:154
  248.2 120.7 %copy-start.2 = (bf16[144,3,128]{2,0,1:T(8,128)(2,1)S(1)}, bf16[144,3,128]{2,0,1:T(8,128)(2,1)}, u32[]{:S(2)}) copy-start(bf16[144,3,128]{2,0,1:T(8,128)(2,1)} %copy_bitcast_fusion.4) | copy-start | bytes 331780
  368.8 45.4 %copy-start = (bf16[144,3,128]{2,0,1:T(8,128)(2,1)S(1)}, bf16[144,3,128]{2,0,1:T(8,128)(2,1)}, u32[]{:S(2)}) copy-start(bf16[144,3,128]{2,0,1:T(8,128)(2,1)} %copy_bitcast_fusion.7) | copy-start | bytes 331780
  368.9 45.4 %copy-start.1 = (bf16[144,3,128]{2,0,1:T(8,128)(2,1)S(1)}, bf16[144,3,128]{2,0,1:T(8,128)(2,1)}, u32[]{:S(2)}) copy-start(bf16[144,3,128]{2,0,1:T(8,128)(2,1)} %copy_bitcast_fusion.5) | copy-start | bytes 331780
Sparse Core Ops, SparseCore 0:
  94.3 73.0 all-gather.6
  170.7 77.4 all-gather.8
  251.4 77.5 all-gather.10
  332.2 77.7 all-gather.12
where the time goes:
time: 588 us; the launch traced here: 584 us
  blocking collectives  243 us (41%)
  matrix products  150 us (26%)
  waiting for transfers between devices  141 us (24%)
  between operations  24.2 us (4%)
  other arithmetic  21.3 us (4%)
    pmax x1, blocking collectives, on_device(): lax.pmax((jnp.max(jnp.abs(attended)), local_peak(out_grad)), ('seq', 'ten...  91.6 us
    pmax x1, blocking collectives, on_device(): lax.pmax((local_peak(queries), local_peak(keys), local_peak(values)), ('s...  81.6 us
    all_gather x1, waiting for transfers between devices, on_device(): lax.all_gather(value_cube, 'seq', axis=0, tiled=True)  80.7 us
    all_gather x1, waiting for transfers between devices, on_device(): lax.all_gather(key_cube, 'seq', axis=0, tiled=True)  60.4 us
    all_gather x1, blocking collectives, on_device(): lax.all_gather(log_total, 'seq', axis=1, tiled=True)  35.6 us
    all_gather x1, blocking collectives, on_device(): lax.all_gather(row_delta, 'seq', axis=1, tiled=True)  33.8 us
    dot_general x16, matrix products, query_block(): jnp.einsum('hqk,khd->hqd', grad_scores, key_block, preferred_element_type...  24.1 us
    dot_general x16, matrix products, key_block_grads(): jnp.einsum('hqk,qhd->hkd', grad_scores, query_rows, preferred_element_typ...  23.9 us
  transfers between devices with their start and end apart: 4, of which 2 were waited for; matrix products, arithmetic and copies ran while one was open for 17% of the time, Pallas kernels for 0%

commit v1 on v0

v1 whole, which is shorter than its diff:
```python
import functools
import math

import jax
import jax.numpy as jnp
from jax import lax
from jax.experimental import pallas as pl
from jax.experimental.pallas import tpu as pltpu
from jax.sharding import Mesh
from jax.sharding import PartitionSpec as P

HD = 128
TOP = 4.0
ROOT = math.sqrt(HD)
NT = (((1,), (1,)), ((), ()))
TN = (((0,), (0,)), ((), ()))
NN = (((1,), (0,)), ((), ()))
F32 = jnp.float32
BF16 = jnp.bfloat16
VMEM_LIMIT = 48 * 1024 * 1024


def mxu(a, b, dims):
    return lax.dot_general(a, b, dims, preferred_element_type=F32)


def call(body, name, out_shape, args, scratch=(), flops=0, nbytes=0, exps=0):
    return pl.pallas_call(
        body,
        name=name,
        out_shape=out_shape,
        scratch_shapes=list(scratch),
        compiler_params=pltpu.CompilerParams(vmem_limit_bytes=VMEM_LIMIT),
        cost_estimate=pl.CostEstimate(flops=flops, bytes_accessed=nbytes, transcendentals=exps),
    )(*args)


def lanes_of(values):
    lane = lax.broadcasted_iota(jnp.int32, (1, 128), 1)
    row = jnp.zeros((1, 128), F32)
    for i, value in enumerate(values):
        row = jnp.where(lane == i, value, row)
    return row


def peak_lanes(ref):
    return jnp.max(ref[...], axis=0)


def biggest(x):
    return jnp.max(jnp.abs(x.astype(F32)), keepdims=True)


def prep_kernel(q_ref, k_ref, v_ref, g_ref, qg_ref, kv_ref, pk_ref):
    width = q_ref.shape[1]
    qg_ref[:, :width] = q_ref[...]
    qg_ref[:, width:] = g_ref[...]
    kv_ref[:, :width] = k_ref[...]
    kv_ref[:, width:] = v_ref[...]
    row = lanes_of([biggest(r[...]) for r in (q_ref, k_ref, v_ref, g_ref)])
    pk_ref[...] = jnp.broadcast_to(row[None], pk_ref.shape)


def scaled(x, factor):
    return (x.astype(F32) * factor).astype(BF16)


def load_keys(kv_refs, kb, vb, rk, rv):
    rows, width = kv_refs[0].shape[0], kb.shape[1]
    for s, ref in enumerate(kv_refs):
        kb[s * rows : (s + 1) * rows, :] = scaled(ref[:, :width], rk)
        vb[s * rows : (s + 1) * rows, :] = scaled(ref[:, width:], rv)


def forward_kernel(heads, tile, qg_ref, kv0, kv1, kv2, kv3, pk_ref, o_ref, st_ref, kb, vb):
    pk = peak_lanes(pk_ref)
    pq, pkk, pv, pg = (pk[:, i : i + 1] for i in range(4))
    load_keys((kv0, kv1, kv2, kv3), kb, vb, TOP / pkk, TOP / pv)
    score_scale = pq * pkk / (TOP * TOP * ROOT)
    width = heads * HD
    st_ref[...] = jnp.zeros_like(st_ref)
    for h in range(heads):
        cols = slice(h * HD, (h + 1) * HD)
        gcols = slice(width + h * HD, width + (h + 1) * HD)
        for t in range(qg_ref.shape[0] // tile):
            rows = slice(t * tile, (t + 1) * tile)
            q = scaled(qg_ref[rows, cols], TOP / pq)
            g = scaled(qg_ref[rows, gcols], TOP / pg)
            s = mxu(kb[:, cols], q, NT) * score_scale
            m = jnp.max(s, axis=0, keepdims=True)
            e = jnp.exp(s - m)
            total = jnp.sum(e, axis=0, keepdims=True)
            o = mxu(vb[:, cols], e.astype(BF16), TN) / total
            d = jnp.sum(o * g.T.astype(F32), axis=0, keepdims=True)
            o_ref[rows, cols] = o.astype(BF16).T
            lse = m + jnp.log(total)
            for p in range(st_ref.shape[0]):
                st_ref[p, 2 * h : 2 * h + 1, rows] = lse
                st_ref[p, 2 * h + 1 : 2 * h + 2, rows] = d


def backward_kernel(heads, tile, qg_ref, kv0, kv1, kv2, kv3, pk_ref, st_ref, dq_ref, dk_ref, dv_ref, kb, vb):
    pk = peak_lanes(pk_ref)
    pq, pkk, pv, pg = (pk[:, i : i + 1] for i in range(4))
    load_keys((kv0, kv1, kv2, kv3), kb, vb, TOP / pkk, TOP / pv)
    score_scale = pq * pkk / (TOP * TOP * ROOT)
    grad_scale = pg * pv / (TOP * TOP)
    width = heads * HD
    for h in range(heads):
        cols = slice(h * HD, (h + 1) * HD)
        gcols = slice(width + h * HD, width + (h + 1) * HD)
        lse = st_ref[:, 2 * h, :]
        top = jnp.max(lse, axis=0, keepdims=True)
        log_total = top + jnp.log(jnp.sum(jnp.exp(lse - top), axis=0, keepdims=True))
        delta = jnp.sum(jnp.exp(lse - log_total) * st_ref[:, 2 * h + 1, :], axis=0, keepdims=True)
        delta = delta * grad_scale
        dk = jnp.zeros((kb.shape[0], HD), F32)
        dv = jnp.zeros((kb.shape[0], HD), F32)
        for t in range(qg_ref.shape[0] // tile):
            rows = slice(t * tile, (t + 1) * tile)
            q = scaled(qg_ref[rows, cols], TOP / pq)
            g = scaled(qg_ref[rows, gcols], TOP / pg)
            s = mxu(kb[:, cols], q, NT) * score_scale
            p = jnp.exp(s - log_total[:, rows])
            dv = dv + mxu(p.astype(BF16), g, NN)
            dp = mxu(vb[:, cols], g, NT) * grad_scale
            ds = (p * (dp - delta[:, rows])).astype(BF16)
            dk = dk + mxu(ds, q, NN)
            dq = mxu(kb[:, cols], ds, TN) * (pkk / (TOP * ROOT))
            dq_ref[rows, cols] = dq.astype(BF16).T
        dk_ref[:, cols] = (dk * (pq / (TOP * ROOT))).astype(BF16)
        dv_ref[:, cols] = (dv * (pg / TOP)).astype(BF16)


def attended_kernel(heads, o_ref, w_ref, pk_ref, out_ref):
    pk = peak_lanes(pk_ref)
    factor = pk[:, 2:3] / TOP
    for h in range(heads):
        cols = slice(h * HD, (h + 1) * HD)
        total = jnp.zeros((o_ref.shape[1], HD), F32)
        for p in range(o_ref.shape[0]):
            total = total + w_ref[p, :, h : h + 1] * o_ref[p, :, cols].astype(F32)
        out_ref[:, cols] = total * factor


def sums_kernel(at_ref, dq_ref, dk0, dk1, dk2, dk3, dv0, dv1, dv2, dv3, gq_ref, gk_ref, gv_ref, pk_ref):
    gq = dq_ref[0].astype(F32)
    for p in range(1, dq_ref.shape[0]):
        gq = gq + dq_ref[p].astype(F32)
    gk = (dk0[...].astype(F32) + dk1[...].astype(F32)) + (dk2[...].astype(F32) + dk3[...].astype(F32))
    gv = (dv0[...].astype(F32) + dv1[...].astype(F32)) + (dv2[...].astype(F32) + dv3[...].astype(F32))
    gq_ref[...] = gq
    gk_ref[...] = gk
    gv_ref[...] = gv
    row = lanes_of([biggest(x) for x in (at_ref[...], gq, gk, gv)])
    pk_ref[...] = jnp.broadcast_to(row[None], pk_ref.shape)


def cast_kernel(at_ref, gq_ref, gk_ref, gv_ref, pk_ref, o0, o1, o2, o3):
    pk = peak_lanes(pk_ref)
    for i, (src, dst) in enumerate(((at_ref, o0), (gq_ref, o1), (gk_ref, o2), (gv_ref, o3))):
        dst[...] = scaled(src[...], TOP / pk[:, i : i + 1])


def shift(n, s):
    return [(i, (i + s) % n) for i in range(n)]


def on_device(sizes, queries, keys, values, out_grad):
    nx, nz, everyone = sizes["x"], sizes["z"], math.prod(sizes.values())
    axes = ("x", "z", "y", "c")
    rows, width = queries.shape
    heads = width // HD
    q_rows, k_rows = rows * nz, rows * nx
    pairs = q_rows * k_rows * heads
    tile = q_rows // 3
    peaks = jax.ShapeDtypeStruct((everyone, 1, 128), F32)
    block = jax.ShapeDtypeStruct((rows, width), F32)
    wide = jax.ShapeDtypeStruct((rows, 2 * width), BF16)

    qg, kv, pk = call(prep_kernel, "prep", (wide, wide, peaks), (queries, keys, values, out_grad), nbytes=2**20)
    kvs = [kv] + [lax.ppermute(kv, "x", shift(nx, s)) for s in range(1, nx)]
    qg_all = lax.all_gather(qg, "z", axis=0, tiled=True)
    pk = lax.all_to_all(pk, axes, 0, 0, tiled=True)

    key_scratch = [pltpu.VMEM((k_rows, width), BF16)] * 2
    o, stats = call(
        functools.partial(forward_kernel, heads, tile),
        "forward",
        (
            jax.ShapeDtypeStruct((q_rows, width), BF16),
            jax.ShapeDtypeStruct((nz, 8, q_rows), F32),
        ),
        (qg_all, *kvs, pk),
        key_scratch,
        flops=4 * pairs * HD,
        nbytes=4 * 2**20,
        exps=pairs,
    )
    stats = lax.all_to_all(stats, "z", 0, 0, tiled=True)
    o = lax.all_to_all(o.reshape(nz, rows, width), "z", 0, 0, tiled=True)
    dq, dk, dv = call(
        functools.partial(backward_kernel, heads, tile),
        "backward",
        (
            jax.ShapeDtypeStruct((q_rows, width), BF16),
            jax.ShapeDtypeStruct((k_rows, width), BF16),
            jax.ShapeDtypeStruct((k_rows, width), BF16),
        ),
        (qg_all, *kvs, pk, stats),
        key_scratch,
        flops=10 * pairs * HD,
        nbytes=6 * 2**20,
        exps=pairs,
    )
    home = lambda d: [d[:rows]] + [
        lax.ppermute(d[s * rows : (s + 1) * rows], "x", shift(nx, nx - s)) for s in range(1, nx)
    ]
    dvs, dks = home(dv), home(dk)
    dq = lax.all_to_all(dq.reshape(nz, rows, width), "z", 0, 0, tiled=True)

    own = lax.dynamic_slice_in_dim(stats, lax.axis_index("z") * rows, rows, 2)[:, 0 : 2 * heads : 2]
    weights = jnp.transpose(jax.nn.softmax(own, axis=0), (0, 2, 1))
    attended = call(functools.partial(attended_kernel, heads), "attended", block, (o, weights, pk), nbytes=2**20)
    gq, gk, gv, tops = call(
        sums_kernel, "sums", (block, block, block, peaks), (attended, dq, *dks, *dvs), nbytes=3 * 2**20
    )
    tops = lax.all_to_all(tops, axes, 0, 0, tiled=True)
    result = jax.ShapeDtypeStruct((rows, width), BF16)
    return call(cast_kernel, "cast", (result,) * 4, (attended, gq, gk, gv, tops), nbytes=2**20)


def solution(mesh):
    sizes = dict(x=4, z=8, y=4, c=2)
    fine = Mesh(mesh.devices.reshape(tuple(sizes.values())), tuple(sizes))
    spec = P(("x", "z"), ("y", "c"))
    return jax.shard_map(
        functools.partial(on_device, sizes),
        mesh=fine,
        in_specs=(spec,) * 4,
        out_specs=(spec,) * 4,
        check_vma=False,
    )
```

time: 588 us -> 161 us (0.27)
  blocking collectives: 243 us -> 36.9 us
  matrix products: 150 us -> 0 us
  waiting for transfers between devices: 141 us -> 49 us
  starting transfers between devices: 0.16 us -> 35 us
  other arithmetic: 21.3 us -> 0.07 us
  Pallas kernels: 0 us -> 17.2 us
  between operations: 24.2 us -> 14.1 us
    pmax x2 -> x0, blocking collectives: 173 us -> none  [the longest x1 91.6 us: on_device(): lax.pmax((jnp.max(jnp.abs(attended)), local_peak(out_grad)), ('seq', 'ten...]
    dot_general x112 -> x0, matrix products: 150 us -> none  [the longest x16 24.1 us: query_block(): jnp.einsum('hqk,khd->hqd', grad_scores, key_block, preferred_element_type...]
    all_gather x4 -> x1, waiting for transfers between devices: 141 us -> 12.6 us  [on_device(): qg_all = lax.all_gather(qg, 'z', axis=0, tiled=True)]
    all_gather x2 -> x0, blocking collectives: 69.5 us -> none  [the longest x1 35.6 us: on_device(): lax.all_gather(log_total, 'seq', axis=1, tiled=True)]
    all_to_all x0 -> x2, blocking collectives: none -> 36.9 us  [the longest x1 23.5 us: on_device(): tops = lax.all_to_all(tops, axes, 0, 0, tiled=True)]
    all_to_all x0 -> x3, starting transfers between devices: none -> 22.9 us  [the longest x1 15.7 us: on_device(): pk = lax.all_to_all(pk, axes, 0, 0, tiled=True)]
    all_to_all x0 -> x3, waiting for transfers between devices: none -> 19.7 us  [the longest x1 13.1 us: on_device(): o = lax.all_to_all(o.reshape(nz, rows, width), 'z', 0, 0, tiled=True)]
    pallas_call x0 -> x6, Pallas kernels: none -> 17.2 us  [call(): pl.pallas_call(body, name=name, out_shape=out_shape, scratch_shapes=list(...]
  transfers between devices with their start and end apart: 4 -> 13, of which waited for: 2 -> 9; matrix products, arithmetic and copies ran while one was open for 17% -> 1% of each run, Pallas kernels for 0% -> 5%
where the time goes in v1:
time: 161 us
  waiting for transfers between devices  49 us (30%)
  blocking collectives  36.9 us (23%)
  starting transfers between devices  35 us (22%)
  Pallas kernels  17.2 us (11%)
  between operations  14.1 us (9%)
  local copies, waits for them, and re-layouts  8.36 us (5%)
    all_to_all x1, blocking collectives, on_device(): tops = lax.all_to_all(tops, axes, 0, 0, tiled=True)  23.5 us
    pallas_call x6, Pallas kernels, call(): pl.pallas_call(body, name=name, out_shape=out_shape, scratch_shapes=list(...  17.2 us
    all_to_all x1, starting transfers between devices, on_device(): pk = lax.all_to_all(pk, axes, 0, 0, tiled=True)  15.7 us
    all_to_all x1, blocking collectives, on_device(): stats = lax.all_to_all(stats, 'z', 0, 0, tiled=True)  13.4 us
    all_to_all x1, waiting for transfers between devices, on_device(): o = lax.all_to_all(o.reshape(nz, rows, width), 'z', 0, 0, tiled=True)  13.1 us
    all_gather x1, waiting for transfers between devices, on_device(): qg_all = lax.all_gather(qg, 'z', axis=0, tiled=True)  12.6 us
    ppermute x3, waiting for transfers between devices, on_device(): kvs = [kv] + [lax.ppermute(kv, 'x', shift(nx, s)) for s in range(1, nx)]  9.96 us
    ppermute x6, starting transfers between devices, on_device(): lax.ppermute(d[s * rows:(s + 1) * rows], 'x', shift(nx, nx - s))  6.97 us
  transfers between devices with their start and end apart: 13, of which 9 were waited for; matrix products, arithmetic and copies ran while one was open for 1% of the time, Pallas kernels for 5%

profile of v1, /device:TPU:1, one launch (start us, length us, event | category | flops | bytes accessed | tf_op | source)
XLA Modules:
  0.0 160.7 jit_solution(6958010068492015229)
XLA Ops:
  7.2 0.9 copy-done
  8.1 0.9 copy-done.1
  9.0 0.9 copy-done.2
  9.9 0.9 copy-done.3
  10.8 0.9 prep.1
  11.7 15.7 %all-to-all-start = ((f32[256,1,128]{2,1,0:T(1,128)}), f32[256,1,128]{2,1,0:T(1,128)S(1)}, u32[]{:S(2)}, u32[]{:S(2)}) async-start(f32[256,1,128]{2,1,0:T(1,128)} %get-tuple-element.18), calls=%async_computation | async-start | bytes 262144 | tf_op jit(solution)/shard_map/all_to_all | solution.py:184
  27.4 1.5 collective-permute-start
  28.9 2.4 %collective-permute-start.1 = (bf16[144,768]{1,0:T(8,128)(2,1)S(1)}, bf16[144,768]{1,0:T(8,128)(2,1)S(1)}, u32[]{:S(2)}, u32[]{:S(2)}) collective-permute-start(bf16[144,768]{1,0:T(8,128)(2,1)S(1)} %get-tuple-element.17.kv0), channel_id=1, source_target_pairs={{0,128},{64,192},{128,0},{192,64},{1,129},{65,193},{129,1},{193,65... | collective-permute-start | bytes 663560 | tf_op jit(solution)/shard_map/ppermute | solution.py:182
  31.3 1.2 collective-permute-start.2
  32.4 1.9 %collective-permute-done.kv1 = bf16[144,768]{1,0:T(8,128)(2,1)S(1)} collective-permute-done((bf16[144,768]{1,0:T(8,128)(2,1)S(1)}, bf16[144,768]{1,0:T(8,128)(2,1)S(1)}, u32[]{:S(2)}, u32[]{:S(2)}) %collective-permute-start) | collective-permute-done | bytes 221216 | tf_op jit(solution)/shard_map/ppermute | solution.py:182
  34.4 8.0 %collective-permute-done.1.kv2 = bf16[144,768]{1,0:T(8,128)(2,1)S(1)} collective-permute-done((bf16[144,768]{1,0:T(8,128)(2,1)S(1)}, bf16[144,768]{1,0:T(8,128)(2,1)S(1)}, u32[]{:S(2)}, u32[]{:S(2)}) %collective-permute-start.1) | collective-permute-done | bytes 221216 | tf_op jit(solution)/shard_map/ppermute | solution.py:182
  42.4 12.6 %all-gather.2.cloned.1.call-done.qg_ref = bf16[1152,768]{1,0:T(8,128)(2,1)} async-done(((bf16[144,768]{1,0:T(8,128)(2,1)}), bf16[1152,768]{1,0:T(8,128)(2,1)}) %all-gather.2.cloned.1.call-update) | async-done | bytes 1769488 | tf_op jit(solution)/shard_map/all_gather | solution.py:183
  55.0 1.5 copy-done.4
  56.5 6.3 %forward.1 = (bf16[1152,384]{1,0:T(8,128)(2,1)}, f32[8,8,1152]{2,1,0:T(8,128)S(1)}) custom-call(bf16[1152,768]{1,0:T(8,128)(2,1)S(1)} %copy-done.4, bf16[144,768]{1,0:T(8,128)(2,1)S(1)} %get-tuple-element.17.kv0, bf16[144,768]{1,0:T(8,128)(2,1)S(1)} %collective-permute-done.kv1, bf16[144,768]{1,0:T(8,128)(2,1)S(1)} %collective-permute-done.1.kv2, ...), custom_call_target="tpu_custom_call" | custom-call | flops 1019215872 | bytes 4194304 | tf_op jit(solution)/shard_map/forward/pallas_call | solution.py:28
  62.8 13.4 %all_to_all.25.st_ref = f32[8,8,1152]{2,1,0:T(8,128)S(1)} all-to-all(f32[8,8,1152]{2,1,0:T(8,128)S(1)} %get-tuple-element.20), channel_id=1, replica_groups=mesh['x'=4,'z'=8,'y'=4,'c'=2] {'z'}, dimensions={0} | all-to-all | bytes 589824 | tf_op jit(solution)/shard_map/all_to_all | solution.py:200
  76.1 3.7 %all-to-all-start.1 = ((bf16[8,144,384]{2,1,0:T(8,128)(2,1)}), bf16[8,144,384]{2,1,0:T(8,128)(2,1)S(1)}, u32[]{:S(2)}, u32[]{:S(2)}) async-start(bf16[8,144,384]{2,1,0:T(8,128)(2,1)} %bitcast), calls=%async_computation.1 | async-start | bytes 1769472 | tf_op jit(solution)/shard_map/all_to_all | solution.py:201
  79.9 1.5 copy-done.5
  81.3 7.2 %backward.1 = (bf16[1152,384]{1,0:T(8,128)(2,1)}, bf16[576,384]{1,0:T(8,128)(2,1)S(1)}, bf16[576,384]{1,0:T(8,128)(2,1)S(1)}) custom-call(bf16[1152,768]{1,0:T(8,128)(2,1)S(1)} %copy-done.5, bf16[144,768]{1,0:T(8,128)(2,1)S(1)} %get-tuple-element.17.kv0, bf16[144,768]{1,0:T(8,128)(2,1)S(1)} %collective-permute-done.kv1, ...), custom_call_target="tpu_custom_call" | custom-call | flops 2548039680 | bytes 6291456 | tf_op jit(solution)/shard_map/backward/pallas_call | solution.py:28
  88.6 13.1 %all-to-all-done.1.o_ref = bf16[8,144,384]{2,1,0:T(8,128)(2,1)S(1)} async-done(((bf16[8,144,384]{2,1,0:T(8,128)(2,1)}), bf16[8,144,384]{2,1,0:T(8,128)(2,1)S(1)}, u32[]{:S(2)}, u32[]{:S(2)}) %all-to-all-start.1) | async-done | bytes 884768 | tf_op jit(solution)/shard_map/all_to_all | solution.py:201
  101.6 3.6 %all-to-all-start.3 = ((bf16[8,144,384]{2,1,0:T(8,128)(2,1)}), bf16[8,144,384]{2,1,0:T(8,128)(2,1)S(1)}, u32[]{:S(2)}, u32[]{:S(2)}) async-start(bf16[8,144,384]{2,1,0:T(8,128)(2,1)} %bitcast.2), calls=%async_computation.3 | async-start | bytes 1769472 | tf_op jit(solution)/shard_map/all_to_all | solution.py:220
  105.3 0.7 fusion.2
  106.0 2.4 %collective-permute-start.3 = (bf16[144,384]{1,0:T(8,128)(2,1)S(1)}, bf16[144,384]{1,0:T(8,128)(2,1)S(1)}, u32[]{:S(2)}, u32[]{:S(2)}) collective-permute-start(bf16[144,384]{1,0:T(8,128)(2,1)S(1)} %get-tuple-element.34), channel_id=1, source_target_pairs={{0,192},{64,0},{128,64},{192,128},{1,193},{65,1},{129,65},{193,129... | collective-permute-start | bytes 331784 | tf_op jit(solution)/shard_map/ppermute | solution.py:217
  109.6 0.7 fusion.1
  110.4 2.0 %collective-permute-start.6 = (bf16[144,384]{1,0:T(8,128)(2,1)}, bf16[144,384]{1,0:T(8,128)(2,1)S(1)}, u32[]{:S(2)}, u32[]{:S(2)}) collective-permute-start(bf16[144,384]{1,0:T(8,128)(2,1)} %get-tuple-element.30), channel_id=1, source_target_pairs={{0,192},{64,0},{128,64},{192,128},{1,193},{65,1},{129,65},{193,129... | collective-permute-start | bytes 331784 | tf_op jit(solution)/shard_map/ppermute | solution.py:217
  112.4 1.3 collective-permute-start.7
  115.0 2.4 %collective-permute-done.6.dv1 = bf16[144,384]{1,0:T(8,128)(2,1)S(1)} collective-permute-done((bf16[144,384]{1,0:T(8,128)(2,1)}, bf16[144,384]{1,0:T(8,128)(2,1)S(1)}, u32[]{:S(2)}, u32[]{:S(2)}) %collective-permute-start.6) | collective-permute-done | bytes 110624 | tf_op jit(solution)/shard_map/ppermute | solution.py:217
  117.3 1.9 %collective-permute-done.7.dv2 = bf16[144,384]{1,0:T(8,128)(2,1)S(1)} collective-permute-done((bf16[144,384]{1,0:T(8,128)(2,1)}, bf16[144,384]{1,0:T(8,128)(2,1)S(1)}, u32[]{:S(2)}, u32[]{:S(2)}) %collective-permute-start.7) | collective-permute-done | bytes 110624 | tf_op jit(solution)/shard_map/ppermute | solution.py:217
  119.2 2.2 %collective-permute-done.8.dv3 = bf16[144,384]{1,0:T(8,128)(2,1)} collective-permute-done((bf16[144,384]{1,0:T(8,128)(2,1)}, bf16[144,384]{1,0:T(8,128)(2,1)}, u32[]{:S(2)}, u32[]{:S(2)}) %collective-permute-start.8) | collective-permute-done | bytes 110624 | tf_op jit(solution)/shard_map/ppermute | solution.py:217
  121.4 6.7 %all-to-all-done.3.dq_ref = bf16[8,144,384]{2,1,0:T(8,128)(2,1)S(1)} async-done(((bf16[8,144,384]{2,1,0:T(8,128)(2,1)}), bf16[8,144,384]{2,1,0:T(8,128)(2,1)S(1)}, u32[]{:S(2)}, u32[]{:S(2)}) %all-to-all-start.3) | async-done | bytes 884768 | tf_op jit(solution)/shard_map/all_to_all | solution.py:220
  128.1 1.3 sums.1
  129.4 23.5 %all_to_all.26.pk_ref = f32[256,1,128]{2,1,0:T(1,128)S(1)} all-to-all(f32[256,1,128]{2,1,0:T(1,128)S(1)} %get-tuple-element.27), channel_id=1, replica_groups=mesh['x'=4,'z'=8,'y'=4,'c'=2] {'x','z','y','c'}, dimensions={0} | all-to-all | bytes 262144 | tf_op jit(solution)/shard_map/all_to_all | solution.py:228
  152.9 0.9 cast.1
  (23 shorter events, 2.6 us)
Async XLA Ops:
  7.2 47.8 %all-gather.2.cloned.1.call-start = ((), (), s32[]{:S(2)}) async-start(), calls=%async_computation.5 | async-start | bytes 1990656 | tf_op jit(solution)/shard_map/all_gather | solution.py:183
  7.2 0.9 copy-start
  8.1 0.9 copy-start.1
  9.0 0.9 copy-start.2
  9.9 0.9 copy-start.3
  11.7 30.7 %all-to-all-start = ((f32[256,1,128]{2,1,0:T(1,128)}), f32[256,1,128]{2,1,0:T(1,128)S(1)}, u32[]{:S(2)}, u32[]{:S(2)}) async-start(f32[256,1,128]{2,1,0:T(1,128)} %get-tuple-element.18), calls=%async_computation | async-start | bytes 262144 | tf_op jit(solution)/shard_map/all_to_all | solution.py:184
  27.4 7.0 %collective-permute-start = (bf16[144,768]{1,0:T(8,128)(2,1)S(1)}, bf16[144,768]{1,0:T(8,128)(2,1)S(1)}, u32[]{:S(2)}, u32[]{:S(2)}) collective-permute-start(bf16[144,768]{1,0:T(8,128)(2,1)S(1)} %get-tuple-element.17.kv0), channel_id=1, source_target_pairs={{0,64},{64,128},{128,192},{192,0},{1,65},{65,129},{129,193},{193,1... | collective-permute-start | bytes 663560 | tf_op jit(solution)/shard_map/ppermute | solution.py:182
  28.9 13.5 %collective-permute-start.1 = (bf16[144,768]{1,0:T(8,128)(2,1)S(1)}, bf16[144,768]{1,0:T(8,128)(2,1)S(1)}, u32[]{:S(2)}, u32[]{:S(2)}) collective-permute-start(bf16[144,768]{1,0:T(8,128)(2,1)S(1)} %get-tuple-element.17.kv0), channel_id=1, source_target_pairs={{0,128},{64,192},{128,0},{192,64},{1,129},{65,193},{129,1},{193,65... | collective-permute-start | bytes 663560 | tf_op jit(solution)/shard_map/ppermute | solution.py:182
  31.3 11.1 %collective-permute-start.2 = (bf16[144,768]{1,0:T(8,128)(2,1)S(1)}, bf16[144,768]{1,0:T(8,128)(2,1)S(1)}, u32[]{:S(2)}, u32[]{:S(2)}) collective-permute-start(bf16[144,768]{1,0:T(8,128)(2,1)S(1)} %get-tuple-element.17.kv0), channel_id=1, source_target_pairs={{0,192},{64,0},{128,64},{192,128},{1,193},{65,1},{129,65},{193,129... | collective-permute-start | bytes 663560 | tf_op jit(solution)/shard_map/ppermute | solution.py:182
  55.0 1.5 copy-start.4
  76.1 25.5 %all-to-all-start.1 = ((bf16[8,144,384]{2,1,0:T(8,128)(2,1)}), bf16[8,144,384]{2,1,0:T(8,128)(2,1)S(1)}, u32[]{:S(2)}, u32[]{:S(2)}) async-start(bf16[8,144,384]{2,1,0:T(8,128)(2,1)} %bitcast), calls=%async_computation.1 | async-start | bytes 1769472 | tf_op jit(solution)/shard_map/all_to_all | solution.py:201
  79.9 1.5 copy-start.5
  101.6 26.4 %all-to-all-start.3 = ((bf16[8,144,384]{2,1,0:T(8,128)(2,1)}), bf16[8,144,384]{2,1,0:T(8,128)(2,1)S(1)}, u32[]{:S(2)}, u32[]{:S(2)}) async-start(bf16[8,144,384]{2,1,0:T(8,128)(2,1)} %bitcast.2), calls=%async_computation.3 | async-start | bytes 1769472 | tf_op jit(solution)/shard_map/all_to_all | solution.py:220
  106.0 7.7 %collective-permute-start.3 = (bf16[144,384]{1,0:T(8,128)(2,1)S(1)}, bf16[144,384]{1,0:T(8,128)(2,1)S(1)}, u32[]{:S(2)}, u32[]{:S(2)}) collective-permute-start(bf16[144,384]{1,0:T(8,128)(2,1)S(1)} %get-tuple-element.34), channel_id=1, source_target_pairs={{0,192},{64,0},{128,64},{192,128},{1,193},{65,1},{129,65},{193,129... | collective-permute-start | bytes 331784 | tf_op jit(solution)/shard_map/ppermute | solution.py:217
  108.5 6.2 %collective-permute-start.4 = (bf16[144,384]{1,0:T(8,128)(2,1)}, bf16[144,384]{1,0:T(8,128)(2,1)S(1)}, u32[]{:S(2)}, u32[]{:S(2)}) collective-permute-start(bf16[144,384]{1,0:T(8,128)(2,1)} %get-tuple-element.33), channel_id=1, source_target_pairs={{0,128},{64,192},{128,0},{192,64},{1,129},{65,193},{129,1},{193,65... | collective-permute-start | bytes 331784 | tf_op jit(solution)/shard_map/ppermute | solution.py:217
  109.0 6.0 %collective-permute-start.5 = (bf16[144,384]{1,0:T(8,128)(2,1)}, bf16[144,384]{1,0:T(8,128)(2,1)S(1)}, u32[]{:S(2)}, u32[]{:S(2)}) collective-permute-start(bf16[144,384]{1,0:T(8,128)(2,1)} %get-tuple-element.32), channel_id=1, source_target_pairs={{0,64},{64,128},{128,192},{192,0},{1,65},{65,129},{129,193},{193,1... | collective-permute-start | bytes 331784 | tf_op jit(solution)/shard_map/ppermute | solution.py:217
  110.4 7.0 %collective-permute-start.6 = (bf16[144,384]{1,0:T(8,128)(2,1)}, bf16[144,384]{1,0:T(8,128)(2,1)S(1)}, u32[]{:S(2)}, u32[]{:S(2)}) collective-permute-start(bf16[144,384]{1,0:T(8,128)(2,1)} %get-tuple-element.30), channel_id=1, source_target_pairs={{0,192},{64,0},{128,64},{192,128},{1,193},{65,1},{129,65},{193,129... | collective-permute-start | bytes 331784 | tf_op jit(solution)/shard_map/ppermute | solution.py:217
  112.4 6.8 %collective-permute-start.7 = (bf16[144,384]{1,0:T(8,128)(2,1)}, bf16[144,384]{1,0:T(8,128)(2,1)S(1)}, u32[]{:S(2)}, u32[]{:S(2)}) collective-permute-start(bf16[144,384]{1,0:T(8,128)(2,1)} %get-tuple-element.29), channel_id=1, source_target_pairs={{0,128},{64,192},{128,0},{192,64},{1,129},{65,193},{129,1},{193,65... | collective-permute-start | bytes 331784 | tf_op jit(solution)/shard_map/ppermute | solution.py:217
  113.7 7.7 %collective-permute-start.8 = (bf16[144,384]{1,0:T(8,128)(2,1)}, bf16[144,384]{1,0:T(8,128)(2,1)}, u32[]{:S(2)}, u32[]{:S(2)}) collective-permute-start(bf16[144,384]{1,0:T(8,128)(2,1)} %get-tuple-element.28), channel_id=1, source_target_pairs={{0,64},{64,128},{128,192},{192,0},{1,65},{65,129},{129,193},{193,1... | collective-permute-start | bytes 331784 | tf_op jit(solution)/shard_map/ppermute | solution.py:217
Sparse Core Ops, SparseCore 0:
  11.8 43.1 all-gather.1

commit v2 on v1

v2 whole, which is shorter than its diff:
```python
import functools
import math

import jax
import jax.numpy as jnp
from jax import lax
from jax.experimental import pallas as pl
from jax.experimental.pallas import tpu as pltpu
from jax.sharding import Mesh
from jax.sharding import PartitionSpec as P

HD = 128
TOP = 4.0
ROOT = math.sqrt(HD)
NT = (((1,), (1,)), ((), ()))
TN = (((0,), (0,)), ((), ()))
NN = (((1,), (0,)), ((), ()))
F32 = jnp.float32
BF16 = jnp.bfloat16
VMEM_LIMIT = 48 * 1024 * 1024
PREP_LIMIT = 62 * 1024 * 1024


def mxu(a, b, dims):
    return lax.dot_general(a, b, dims, preferred_element_type=F32)


def call(body, name, out_shape, args, scratch=(), flops=0, nbytes=0, exps=0, limit=VMEM_LIMIT, **more):
    return pl.pallas_call(
        body,
        name=name,
        out_shape=out_shape,
        scratch_shapes=list(scratch),
        **more,
        compiler_params=pltpu.CompilerParams(vmem_limit_bytes=limit),
        cost_estimate=pl.CostEstimate(flops=flops, bytes_accessed=nbytes, transcendentals=exps),
    )(*args)


def lanes_of(values):
    lane = lax.broadcasted_iota(jnp.int32, (1, 128), 1)
    row = jnp.zeros((1, 128), F32)
    for i, value in enumerate(values):
        row = jnp.where(lane == i, value, row)
    return row


def peak_lanes(ref):
    return jnp.max(ref[...], axis=0)


def biggest(x):
    return jnp.max(jnp.abs(x.astype(F32)), keepdims=True)


def scaled(x, factor):
    return (x.astype(F32) * factor).astype(BF16)


def prep_kernel(q_ref, k_ref, v_ref, g_ref, qg_ref, kv_ref, pk_ref, sems):
    width = q_ref.shape[1]
    left, right = slice(0, width), slice(width, 2 * width)
    places = [(q_ref, qg_ref, left), (k_ref, kv_ref, left), (v_ref, kv_ref, right), (g_ref, qg_ref, right)]
    copies = [
        pltpu.make_async_copy(src, dst.at[:, cols], sems.at[i]) for i, (src, dst, cols) in enumerate(places)
    ]
    for copy in copies:
        copy.start()
    for copy in copies:
        copy.wait()
    row = lanes_of([biggest(dst[:, cols]) for _, dst, cols in places])
    pk_ref[...] = jnp.broadcast_to(row[None], pk_ref.shape)


def place_of(zh, groups, rows, s):
    return pl.ds(pl.multiple_of(lax.rem(zh + groups - s, groups) * rows, 16), rows)


def forward_kernel(heads, groups, wide, zh_ref, *refs):
    qgs, kvs = refs[:groups], refs[groups : groups + wide]
    pk_ref, ot_ref, st_ref, qs, gs, kb, vb = refs[groups + wide :]
    rows, width = qgs[0].shape[0], qs.shape[1]
    span = kvs[0].shape[0]
    pk = peak_lanes(pk_ref)
    pq, pkk, pv, pg = (pk[:, i : i + 1] for i in range(4))
    zh = zh_ref[0]
    for s, ref in enumerate(qgs):
        qs[place_of(zh, groups, rows, s), :] = scaled(ref[:, :width], TOP / pq)
        gs[place_of(zh, groups, rows, s), :] = scaled(ref[:, width:], TOP / pg)
    for s, ref in enumerate(kvs):
        kb[s * span : (s + 1) * span, :] = scaled(ref[:, :width], TOP / pkk)
        vb[s * span : (s + 1) * span, :] = scaled(ref[:, width:], TOP / pv)
    score_scale = pq * pkk / (TOP * TOP * ROOT)
    rows_out = []
    for h in range(heads):
        cols = slice(h * HD, (h + 1) * HD)
        s = mxu(kb[:, cols], qs[:, cols], NT) * score_scale
        m = jnp.max(s, axis=0, keepdims=True)
        e = jnp.exp(s - m)
        total = jnp.sum(e, axis=0, keepdims=True)
        o = mxu(vb[:, cols], e.astype(BF16), TN) / total
        ot_ref[cols, :] = o
        rows_out.append(m + jnp.log(total))
        rows_out.append(jnp.sum(o * gs[:, cols].T.astype(F32), axis=0, keepdims=True))
    for p in range(groups):
        for i, row in enumerate(rows_out):
            st_ref[p, i : i + 1, :] = row
        st_ref[p, len(rows_out) :, :] = jnp.zeros_like(st_ref[p, len(rows_out) :, :])


def backward_kernel(heads, groups, zh_ref, own_ref, st_ref, pk_ref, ot_ref, qs, gs, kb, vb, *refs):
    oqs, dkvs, (oqa,) = refs[:groups], refs[groups : 2 * groups], refs[2 * groups :]
    rows, width = oqs[0].shape[0], qs.shape[1]
    pk = peak_lanes(pk_ref)
    pq, pkk, pv, pg = (pk[:, i : i + 1] for i in range(4))
    score_scale = pq * pkk / (TOP * TOP * ROOT)
    grad_scale = pg * pv / (TOP * TOP)
    zh = zh_ref[0]
    span = kb.shape[0] // groups
    for h in range(heads):
        cols = slice(h * HD, (h + 1) * HD)
        right = slice(width + h * HD, width + (h + 1) * HD)
        lse = st_ref[:, 2 * h, :]
        top = jnp.max(lse, axis=0, keepdims=True)
        log_total = top + jnp.log(jnp.sum(jnp.exp(lse - top), axis=0, keepdims=True))
        delta = jnp.sum(jnp.exp(lse - log_total) * st_ref[:, 2 * h + 1, :], axis=0, keepdims=True)
        delta = delta * grad_scale
        weight = jnp.exp(own_ref[0, 2 * h : 2 * h + 1, :] - log_total) * (pv / TOP)
        oqa[:, cols] = (ot_ref[cols, :] * weight).astype(BF16).T
        q, g, k = qs[:, cols], gs[:, cols], kb[:, cols]
        p = jnp.exp(mxu(k, q, NT) * score_scale - log_total)
        dv = mxu(p.astype(BF16), g, NN) * (pg / TOP)
        dp = mxu(vb[:, cols], g, NT) * grad_scale
        ds = (p * (dp - delta)).astype(BF16)
        dk = mxu(ds, q, NN) * (pq / (TOP * ROOT))
        dq = mxu(k, ds, TN) * (pkk / (TOP * ROOT))
        oqa[:, right] = dq.astype(BF16).T
        for s, ref in enumerate(dkvs):
            part = slice(s * span, (s + 1) * span)
            ref[:, cols] = dk[part].astype(BF16)
            ref[:, right] = dv[part].astype(BF16)
    for s, ref in enumerate(oqs):
        ref[...] = oqa[place_of(zh, groups, rows, s), :]


def fold_kernel(*refs):
    parts, (own_ref, send_ref) = refs[:-2], refs[-2:]
    rows = own_ref.shape[0]
    own_ref[...] = sum(r[:rows, :].astype(F32) for r in parts)
    send_ref[...] = sum(r[rows:, :].astype(F32) for r in parts).astype(BF16)


def sums_kernel(groups, own_ref, got_ref, *refs):
    oqs, (goq_ref, gkv_ref, pk_ref) = refs[:groups], refs[groups:]
    width = own_ref.shape[1] // 2
    goq_ref[...] = sum(r[...].astype(F32) for r in oqs)
    gkv_ref[...] = own_ref[...] + got_ref[...].astype(F32)
    row = lanes_of([biggest(r[:, c]) for r in (goq_ref, gkv_ref) for c in (slice(0, width), slice(width, 2 * width))])
    pk_ref[...] = jnp.broadcast_to(row[None], pk_ref.shape)


def cast_kernel(goq_ref, gkv_ref, pk_ref, *outs):
    pk = peak_lanes(pk_ref)
    width = outs[0].shape[1]
    sources = [r[:, c] for r in (goq_ref, gkv_ref) for c in (slice(0, width), slice(width, 2 * width))]
    for i, (src, dst) in enumerate(zip(sources, outs)):
        dst[...] = scaled(src, TOP / pk[:, i : i + 1])


def shift(n, s):
    return [(i, (i + s) % n) for i in range(n)]


def spread(x, axis, n):
    return [x] + [lax.ppermute(x, axis, shift(n, s)) for s in range(1, n)]


def home(parts, axis):
    n = len(parts)
    return [parts[0]] + [lax.ppermute(parts[s], axis, shift(n, n - s)) for s in range(1, n)]


def like(dtype, *shape):
    return jax.ShapeDtypeStruct(shape, dtype)


def on_device(sizes, queries, keys, values, out_grad):
    groups, everyone = sizes["zh"], math.prod(sizes.values())
    axes = tuple(sizes)
    rows, width = queries.shape
    heads = width // HD
    q_rows, k_rows = rows * groups, rows * sizes["x"] * sizes["zl"]
    pairs = q_rows * k_rows * heads
    peaks = like(F32, everyone, 1, 128)
    wide = like(BF16, rows, 2 * width)
    zh = lax.axis_index("zh").astype(jnp.int32).reshape(1)
    smem = pl.BlockSpec(memory_space=pltpu.SMEM)
    vmem = pl.BlockSpec(memory_space=pltpu.VMEM)
    hbm = pl.BlockSpec(memory_space=pltpu.HBM)

    qg, kv, pk = call(
        prep_kernel,
        "prep",
        (wide, wide, peaks),
        (queries, keys, values, out_grad),
        [pltpu.SemaphoreType.DMA((4,))],
        nbytes=2**20,
        limit=PREP_LIMIT,
        in_specs=[hbm] * 4,
    )
    twin = lax.ppermute(kv, "zl", shift(2, 1))
    near = spread(kv, "x", sizes["x"])
    qgs = spread(qg, "zh", groups)
    far = spread(twin, "x", sizes["x"])
    pk = lax.all_to_all(pk, axes, 0, 0, tiled=True)
    kvs = [one for two in zip(near, far) for one in two]

    ot, stats, qs, gs, kb, vb = call(
        functools.partial(forward_kernel, heads, groups, len(kvs)),
        "forward",
        (like(F32, width, q_rows), like(F32, groups, 8, q_rows))
        + (like(BF16, q_rows, width),) * 2
        + (like(BF16, k_rows, width),) * 2,
        (zh, *qgs, *kvs, pk),
        flops=4 * pairs * HD,
        nbytes=4 * 2**20,
        exps=pairs,
        in_specs=[smem] + [vmem] * (groups + len(kvs) + 1),
    )
    sts = lax.all_to_all(stats, "zh", 0, 0, tiled=True)
    outs = call(
        functools.partial(backward_kernel, heads, groups),
        "backward",
        (wide,) * groups + (like(BF16, k_rows // groups, 2 * width),) * groups,
        (zh, stats, sts, pk, ot, qs, gs, kb, vb),
        [pltpu.VMEM((q_rows, 2 * width), BF16)],
        flops=10 * pairs * HD,
        nbytes=6 * 2**20,
        exps=pairs,
        in_specs=[smem] + [vmem] * 8,
    )
    dkvs = home(outs[groups:], "x")
    oqs = home(outs[:groups], "zh")
    own, send = call(fold_kernel, "fold", (like(F32, rows, 2 * width), wide), dkvs, nbytes=2 * 2**20)
    got = lax.ppermute(send, "zl", shift(2, 1))
    goq, gkv, tops = call(
        functools.partial(sums_kernel, groups),
        "sums",
        (like(F32, rows, 2 * width), like(F32, rows, 2 * width), peaks),
        (own, got, *oqs),
        nbytes=3 * 2**20,
    )
    tops = lax.all_to_all(tops, axes, 0, 0, tiled=True)
    return call(cast_kernel, "cast", (like(BF16, rows, width),) * 4, (goq, gkv, tops), nbytes=2**20)


def solution(mesh):
    sizes = dict(x=4, zh=4, zl=2, y=4, c=2)
    fine = Mesh(mesh.devices.reshape(tuple(sizes.values())), tuple(sizes))
    spec = P(("x", "zh", "zl"), ("y", "c"))
    return jax.shard_map(
        functools.partial(on_device, sizes),
        mesh=fine,
        in_specs=(spec,) * 4,
        out_specs=(spec,) * 4,
        check_vma=False,
    )
```

time: 161 us -> 134 us (0.83)
  between operations: 14.1 us -> 0.71 us
  local copies, waits for them, and re-layouts: 8.36 us -> 0.94 us
  waiting for transfers between devices: 49 us -> 41.9 us
  starting transfers between devices: 35 us -> 38.4 us
    all_to_all x2 -> x0, waiting for transfers between devices: 19.7 us -> none  [the longest x1 13.1 us: on_device(): o = lax.all_to_all(o.reshape(nz, rows, width), 'z', 0, 0, tiled=True)]
    ppermute x9 -> x17, waiting for transfers between devices: 16.7 us -> 33.6 us  [the longest x6 17.1 us: home(): lax.ppermute(parts[s], axis, shift(n, n - s))]
    ppermute x9 -> x17, starting transfers between devices: 12 us -> 28.4 us  [the longest x9 20.6 us: spread(): return [x] + [lax.ppermute(x, axis, shift(n, s)) for s in range(1, n)]]
    all_gather x1 -> x0, waiting for transfers between devices: 12.6 us -> none  [on_device(): qg_all = lax.all_gather(qg, 'z', axis=0, tiled=True)]
    all_to_all x1, waiting for transfers between devices: 0.01 us -> 8.3 us  [on_device(): pk = lax.all_to_all(pk, axes, 0, 0, tiled=True)]
    all_to_all x2 -> x0, starting transfers between devices: 7.28 us -> none  [the longest x1 3.73 us: on_device(): o = lax.all_to_all(o.reshape(nz, rows, width), 'z', 0, 0, tiled=True)]
    all_to_all x1, starting transfers between devices: 15.7 us -> 9.97 us  [on_device(): pk = lax.all_to_all(pk, axes, 0, 0, tiled=True)]
    unnamed x12 -> x4, local copies, waits for them, and re-layouts: 6.52 us -> 0.94 us
  transfers between devices with their start and end apart: 13 -> 18, of which waited for: 9 -> 7; matrix products, arithmetic and copies ran while one was open for 1% -> 0% of each run, Pallas kernels for 5% -> 0%
where the time goes in v2:
time: 134 us
  waiting for transfers between devices  41.9 us (31%)
  starting transfers between devices  38.4 us (29%)
  blocking collectives  36.1 us (27%)
  Pallas kernels  15.7 us (12%)
    all_to_all x1, blocking collectives, on_device(): tops = lax.all_to_all(tops, axes, 0, 0, tiled=True)  23 us
    ppermute x9, starting transfers between devices, spread(): return [x] + [lax.ppermute(x, axis, shift(n, s)) for s in range(1, n)]  20.6 us
    ppermute x6, waiting for transfers between devices, home(): lax.ppermute(parts[s], axis, shift(n, n - s))  17.1 us
    pallas_call x6, Pallas kernels, call(): pl.pallas_call(body, name=name, out_shape=out_shape, scratch_shapes=list(...  15.7 us
    all_to_all x1, blocking collectives, on_device(): sts = lax.all_to_all(stats, 'zh', 0, 0, tiled=True)  13.1 us
    all_to_all x1, starting transfers between devices, on_device(): pk = lax.all_to_all(pk, axes, 0, 0, tiled=True)  9.97 us
    all_to_all x1, waiting for transfers between devices, on_device(): pk = lax.all_to_all(pk, axes, 0, 0, tiled=True)  8.3 us
    ppermute x1, waiting for transfers between devices, on_device(): got = lax.ppermute(send, 'zl', shift(2, 1))  7.52 us
  transfers between devices with their start and end apart: 18, of which 7 were waited for; matrix products, arithmetic and copies ran while one was open for 0% of the time, Pallas kernels for 0%

profile of v2, /device:TPU:1, one launch (start us, length us, event | category | flops | bytes accessed | tf_op | source)
XLA Modules:
  0.0 133.8 jit_solution(6846435754068186750)
XLA Ops:
  0.6 2.0 %prep.1 = (bf16[144,768]{1,0:T(8,128)(2,1)}, bf16[144,768]{1,0:T(8,128)(2,1)}, f32[256,1,128]{2,1,0:T(1,128)}) custom-call(bf16[144,384]{1,0:T(8,128)(2,1)} %q_ref.1, bf16[144,384]{1,0:T(8,128)(2,1)} %k_ref.1, bf16[144,384]{1,0:T(8,128)(2,1)} %v_ref.1, bf16[144,384]{1,0:T(8,128)(2,1)} %g_ref.1), custom_call_target="tpu_custom_call" | custom-call | bytes 1048576 | tf_op jit(solution)/shard_map/prep/pallas_call | solution.py:29
  2.6 6.9 %collective-permute-start.2 = (bf16[144,768]{1,0:T(8,128)(2,1)}, bf16[144,768]{1,0:T(8,128)(2,1)S(1)}, u32[]{:S(2)}, u32[]{:S(2)}) collective-permute-start(bf16[144,768]{1,0:T(8,128)(2,1)} %get-tuple-element.26.refs_0_), channel_id=1, source_target_pairs={{0,48},{16,0},{32,16},{48,32},{1,49},{17,1},{33,17},{49,33},{2,50}... | collective-permute-start | bytes 663560 | tf_op jit(solution)/shard_map/ppermute | solution.py:175
  9.6 1.0 collective-permute-start.1
  10.5 0.9 collective-permute-start.3
  11.5 2.1 %collective-permute-start = (bf16[144,768]{1,0:T(8,128)(2,1)}, bf16[144,768]{1,0:T(8,128)(2,1)S(1)}, u32[]{:S(2)}, u32[]{:S(2)}) collective-permute-start(bf16[144,768]{1,0:T(8,128)(2,1)} %get-tuple-element.26.refs_0_), channel_id=1, source_target_pairs={{0,16},{16,32},{32,48},{48,0},{1,17},{17,33},{33,49},{49,1},{2,18}... | collective-permute-start | bytes 663560 | tf_op jit(solution)/shard_map/ppermute | solution.py:175
  13.5 2.5 %collective-permute-start.8 = (bf16[144,768]{1,0:T(8,128)(2,1)}, bf16[144,768]{1,0:T(8,128)(2,1)S(1)}, u32[]{:S(2)}, u32[]{:S(2)}) collective-permute-start(bf16[144,768]{1,0:T(8,128)(2,1)} %get-tuple-element.27.refs_4_), channel_id=1, source_target_pairs={{0,192},{64,0},{128,64},{192,128},{1,193},{65,1},{129,65},{193,129... | collective-permute-start | bytes 663560 | tf_op jit(solution)/shard_map/ppermute | solution.py:175
  16.0 10.0 %all-to-all-start = ((f32[256,1,128]{2,1,0:T(1,128)}), f32[256,1,128]{2,1,0:T(1,128)S(1)}, u32[]{:S(2)}, u32[]{:S(2)}) async-start(f32[256,1,128]{2,1,0:T(1,128)} %get-tuple-element.28), calls=%async_computation | async-start | bytes 262144 | tf_op jit(solution)/shard_map/all_to_all | solution.py:215
  26.0 3.0 %collective-permute-start.6 = (bf16[144,768]{1,0:T(8,128)(2,1)}, bf16[144,768]{1,0:T(8,128)(2,1)S(1)}, u32[]{:S(2)}, u32[]{:S(2)}) collective-permute-start(bf16[144,768]{1,0:T(8,128)(2,1)} %get-tuple-element.27.refs_4_), channel_id=1, source_target_pairs={{0,128},{64,192},{128,0},{192,64},{1,129},{65,193},{129,1},{193,65... | collective-permute-start | bytes 663560 | tf_op jit(solution)/shard_map/ppermute | solution.py:175
  29.0 1.0 collective-permute-start.4
  30.0 4.6 %collective-permute-done.3.refs_5_ = bf16[144,768]{1,0:T(8,128)(2,1)S(1)} collective-permute-done((bf16[144,768]{1,0:T(8,128)(2,1)}, bf16[144,768]{1,0:T(8,128)(2,1)S(1)}, u32[]{:S(2)}, u32[]{:S(2)}) %collective-permute-start.3) | collective-permute-done | bytes 221216 | tf_op jit(solution)/shard_map/ppermute | solution.py:211
  34.6 2.5 %collective-permute-start.9 = (bf16[144,768]{1,0:T(8,128)(2,1)S(1)}, bf16[144,768]{1,0:T(8,128)(2,1)S(1)}, u32[]{:S(2)}, u32[]{:S(2)}) collective-permute-start(bf16[144,768]{1,0:T(8,128)(2,1)S(1)} %collective-permute-done.3.refs_5_), channel_id=1, source_target_pairs={{0,192},{64,0},{128,64},{192,128},{1,193},{65,1},{129,65},{193,129... | collective-permute-start | bytes 663560 | tf_op jit(solution)/shard_map/ppermute | solution.py:175
  37.1 1.3 collective-permute-start.7
  38.4 0.3 collective-permute-start.5
  38.8 8.3 %all-to-all-done.refs_12_.pk_ref = f32[256,1,128]{2,1,0:T(1,128)S(1)} async-done(((f32[256,1,128]{2,1,0:T(1,128)}), f32[256,1,128]{2,1,0:T(1,128)S(1)}, u32[]{:S(2)}, u32[]{:S(2)}) %all-to-all-start) | async-done | bytes 131104 | tf_op jit(solution)/shard_map/all_to_all | solution.py:215
  47.1 4.3 %collective-permute-done.5.refs_7_ = bf16[144,768]{1,0:T(8,128)(2,1)S(1)} collective-permute-done((bf16[144,768]{1,0:T(8,128)(2,1)S(1)}, bf16[144,768]{1,0:T(8,128)(2,1)S(1)}, u32[]{:S(2)}, u32[]{:S(2)}) %collective-permute-start.5) | collective-permute-done | bytes 221216 | tf_op jit(solution)/shard_map/ppermute | solution.py:175
  51.4 0.9 copy-done.1
  52.3 5.2 %forward.1 = (f32[384,576]{1,0:T(8,128)}, f32[4,8,576]{2,1,0:T(8,128)S(1)}, bf16[576,384]{1,0:T(8,128)(2,1)S(1)}, bf16[576,384]{1,0:T(8,128)(2,1)S(1)}, bf16[115...) custom-call(s32[1]{0:T(128)} %bitcast.zh_ref, bf16[144,768]{1,0:T(8,128)(2,1)S(1)} %copy-done, ...), custom_call_target="tpu_custom_call" | custom-call | flops 1019215872 | bytes 4194304 | tf_op jit(solution)/shard_map/forward/pallas_call | solution.py:29
  57.5 13.1 %all_to_all.15.st_ref = f32[4,8,576]{2,1,0:T(8,128)S(1)} all-to-all(f32[4,8,576]{2,1,0:T(8,128)S(1)} %get-tuple-element.29.own_ref), channel_id=1, replica_groups=mesh['x'=4,'zh'=4,'zl'=2,'y'=4,'c'=2] {'zh'}, dimensions={0} | all-to-all | bytes 147456 | tf_op jit(solution)/shard_map/all_to_all | solution.py:230
  70.6 7.1 %backward.1 = (bf16[144,768]{1,0:T(8,128)(2,1)S(1)}, bf16[144,768]{1,0:T(8,128)(2,1)S(1)}, bf16[144,768]{1,0:T(8,128)(2,1)S(1)}, bf16[144,768]{1,0:T(8,128)(2,1)...) custom-call(s32[1]{0:T(128)} %bitcast.zh_ref, ...), custom_call_target="tpu_custom_call" | custom-call | flops 2548039680 | bytes 6291456 | tf_op jit(solution)/shard_map/backward/pallas_call | solution.py:29
  77.8 1.8 %collective-permute-start.11 = (bf16[288,768]{1,0:T(8,128)(2,1)S(1)}, bf16[288,768]{1,0:T(8,128)(2,1)S(1)}, u32[]{:S(2)}, u32[]{:S(2)}) collective-permute-start(bf16[288,768]{1,0:T(8,128)(2,1)S(1)} %get-tuple-element.37), channel_id=1, source_target_pairs={{0,128},{64,192},{128,0},{192,64},{1,129},{65,193},{129,1},{193,65... | collective-permute-start | bytes 1327112 | tf_op jit(solution)/shard_map/ppermute | solution.py:180
  79.7 0.3 collective-permute-start.12
  80.0 0.6 collective-permute-start.14
  80.5 2.9 %collective-permute-start.15 = (bf16[144,768]{1,0:T(8,128)(2,1)S(1)}, bf16[144,768]{1,0:T(8,128)(2,1)S(1)}, u32[]{:S(2)}, u32[]{:S(2)}) collective-permute-start(bf16[144,768]{1,0:T(8,128)(2,1)S(1)} %get-tuple-element.43), channel_id=1, source_target_pairs={{0,32},{16,48},{32,0},{48,16},{1,33},{17,49},{33,1},{49,17},{2,34}... | collective-permute-start | bytes 663560 | tf_op jit(solution)/shard_map/ppermute | solution.py:180
  83.4 3.6 %collective-permute-done.10.refs_1_ = bf16[288,768]{1,0:T(8,128)(2,1)S(1)} collective-permute-done((bf16[288,768]{1,0:T(8,128)(2,1)S(1)}, bf16[288,768]{1,0:T(8,128)(2,1)S(1)}, u32[]{:S(2)}, u32[]{:S(2)}) %collective-permute-start.10) | collective-permute-done | bytes 442400 | tf_op jit(solution)/shard_map/ppermute | solution.py:180
  87.1 0.4 collective-permute-start.16
  87.5 0.8 collective-permute-done.11.refs_2_
  88.3 12.7 %collective-permute-done.12.refs_3_ = bf16[288,768]{1,0:T(8,128)(2,1)S(1)} collective-permute-done((bf16[288,768]{1,0:T(8,128)(2,1)S(1)}, bf16[288,768]{1,0:T(8,128)(2,1)S(1)}, u32[]{:S(2)}, u32[]{:S(2)}) %collective-permute-start.12) | collective-permute-done | bytes 442400 | tf_op jit(solution)/shard_map/ppermute | solution.py:180
  101.2 0.8 collective-permute-start.13
  102.0 7.5 %collective-permute-done.13.got_ref = bf16[144,768]{1,0:T(8,128)(2,1)S(1)} collective-permute-done((bf16[144,768]{1,0:T(8,128)(2,1)S(1)}, bf16[144,768]{1,0:T(8,128)(2,1)S(1)}, u32[]{:S(2)}, u32[]{:S(2)}) %collective-permute-start.13) | collective-permute-done | bytes 221216 | tf_op jit(solution)/shard_map/ppermute | solution.py:245
  109.5 0.3 sums.1
  109.9 23.0 %all_to_all.16.pk_ref = f32[256,1,128]{2,1,0:T(1,128)S(1)} all-to-all(f32[256,1,128]{2,1,0:T(1,128)S(1)} %get-tuple-element.47), channel_id=1, replica_groups=mesh['x'=4,'zh'=4,'zl'=2,'y'=4,'c'=2] {'x','zh','zl','y','c'}, dimensions={0} | all-to-all | bytes 262144 | tf_op jit(solution)/shard_map/all_to_all | solution.py:253
  132.9 0.9 cast.1
  (16 shorter events, 0.3 us)
Async XLA Ops:
  2.6 48.8 %copy-start = (bf16[144,768]{1,0:T(8,128)(2,1)S(1)}, bf16[144,768]{1,0:T(8,128)(2,1)}, u32[]{:S(2)}) copy-start(bf16[144,768]{1,0:T(8,128)(2,1)} %get-tuple-element.26.refs_0_) | copy-start | bytes 663556
  2.6 23.4 %collective-permute-start.2 = (bf16[144,768]{1,0:T(8,128)(2,1)}, bf16[144,768]{1,0:T(8,128)(2,1)S(1)}, u32[]{:S(2)}, u32[]{:S(2)}) collective-permute-start(bf16[144,768]{1,0:T(8,128)(2,1)} %get-tuple-element.26.refs_0_), channel_id=1, source_target_pairs={{0,48},{16,0},{32,16},{48,32},{1,49},{17,1},{33,17},{49,33},{2,50}... | collective-permute-start | bytes 663560 | tf_op jit(solution)/shard_map/ppermute | solution.py:175
  9.6 19.4 %collective-permute-start.1 = (bf16[144,768]{1,0:T(8,128)(2,1)}, bf16[144,768]{1,0:T(8,128)(2,1)S(1)}, u32[]{:S(2)}, u32[]{:S(2)}) collective-permute-start(bf16[144,768]{1,0:T(8,128)(2,1)} %get-tuple-element.26.refs_0_), channel_id=1, source_target_pairs={{0,32},{16,48},{32,0},{48,16},{1,33},{17,49},{33,1},{49,17},{2,34}... | collective-permute-start | bytes 663560 | tf_op jit(solution)/shard_map/ppermute | solution.py:175
  10.5 24.1 %collective-permute-start.3 = (bf16[144,768]{1,0:T(8,128)(2,1)}, bf16[144,768]{1,0:T(8,128)(2,1)S(1)}, u32[]{:S(2)}, u32[]{:S(2)}) collective-permute-start(bf16[144,768]{1,0:T(8,128)(2,1)} %get-tuple-element.27.refs_4_), channel_id=1, source_target_pairs={{0,8},{8,0},{1,9},{9,1},{2,10},{10,2},{3,11},{11,3},{4,12},{12,4},... | collective-permute-start | bytes 663560 | tf_op jit(solution)/shard_map/ppermute | solution.py:211
  11.5 25.7 %collective-permute-start = (bf16[144,768]{1,0:T(8,128)(2,1)}, bf16[144,768]{1,0:T(8,128)(2,1)S(1)}, u32[]{:S(2)}, u32[]{:S(2)}) collective-permute-start(bf16[144,768]{1,0:T(8,128)(2,1)} %get-tuple-element.26.refs_0_), channel_id=1, source_target_pairs={{0,16},{16,32},{32,48},{48,0},{1,17},{17,33},{33,49},{49,1},{2,18}... | collective-permute-start | bytes 663560 | tf_op jit(solution)/shard_map/ppermute | solution.py:175
  13.5 24.9 %collective-permute-start.8 = (bf16[144,768]{1,0:T(8,128)(2,1)}, bf16[144,768]{1,0:T(8,128)(2,1)S(1)}, u32[]{:S(2)}, u32[]{:S(2)}) collective-permute-start(bf16[144,768]{1,0:T(8,128)(2,1)} %get-tuple-element.27.refs_4_), channel_id=1, source_target_pairs={{0,192},{64,0},{128,64},{192,128},{1,193},{65,1},{129,65},{193,129... | collective-permute-start | bytes 663560 | tf_op jit(solution)/shard_map/ppermute | solution.py:175
  16.0 31.0 %all-to-all-start = ((f32[256,1,128]{2,1,0:T(1,128)}), f32[256,1,128]{2,1,0:T(1,128)S(1)}, u32[]{:S(2)}, u32[]{:S(2)}) async-start(f32[256,1,128]{2,1,0:T(1,128)} %get-tuple-element.28), calls=%async_computation | async-start | bytes 262144 | tf_op jit(solution)/shard_map/all_to_all | solution.py:215
  26.0 12.7 %collective-permute-start.6 = (bf16[144,768]{1,0:T(8,128)(2,1)}, bf16[144,768]{1,0:T(8,128)(2,1)S(1)}, u32[]{:S(2)}, u32[]{:S(2)}) collective-permute-start(bf16[144,768]{1,0:T(8,128)(2,1)} %get-tuple-element.27.refs_4_), channel_id=1, source_target_pairs={{0,128},{64,192},{128,0},{192,64},{1,129},{65,193},{129,1},{193,65... | collective-permute-start | bytes 663560 | tf_op jit(solution)/shard_map/ppermute | solution.py:175
  29.0 9.8 %collective-permute-start.4 = (bf16[144,768]{1,0:T(8,128)(2,1)}, bf16[144,768]{1,0:T(8,128)(2,1)S(1)}, u32[]{:S(2)}, u32[]{:S(2)}) collective-permute-start(bf16[144,768]{1,0:T(8,128)(2,1)} %get-tuple-element.27.refs_4_), channel_id=1, source_target_pairs={{0,64},{64,128},{128,192},{192,0},{1,65},{65,129},{129,193},{193,1... | collective-permute-start | bytes 663560 | tf_op jit(solution)/shard_map/ppermute | solution.py:175
  34.6 12.4 %collective-permute-start.9 = (bf16[144,768]{1,0:T(8,128)(2,1)S(1)}, bf16[144,768]{1,0:T(8,128)(2,1)S(1)}, u32[]{:S(2)}, u32[]{:S(2)}) collective-permute-start(bf16[144,768]{1,0:T(8,128)(2,1)S(1)} %collective-permute-done.3.refs_5_), channel_id=1, source_target_pairs={{0,192},{64,0},{128,64},{192,128},{1,193},{65,1},{129,65},{193,129... | collective-permute-start | bytes 663560 | tf_op jit(solution)/shard_map/ppermute | solution.py:175
  37.1 10.0 %collective-permute-start.7 = (bf16[144,768]{1,0:T(8,128)(2,1)S(1)}, bf16[144,768]{1,0:T(8,128)(2,1)S(1)}, u32[]{:S(2)}, u32[]{:S(2)}) collective-permute-start(bf16[144,768]{1,0:T(8,128)(2,1)S(1)} %collective-permute-done.3.refs_5_), channel_id=1, source_target_pairs={{0,128},{64,192},{128,0},{192,64},{1,129},{65,193},{129,1},{193,65... | collective-permute-start | bytes 663560 | tf_op jit(solution)/shard_map/ppermute | solution.py:175
  38.4 12.9 %collective-permute-start.5 = (bf16[144,768]{1,0:T(8,128)(2,1)S(1)}, bf16[144,768]{1,0:T(8,128)(2,1)S(1)}, u32[]{:S(2)}, u32[]{:S(2)}) collective-permute-start(bf16[144,768]{1,0:T(8,128)(2,1)S(1)} %collective-permute-done.3.refs_5_), channel_id=1, source_target_pairs={{0,64},{64,128},{128,192},{192,0},{1,65},{65,129},{129,193},{193,1... | collective-permute-start | bytes 663560 | tf_op jit(solution)/shard_map/ppermute | solution.py:175
  51.4 0.9 copy-start.1
  77.7 9.4 %collective-permute-start.10 = (bf16[288,768]{1,0:T(8,128)(2,1)S(1)}, bf16[288,768]{1,0:T(8,128)(2,1)S(1)}, u32[]{:S(2)}, u32[]{:S(2)}) collective-permute-start(bf16[288,768]{1,0:T(8,128)(2,1)S(1)} %get-tuple-element.36), channel_id=1, source_target_pairs={{0,192},{64,0},{128,64},{192,128},{1,193},{65,1},{129,65},{193,129... | collective-permute-start | bytes 1327112 | tf_op jit(solution)/shard_map/ppermute | solution.py:180
  77.8 10.5 %collective-permute-start.11 = (bf16[288,768]{1,0:T(8,128)(2,1)S(1)}, bf16[288,768]{1,0:T(8,128)(2,1)S(1)}, u32[]{:S(2)}, u32[]{:S(2)}) collective-permute-start(bf16[288,768]{1,0:T(8,128)(2,1)S(1)} %get-tuple-element.37), channel_id=1, source_target_pairs={{0,128},{64,192},{128,0},{192,64},{1,129},{65,193},{129,1},{193,65... | collective-permute-start | bytes 1327112 | tf_op jit(solution)/shard_map/ppermute | solution.py:180
  79.7 21.3 %collective-permute-start.12 = (bf16[288,768]{1,0:T(8,128)(2,1)S(1)}, bf16[288,768]{1,0:T(8,128)(2,1)S(1)}, u32[]{:S(2)}, u32[]{:S(2)}) collective-permute-start(bf16[288,768]{1,0:T(8,128)(2,1)S(1)} %get-tuple-element.38), channel_id=1, source_target_pairs={{0,64},{64,128},{128,192},{192,0},{1,65},{65,129},{129,193},{193,1... | collective-permute-start | bytes 1327112 | tf_op jit(solution)/shard_map/ppermute | solution.py:180
  80.0 22.0 %collective-permute-start.14 = (bf16[144,768]{1,0:T(8,128)(2,1)S(1)}, bf16[144,768]{1,0:T(8,128)(2,1)S(1)}, u32[]{:S(2)}, u32[]{:S(2)}) collective-permute-start(bf16[144,768]{1,0:T(8,128)(2,1)S(1)} %get-tuple-element.42), channel_id=1, source_target_pairs={{0,48},{16,0},{32,16},{48,32},{1,49},{17,1},{33,17},{49,33},{2,50}... | collective-permute-start | bytes 663560 | tf_op jit(solution)/shard_map/ppermute | solution.py:180
  80.5 21.5 %collective-permute-start.15 = (bf16[144,768]{1,0:T(8,128)(2,1)S(1)}, bf16[144,768]{1,0:T(8,128)(2,1)S(1)}, u32[]{:S(2)}, u32[]{:S(2)}) collective-permute-start(bf16[144,768]{1,0:T(8,128)(2,1)S(1)} %get-tuple-element.43), channel_id=1, source_target_pairs={{0,32},{16,48},{32,0},{48,16},{1,33},{17,49},{33,1},{49,17},{2,34}... | collective-permute-start | bytes 663560 | tf_op jit(solution)/shard_map/ppermute | solution.py:180
  87.1 14.9 %collective-permute-start.16 = (bf16[144,768]{1,0:T(8,128)(2,1)S(1)}, bf16[144,768]{1,0:T(8,128)(2,1)S(1)}, u32[]{:S(2)}, u32[]{:S(2)}) collective-permute-start(bf16[144,768]{1,0:T(8,128)(2,1)S(1)} %get-tuple-element.44), channel_id=1, source_target_pairs={{0,16},{16,32},{32,48},{48,0},{1,17},{17,33},{33,49},{49,1},{2,18}... | collective-permute-start | bytes 663560 | tf_op jit(solution)/shard_map/ppermute | solution.py:180
  101.2 8.4 %collective-permute-start.13 = (bf16[144,768]{1,0:T(8,128)(2,1)S(1)}, bf16[144,768]{1,0:T(8,128)(2,1)S(1)}, u32[]{:S(2)}, u32[]{:S(2)}) collective-permute-start(bf16[144,768]{1,0:T(8,128)(2,1)S(1)} %get-tuple-element.40), channel_id=1, source_target_pairs={{0,8},{8,0},{1,9},{9,1},{2,10},{10,2},{3,11},{11,3},{4,12},{12,4},... | collective-permute-start | bytes 663560 | tf_op jit(solution)/shard_map/ppermute | solution.py:245

commit v3 on v2

--- a/solution.py
+++ b/solution.py
@@ -18,6 +18,8 @@
 F32 = jnp.float32
 BF16 = jnp.bfloat16
 VMEM_LIMIT = 48 * 1024 * 1024
+WORK_LIMIT = 24 * 1024 * 1024
+FORWARD_LIMIT = 32 * 1024 * 1024
 PREP_LIMIT = 62 * 1024 * 1024
 
 
@@ -76,11 +78,10 @@
     return pl.ds(pl.multiple_of(lax.rem(zh + groups - s, groups) * rows, 16), rows)
 
 
-def forward_kernel(heads, groups, wide, zh_ref, *refs):
-    qgs, kvs = refs[:groups], refs[groups : groups + wide]
-    pk_ref, ot_ref, st_ref, qs, gs, kb, vb = refs[groups + wide :]
+def forward_kernel(heads, groups, shards, zh_ref, *refs):
+    qgs, kvs = refs[:groups], refs[groups : groups + shards]
+    pk_ref, e_ref, ot_ref, row_ref, st_ref, qs, gs, kb, vb = refs[groups + shards :]
     rows, width = qgs[0].shape[0], qs.shape[1]
-    span = kvs[0].shape[0]
     pk = peak_lanes(pk_ref)
     pq, pkk, pv, pg = (pk[:, i : i + 1] for i in range(4))
     zh = zh_ref[0]
@@ -88,59 +89,76 @@
         qs[place_of(zh, groups, rows, s), :] = scaled(ref[:, :width], TOP / pq)
         gs[place_of(zh, groups, rows, s), :] = scaled(ref[:, width:], TOP / pg)
     for s, ref in enumerate(kvs):
-        kb[s * span : (s + 1) * span, :] = scaled(ref[:, :width], TOP / pkk)
-        vb[s * span : (s + 1) * span, :] = scaled(ref[:, width:], TOP / pv)
+        kb[s * rows : (s + 1) * rows, :] = scaled(ref[:, :width], TOP / pkk)
+        vb[s * rows : (s + 1) * rows, :] = scaled(ref[:, width:], TOP / pv)
     score_scale = pq * pkk / (TOP * TOP * ROOT)
-    rows_out = []
+    st_ref[...] = jnp.zeros_like(st_ref)
+    row_ref[...] = jnp.zeros_like(row_ref)
     for h in range(heads):
         cols = slice(h * HD, (h + 1) * HD)
         s = mxu(kb[:, cols], qs[:, cols], NT) * score_scale
         m = jnp.max(s, axis=0, keepdims=True)
         e = jnp.exp(s - m)
+        e_ref[h] = e
         total = jnp.sum(e, axis=0, keepdims=True)
         o = mxu(vb[:, cols], e.astype(BF16), TN) / total
         ot_ref[cols, :] = o
-        rows_out.append(m + jnp.log(total))
-        rows_out.append(jnp.sum(o * gs[:, cols].T.astype(F32), axis=0, keepdims=True))
-    for p in range(groups):
-        for i, row in enumerate(rows_out):
-            st_ref[p, i : i + 1, :] = row
-        st_ref[p, len(rows_out) :, :] = jnp.zeros_like(st_ref[p, len(rows_out) :, :])
-
-
-def backward_kernel(heads, groups, zh_ref, own_ref, st_ref, pk_ref, ot_ref, qs, gs, kb, vb, *refs):
-    oqs, dkvs, (oqa,) = refs[:groups], refs[groups : 2 * groups], refs[2 * groups :]
-    rows, width = oqs[0].shape[0], qs.shape[1]
+        row_ref[h : h + 1, :] = m
+        st_ref[2 * h : 2 * h + 1, :] = m + jnp.log(total)
+        st_ref[2 * h + 1 : 2 * h + 2, :] = jnp.sum(o * gs[:, cols].T.astype(F32), axis=0, keepdims=True)
+
+
+def middle_kernel(heads, gs, vb, dp):
+    for h in range(heads):
+        cols = slice(h * HD, (h + 1) * HD)
+        dp[h] = mxu(vb[:, cols], gs[:, cols], NT)
+
+
+def totals(sts, h):
+    lses = [st[2 * h : 2 * h + 1, :] for st in sts]
+    top = functools.reduce(jnp.maximum, lses)
+    log_total = top + jnp.log(sum(jnp.exp(x - top) for x in lses))
+    delta = sum(jnp.exp(x - log_total) * st[2 * h + 1 : 2 * h + 2, :] for x, st in zip(lses, sts))
+    return log_total, delta
+
+
+def keys_kernel(heads, groups, *refs):
+    sts, (pk_ref, qs, gs, e, row_ref, dp, ds), dkvs = refs[:groups], refs[groups : groups + 7], refs[groups + 7 :]
     pk = peak_lanes(pk_ref)
     pq, pkk, pv, pg = (pk[:, i : i + 1] for i in range(4))
-    score_scale = pq * pkk / (TOP * TOP * ROOT)
     grad_scale = pg * pv / (TOP * TOP)
-    zh = zh_ref[0]
-    span = kb.shape[0] // groups
+    width = qs.shape[1]
+    span = e.shape[1] // groups
     for h in range(heads):
-        cols = slice(h * HD, (h + 1) * HD)
+        left = slice(h * HD, (h + 1) * HD)
         right = slice(width + h * HD, width + (h + 1) * HD)
-        lse = st_ref[:, 2 * h, :]
-        top = jnp.max(lse, axis=0, keepdims=True)
-        log_total = top + jnp.log(jnp.sum(jnp.exp(lse - top), axis=0, keepdims=True))
-        delta = jnp.sum(jnp.exp(lse - log_total) * st_ref[:, 2 * h + 1, :], axis=0, keepdims=True)
-        delta = delta * grad_scale
-        weight = jnp.exp(own_ref[0, 2 * h : 2 * h + 1, :] - log_total) * (pv / TOP)
-        oqa[:, cols] = (ot_ref[cols, :] * weight).astype(BF16).T
-        q, g, k = qs[:, cols], gs[:, cols], kb[:, cols]
-        p = jnp.exp(mxu(k, q, NT) * score_scale - log_total)
-        dv = mxu(p.astype(BF16), g, NN) * (pg / TOP)
-        dp = mxu(vb[:, cols], g, NT) * grad_scale
-        ds = (p * (dp - delta)).astype(BF16)
-        dk = mxu(ds, q, NN) * (pq / (TOP * ROOT))
-        dq = mxu(k, ds, TN) * (pkk / (TOP * ROOT))
-        oqa[:, right] = dq.astype(BF16).T
+        log_total, delta = totals(sts, h)
+        p = e[h] * jnp.exp(row_ref[h : h + 1, :] - log_total)
+        dv = mxu(p.astype(BF16), gs[:, left], NN) * (pg / TOP)
+        d = (p * (dp[h] * grad_scale - delta * grad_scale)).astype(BF16)
+        ds[h] = d
+        dk = mxu(d, qs[:, left], NN) * (pq / (TOP * ROOT))
         for s, ref in enumerate(dkvs):
             part = slice(s * span, (s + 1) * span)
-            ref[:, cols] = dk[part].astype(BF16)
+            ref[:, left] = dk[part].astype(BF16)
             ref[:, right] = dv[part].astype(BF16)
+
+
+def queries_kernel(heads, groups, zh_ref, *refs):
+    sts, (pk_ref, ot_ref, kb, ds) = refs[:groups], refs[groups : groups + 4]
+    oqs, oqa = refs[groups + 4 : -1], refs[-1]
+    rows, width = oqs[0].shape[0], kb.shape[1]
+    pk = peak_lanes(pk_ref)
+    for h in range(heads):
+        left = slice(h * HD, (h + 1) * HD)
+        right = slice(width + h * HD, width + (h + 1) * HD)
+        log_total, _ = totals(sts, h)
+        weight = jnp.exp(sts[0][2 * h : 2 * h + 1, :] - log_total) * (pk[:, 2:3] / TOP)
+        oqa[:, left] = (ot_ref[left, :] * weight).astype(BF16).T
+        dq = mxu(kb[:, left], ds[h], TN) * (pk[:, 1:2] / (TOP * ROOT))
+        oqa[:, right] = dq.astype(BF16).T
     for s, ref in enumerate(oqs):
-        ref[...] = oqa[place_of(zh, groups, rows, s), :]
+        ref[...] = oqa[place_of(zh_ref[0], groups, rows, s), :]
 
 
 def fold_kernel(*refs):
@@ -215,32 +233,53 @@
     pk = lax.all_to_all(pk, axes, 0, 0, tiled=True)
     kvs = [one for two in zip(near, far) for one in two]
 
-    ot, stats, qs, gs, kb, vb = call(
+    square = like(F32, heads, k_rows, q_rows)
+    some_rows = like(F32, 8, q_rows)
+    e, ot, top, stats, qs, gs, kb, vb = call(
         functools.partial(forward_kernel, heads, groups, len(kvs)),
         "forward",
-        (like(F32, width, q_rows), like(F32, groups, 8, q_rows))
+        (square, like(F32, width, q_rows), some_rows, some_rows)
         + (like(BF16, q_rows, width),) * 2
         + (like(BF16, k_rows, width),) * 2,
         (zh, *qgs, *kvs, pk),
         flops=4 * pairs * HD,
         nbytes=4 * 2**20,
         exps=pairs,
+        limit=FORWARD_LIMIT,
         in_specs=[smem] + [vmem] * (groups + len(kvs) + 1),
     )
-    sts = lax.all_to_all(stats, "zh", 0, 0, tiled=True)
-    outs = call(
-        functools.partial(backward_kernel, heads, groups),
-        "backward",
-        (wide,) * groups + (like(BF16, k_rows // groups, 2 * width),) * groups,
-        (zh, stats, sts, pk, ot, qs, gs, kb, vb),
+    sts = home([stats] * groups, "zh")
+    dp = call(
+        functools.partial(middle_kernel, heads),
+        "middle",
+        square,
+        (gs, vb),
+        flops=2 * pairs * HD,
+        nbytes=8 * 2**20,
+        limit=WORK_LIMIT,
+    )
+    ds, *dkvs = call(
+        functools.partial(keys_kernel, heads, groups),
+        "keys",
+        (like(BF16, heads, k_rows, q_rows),) + (like(BF16, k_rows // groups, 2 * width),) * groups,
+        (*sts, pk, qs, gs, e, top, dp),
+        flops=4 * pairs * HD,
+        nbytes=6 * 2**20,
+        limit=WORK_LIMIT,
+    )
+    oqs = call(
+        functools.partial(queries_kernel, heads, groups),
+        "queries",
+        (wide,) * groups,
+        (zh, *sts, pk, ot, kb, ds),
         [pltpu.VMEM((q_rows, 2 * width), BF16)],
-        flops=10 * pairs * HD,
+        flops=2 * pairs * HD,
         nbytes=6 * 2**20,
-        exps=pairs,
-        in_specs=[smem] + [vmem] * 8,
-    )
-    dkvs = home(outs[groups:], "x")
-    oqs = home(outs[:groups], "zh")
+        limit=WORK_LIMIT,
+        in_specs=[smem] + [vmem] * (groups + 4),
+    )
+    dkvs = home(dkvs, "x")
+    oqs = home(oqs, "zh")
     own, send = call(fold_kernel, "fold", (like(F32, rows, 2 * width), wide), dkvs, nbytes=2 * 2**20)
     got = lax.ppermute(send, "zl", shift(2, 1))
     goq, gkv, tops = call(

time: 134 us -> 131 us (0.978)
  starting transfers between devices: 38.4 us -> 51.7 us
  blocking collectives: 36.1 us -> 23.8 us
  waiting for transfers between devices: 41.9 us -> 38.2 us
  Pallas kernels: 15.7 us -> 14 us
    all_to_all x1 -> x0, blocking collectives: 13.1 us -> none  [on_device(): sts = lax.all_to_all(stats, 'zh', 0, 0, tiled=True)]
    ppermute x6 -> x9, starting transfers between devices: 6.13 us -> 18.8 us  [home(): lax.ppermute(parts[s], axis, shift(n, n - s))]
    ppermute x6 -> x9, waiting for transfers between devices: 17.1 us -> 11.2 us  [home(): lax.ppermute(parts[s], axis, shift(n, n - s))]
    ppermute x1, waiting for transfers between devices: 7.52 us -> 9.67 us  [on_device(): got = lax.ppermute(send, 'zl', shift(2, 1))]
    pallas_call x6 -> x8, Pallas kernels: 15.7 us -> 14 us  [call(): pl.pallas_call(body, name=name, out_shape=out_shape, scratch_shapes=list(...]
  transfers between devices with their start and end apart: 18 -> 21, of which waited for: 7 -> 5; matrix products, arithmetic and copies ran while one was open for 0% -> 0% of each run, Pallas kernels for 0% -> 2%
where the time goes in v3:
time: 131 us; the launch traced here: 130 us
  starting transfers between devices  51.7 us (39%)
  waiting for transfers between devices  38.2 us (29%)
  blocking collectives  23.8 us (18%)
  Pallas kernels  14 us (11%)
  local copies, waits for them, and re-layouts  1.87 us (1%)
    all_to_all x1, blocking collectives, on_device(): tops = lax.all_to_all(tops, axes, 0, 0, tiled=True)  23.8 us
    ppermute x9, starting transfers between devices, spread(): return [x] + [lax.ppermute(x, axis, shift(n, s)) for s in range(1, n)]  20.6 us
    ppermute x9, starting transfers between devices, home(): lax.ppermute(parts[s], axis, shift(n, n - s))  18.8 us
    pallas_call x8, Pallas kernels, call(): pl.pallas_call(body, name=name, out_shape=out_shape, scratch_shapes=list(...  14 us
    ppermute x9, waiting for transfers between devices, home(): lax.ppermute(parts[s], axis, shift(n, n - s))  11.2 us
    all_to_all x1, starting transfers between devices, on_device(): pk = lax.all_to_all(pk, axes, 0, 0, tiled=True)  9.97 us
    ppermute x1, waiting for transfers between devices, on_device(): got = lax.ppermute(send, 'zl', shift(2, 1))  9.67 us
    all_to_all x1, waiting for transfers between devices, on_device(): pk = lax.all_to_all(pk, axes, 0, 0, tiled=True)  8.31 us
  transfers between devices with their start and end apart: 21, of which 5 were waited for; matrix products, arithmetic and copies ran while one was open for 0% of the time, Pallas kernels for 2%

profile of v3, /device:TPU:1, one launch (start us, length us, event | category | flops | bytes accessed | tf_op | source)
XLA Modules:
  0.0 130.3 jit_solution(12982930281701220772)
XLA Ops:
  0.6 2.0 %prep.1 = (bf16[144,768]{1,0:T(8,128)(2,1)}, bf16[144,768]{1,0:T(8,128)(2,1)}, f32[256,1,128]{2,1,0:T(1,128)}) custom-call(bf16[144,384]{1,0:T(8,128)(2,1)} %q_ref.1, bf16[144,384]{1,0:T(8,128)(2,1)} %k_ref.1, bf16[144,384]{1,0:T(8,128)(2,1)} %v_ref.1, bf16[144,384]{1,0:T(8,128)(2,1)} %g_ref.1), custom_call_target="tpu_custom_call" | custom-call | bytes 1048576 | tf_op jit(solution)/shard_map/prep/pallas_call | solution.py:31
  2.6 6.9 %collective-permute-start.2 = (bf16[144,768]{1,0:T(8,128)(2,1)}, bf16[144,768]{1,0:T(8,128)(2,1)S(1)}, u32[]{:S(2)}, u32[]{:S(2)}) collective-permute-start(bf16[144,768]{1,0:T(8,128)(2,1)} %get-tuple-element.29.refs_0_), channel_id=1, source_target_pairs={{0,48},{16,0},{32,16},{48,32},{1,49},{17,1},{33,17},{49,33},{2,50}... | collective-permute-start | bytes 663560 | tf_op jit(solution)/shard_map/ppermute | solution.py:193
  9.5 1.0 collective-permute-start.1
  10.5 0.9 collective-permute-start.3
  11.4 2.1 %collective-permute-start = (bf16[144,768]{1,0:T(8,128)(2,1)}, bf16[144,768]{1,0:T(8,128)(2,1)S(1)}, u32[]{:S(2)}, u32[]{:S(2)}) collective-permute-start(bf16[144,768]{1,0:T(8,128)(2,1)} %get-tuple-element.29.refs_0_), channel_id=1, source_target_pairs={{0,16},{16,32},{32,48},{48,0},{1,17},{17,33},{33,49},{49,1},{2,18}... | collective-permute-start | bytes 663560 | tf_op jit(solution)/shard_map/ppermute | solution.py:193
  13.5 2.5 %collective-permute-start.8 = (bf16[144,768]{1,0:T(8,128)(2,1)}, bf16[144,768]{1,0:T(8,128)(2,1)S(1)}, u32[]{:S(2)}, u32[]{:S(2)}) collective-permute-start(bf16[144,768]{1,0:T(8,128)(2,1)} %get-tuple-element.30.refs_4_), channel_id=1, source_target_pairs={{0,192},{64,0},{128,64},{192,128},{1,193},{65,1},{129,65},{193,129... | collective-permute-start | bytes 663560 | tf_op jit(solution)/shard_map/ppermute | solution.py:193
  16.0 10.0 %all-to-all-start = ((f32[256,1,128]{2,1,0:T(1,128)}), f32[256,1,128]{2,1,0:T(1,128)S(1)}, u32[]{:S(2)}, u32[]{:S(2)}) async-start(f32[256,1,128]{2,1,0:T(1,128)} %get-tuple-element.31), calls=%async_computation | async-start | bytes 262144 | tf_op jit(solution)/shard_map/all_to_all | solution.py:233
  26.0 3.0 %collective-permute-start.6 = (bf16[144,768]{1,0:T(8,128)(2,1)}, bf16[144,768]{1,0:T(8,128)(2,1)S(1)}, u32[]{:S(2)}, u32[]{:S(2)}) collective-permute-start(bf16[144,768]{1,0:T(8,128)(2,1)} %get-tuple-element.30.refs_4_), channel_id=1, source_target_pairs={{0,128},{64,192},{128,0},{192,64},{1,129},{65,193},{129,1},{193,65... | collective-permute-start | bytes 663560 | tf_op jit(solution)/shard_map/ppermute | solution.py:193
  29.0 1.0 collective-permute-start.4
  30.0 4.6 %collective-permute-done.3.refs_5_ = bf16[144,768]{1,0:T(8,128)(2,1)S(1)} collective-permute-done((bf16[144,768]{1,0:T(8,128)(2,1)}, bf16[144,768]{1,0:T(8,128)(2,1)S(1)}, u32[]{:S(2)}, u32[]{:S(2)}) %collective-permute-start.3) | collective-permute-done | bytes 221216 | tf_op jit(solution)/shard_map/ppermute | solution.py:229
  34.6 2.5 %collective-permute-start.9 = (bf16[144,768]{1,0:T(8,128)(2,1)S(1)}, bf16[144,768]{1,0:T(8,128)(2,1)S(1)}, u32[]{:S(2)}, u32[]{:S(2)}) collective-permute-start(bf16[144,768]{1,0:T(8,128)(2,1)S(1)} %collective-permute-done.3.refs_5_), channel_id=1, source_target_pairs={{0,192},{64,0},{128,64},{192,128},{1,193},{65,1},{129,65},{193,129... | collective-permute-start | bytes 663560 | tf_op jit(solution)/shard_map/ppermute | solution.py:193
  37.1 1.3 %collective-permute-start.7 = (bf16[144,768]{1,0:T(8,128)(2,1)S(1)}, bf16[144,768]{1,0:T(8,128)(2,1)S(1)}, u32[]{:S(2)}, u32[]{:S(2)}) collective-permute-start(bf16[144,768]{1,0:T(8,128)(2,1)S(1)} %collective-permute-done.3.refs_5_), channel_id=1, source_target_pairs={{0,128},{64,192},{128,0},{192,64},{1,129},{65,193},{129,1},{193,65... | collective-permute-start | bytes 663560 | tf_op jit(solution)/shard_map/ppermute | solution.py:193
  38.7 8.3 %all-to-all-done.refs_12_.refs_4_ = f32[256,1,128]{2,1,0:T(1,128)S(1)} async-done(((f32[256,1,128]{2,1,0:T(1,128)}), f32[256,1,128]{2,1,0:T(1,128)S(1)}, u32[]{:S(2)}, u32[]{:S(2)}) %all-to-all-start) | async-done | bytes 131104 | tf_op jit(solution)/shard_map/all_to_all | solution.py:233
  47.1 4.3 %collective-permute-done.5.refs_7_ = bf16[144,768]{1,0:T(8,128)(2,1)S(1)} collective-permute-done((bf16[144,768]{1,0:T(8,128)(2,1)S(1)}, bf16[144,768]{1,0:T(8,128)(2,1)S(1)}, u32[]{:S(2)}, u32[]{:S(2)}) %collective-permute-start.5) | collective-permute-done | bytes 221216 | tf_op jit(solution)/shard_map/ppermute | solution.py:193
  51.4 0.9 copy-done
  52.3 0.9 copy-done.1
  53.2 4.5 %forward.1 = (f32[3,1152,576]{2,1,0:T(8,128)S(1)}, f32[384,576]{1,0:T(8,128)S(1)}, f32[8,576]{1,0:T(8,128)S(1)}, f32[8,576]{1,0:T(8,128)S(1)}, bf16[576,384]{1,0...) custom-call(s32[1]{0:T(128)} %bitcast.zh_ref, ...), custom_call_target="tpu_custom_call" | custom-call | flops 1019215872 | bytes 4194304 | tf_op jit(solution)/shard_map/forward/pallas_call | solution.py:31
  57.7 1.9 %collective-permute-start.12 = (f32[8,576]{1,0:T(8,128)S(1)}, f32[8,576]{1,0:T(8,128)S(1)}, u32[]{:S(2)}, u32[]{:S(2)}) collective-permute-start(f32[8,576]{1,0:T(8,128)S(1)} %get-tuple-element.32.refs_0_), channel_id=1, source_target_pairs={{0,16},{16,32},{32,48},{48,0},{1,17},{17,33},{33,49},{49,1},{2,18}... | collective-permute-start | bytes 55304 | tf_op jit(solution)/shard_map/ppermute | solution.py:198
  59.6 4.3 %collective-permute-start.11 = (f32[8,576]{1,0:T(8,128)S(1)}, f32[8,576]{1,0:T(8,128)S(1)}, u32[]{:S(2)}, u32[]{:S(2)}) collective-permute-start(f32[8,576]{1,0:T(8,128)S(1)} %get-tuple-element.32.refs_0_), channel_id=1, source_target_pairs={{0,32},{16,48},{32,0},{48,16},{1,33},{17,49},{33,1},{49,17},{2,34}... | collective-permute-start | bytes 55304 | tf_op jit(solution)/shard_map/ppermute | solution.py:198
  63.9 2.5 %collective-permute-start.10 = (f32[8,576]{1,0:T(8,128)S(1)}, f32[8,576]{1,0:T(8,128)S(1)}, u32[]{:S(2)}, u32[]{:S(2)}) collective-permute-start(f32[8,576]{1,0:T(8,128)S(1)} %get-tuple-element.32.refs_0_), channel_id=1, source_target_pairs={{0,48},{16,0},{32,16},{48,32},{1,49},{17,1},{33,17},{49,33},{2,50}... | collective-permute-start | bytes 55304 | tf_op jit(solution)/shard_map/ppermute | solution.py:198
  66.4 1.3 %middle.1.refs_9_ = f32[3,1152,576]{2,1,0:T(8,128)S(1)} custom-call(bf16[576,384]{1,0:T(8,128)(2,1)S(1)} %get-tuple-element.34.gs.refs_6_, bf16[1152,384]{1,0:T(8,128)(2,1)S(1)} %get-tuple-element.37.vb), custom_call_target="tpu_custom_call" | custom-call | flops 509607936 | bytes 8388608 | tf_op jit(solution)/shard_map/middle/pallas_call | solution.py:31
  67.8 3.5 %keys.1 = (bf16[3,1152,576]{2,1,0:T(8,128)(2,1)S(1)}, bf16[288,768]{1,0:T(8,128)(2,1)S(1)}, bf16[288,768]{1,0:T(8,128)(2,1)S(1)}, bf16[288,768]{1,0:T(8,128)(2,1)S(1)}, bf16[288,768]{1,0:T(8,128)(2,1)S(1)}) custom-call(f32[8,576]{1,0:T(8,128)S(1)} %get-tuple-element.32.refs_0_, f32[8,576]{1,0:T(8,128)S(1)} %collective-permute-done.10.refs_1_, ...), custom_call_target="tpu_custom_call" | custom-call | flops 1019215872 | bytes 6291456 | tf_op jit(solution)/shard_map/keys/pallas_call | solution.py:31
  71.3 2.3 %collective-permute-start.14 = (bf16[288,768]{1,0:T(8,128)(2,1)S(1)}, bf16[288,768]{1,0:T(8,128)(2,1)S(1)}, u32[]{:S(2)}, u32[]{:S(2)}) collective-permute-start(bf16[288,768]{1,0:T(8,128)(2,1)S(1)} %get-tuple-element.40), channel_id=1, source_target_pairs={{0,128},{64,192},{128,0},{192,64},{1,129},{65,193},{129,1},{193,65... | collective-permute-start | bytes 1327112 | tf_op jit(solution)/shard_map/ppermute | solution.py:198
  74.3 1.3 queries.1
  75.6 2.8 %collective-permute-start.17 = (bf16[144,768]{1,0:T(8,128)(2,1)S(1)}, bf16[144,768]{1,0:T(8,128)(2,1)S(1)}, u32[]{:S(2)}, u32[]{:S(2)}) collective-permute-start(bf16[144,768]{1,0:T(8,128)(2,1)S(1)} %get-tuple-element.48), channel_id=1, source_target_pairs={{0,48},{16,0},{32,16},{48,32},{1,49},{17,1},{33,17},{49,33},{2,50}... | collective-permute-start | bytes 663560 | tf_op jit(solution)/shard_map/ppermute | solution.py:198
  78.4 1.7 %collective-permute-start.18 = (bf16[144,768]{1,0:T(8,128)(2,1)S(1)}, bf16[144,768]{1,0:T(8,128)(2,1)S(1)}, u32[]{:S(2)}, u32[]{:S(2)}) collective-permute-start(bf16[144,768]{1,0:T(8,128)(2,1)S(1)} %get-tuple-element.49), channel_id=1, source_target_pairs={{0,32},{16,48},{32,0},{48,16},{1,33},{17,49},{33,1},{49,17},{2,34}... | collective-permute-start | bytes 663560 | tf_op jit(solution)/shard_map/ppermute | solution.py:198
  80.1 2.6 %collective-permute-start.19 = (bf16[144,768]{1,0:T(8,128)(2,1)S(1)}, bf16[144,768]{1,0:T(8,128)(2,1)S(1)}, u32[]{:S(2)}, u32[]{:S(2)}) collective-permute-start(bf16[144,768]{1,0:T(8,128)(2,1)S(1)} %get-tuple-element.50), channel_id=1, source_target_pairs={{0,16},{16,32},{32,48},{48,0},{1,17},{17,33},{33,49},{49,1},{2,18}... | collective-permute-start | bytes 663560 | tf_op jit(solution)/shard_map/ppermute | solution.py:198
  82.7 11.2 %collective-permute-done.15.refs_3_ = bf16[288,768]{1,0:T(8,128)(2,1)S(1)} collective-permute-done((bf16[288,768]{1,0:T(8,128)(2,1)S(1)}, bf16[288,768]{1,0:T(8,128)(2,1)S(1)}, u32[]{:S(2)}, u32[]{:S(2)}) %collective-permute-start.15) | collective-permute-done | bytes 442400 | tf_op jit(solution)/shard_map/ppermute | solution.py:198
  94.1 1.4 %collective-permute-start.16 = (bf16[144,768]{1,0:T(8,128)(2,1)S(1)}, bf16[144,768]{1,0:T(8,128)(2,1)S(1)}, u32[]{:S(2)}, u32[]{:S(2)}) collective-permute-start(bf16[144,768]{1,0:T(8,128)(2,1)S(1)} %get-tuple-element.43), channel_id=1, source_target_pairs={{0,8},{8,0},{1,9},{9,1},{2,10},{10,2},{3,11},{11,3},{4,12},{12,4},... | collective-permute-start | bytes 663560 | tf_op jit(solution)/shard_map/ppermute | solution.py:284
  95.5 9.7 %collective-permute-done.16.got_ref = bf16[144,768]{1,0:T(8,128)(2,1)S(1)} collective-permute-done((bf16[144,768]{1,0:T(8,128)(2,1)S(1)}, bf16[144,768]{1,0:T(8,128)(2,1)S(1)}, u32[]{:S(2)}, u32[]{:S(2)}) %collective-permute-start.16) | collective-permute-done | bytes 221216 | tf_op jit(solution)/shard_map/ppermute | solution.py:284
  105.6 23.8 %all_to_all.10.pk_ref = f32[256,1,128]{2,1,0:T(1,128)S(1)} all-to-all(f32[256,1,128]{2,1,0:T(1,128)S(1)} %get-tuple-element.53), channel_id=1, replica_groups=mesh['x'=4,'zh'=4,'zl'=2,'y'=4,'c'=2] {'x','zh','zl','y','c'}, dimensions={0} | all-to-all | bytes 262144 | tf_op jit(solution)/shard_map/all_to_all | solution.py:292
  129.4 0.9 cast.1
  (23 shorter events, 1.6 us)
Async XLA Ops:
  2.6 23.4 %collective-permute-start.2 = (bf16[144,768]{1,0:T(8,128)(2,1)}, bf16[144,768]{1,0:T(8,128)(2,1)S(1)}, u32[]{:S(2)}, u32[]{:S(2)}) collective-permute-start(bf16[144,768]{1,0:T(8,128)(2,1)} %get-tuple-element.29.refs_0_), channel_id=1, source_target_pairs={{0,48},{16,0},{32,16},{48,32},{1,49},{17,1},{33,17},{49,33},{2,50}... | collective-permute-start | bytes 663560 | tf_op jit(solution)/shard_map/ppermute | solution.py:193
  9.5 19.4 %collective-permute-start.1 = (bf16[144,768]{1,0:T(8,128)(2,1)}, bf16[144,768]{1,0:T(8,128)(2,1)S(1)}, u32[]{:S(2)}, u32[]{:S(2)}) collective-permute-start(bf16[144,768]{1,0:T(8,128)(2,1)} %get-tuple-element.29.refs_0_), channel_id=1, source_target_pairs={{0,32},{16,48},{32,0},{48,16},{1,33},{17,49},{33,1},{49,17},{2,34}... | collective-permute-start | bytes 663560 | tf_op jit(solution)/shard_map/ppermute | solution.py:193
  10.5 24.1 %collective-permute-start.3 = (bf16[144,768]{1,0:T(8,128)(2,1)}, bf16[144,768]{1,0:T(8,128)(2,1)S(1)}, u32[]{:S(2)}, u32[]{:S(2)}) collective-permute-start(bf16[144,768]{1,0:T(8,128)(2,1)} %get-tuple-element.30.refs_4_), channel_id=1, source_target_pairs={{0,8},{8,0},{1,9},{9,1},{2,10},{10,2},{3,11},{11,3},{4,12},{12,4},... | collective-permute-start | bytes 663560 | tf_op jit(solution)/shard_map/ppermute | solution.py:229
  11.4 25.7 %collective-permute-start = (bf16[144,768]{1,0:T(8,128)(2,1)}, bf16[144,768]{1,0:T(8,128)(2,1)S(1)}, u32[]{:S(2)}, u32[]{:S(2)}) collective-permute-start(bf16[144,768]{1,0:T(8,128)(2,1)} %get-tuple-element.29.refs_0_), channel_id=1, source_target_pairs={{0,16},{16,32},{32,48},{48,0},{1,17},{17,33},{33,49},{49,1},{2,18}... | collective-permute-start | bytes 663560 | tf_op jit(solution)/shard_map/ppermute | solution.py:193
  13.5 24.9 %collective-permute-start.8 = (bf16[144,768]{1,0:T(8,128)(2,1)}, bf16[144,768]{1,0:T(8,128)(2,1)S(1)}, u32[]{:S(2)}, u32[]{:S(2)}) collective-permute-start(bf16[144,768]{1,0:T(8,128)(2,1)} %get-tuple-element.30.refs_4_), channel_id=1, source_target_pairs={{0,192},{64,0},{128,64},{192,128},{1,193},{65,1},{129,65},{193,129... | collective-permute-start | bytes 663560 | tf_op jit(solution)/shard_map/ppermute | solution.py:193
  16.0 31.0 %all-to-all-start = ((f32[256,1,128]{2,1,0:T(1,128)}), f32[256,1,128]{2,1,0:T(1,128)S(1)}, u32[]{:S(2)}, u32[]{:S(2)}) async-start(f32[256,1,128]{2,1,0:T(1,128)} %get-tuple-element.31), calls=%async_computation | async-start | bytes 262144 | tf_op jit(solution)/shard_map/all_to_all | solution.py:233
  26.0 12.7 %collective-permute-start.6 = (bf16[144,768]{1,0:T(8,128)(2,1)}, bf16[144,768]{1,0:T(8,128)(2,1)S(1)}, u32[]{:S(2)}, u32[]{:S(2)}) collective-permute-start(bf16[144,768]{1,0:T(8,128)(2,1)} %get-tuple-element.30.refs_4_), channel_id=1, source_target_pairs={{0,128},{64,192},{128,0},{192,64},{1,129},{65,193},{129,1},{193,65... | collective-permute-start | bytes 663560 | tf_op jit(solution)/shard_map/ppermute | solution.py:193
  29.0 9.8 %collective-permute-start.4 = (bf16[144,768]{1,0:T(8,128)(2,1)}, bf16[144,768]{1,0:T(8,128)(2,1)S(1)}, u32[]{:S(2)}, u32[]{:S(2)}) collective-permute-start(bf16[144,768]{1,0:T(8,128)(2,1)} %get-tuple-element.30.refs_4_), channel_id=1, source_target_pairs={{0,64},{64,128},{128,192},{192,0},{1,65},{65,129},{129,193},{193,1... | collective-permute-start | bytes 663560 | tf_op jit(solution)/shard_map/ppermute | solution.py:193
  34.6 12.4 %collective-permute-start.9 = (bf16[144,768]{1,0:T(8,128)(2,1)S(1)}, bf16[144,768]{1,0:T(8,128)(2,1)S(1)}, u32[]{:S(2)}, u32[]{:S(2)}) collective-permute-start(bf16[144,768]{1,0:T(8,128)(2,1)S(1)} %collective-permute-done.3.refs_5_), channel_id=1, source_target_pairs={{0,192},{64,0},{128,64},{192,128},{1,193},{65,1},{129,65},{193,129... | collective-permute-start | bytes 663560 | tf_op jit(solution)/shard_map/ppermute | solution.py:193
  37.1 10.0 %collective-permute-start.7 = (bf16[144,768]{1,0:T(8,128)(2,1)S(1)}, bf16[144,768]{1,0:T(8,128)(2,1)S(1)}, u32[]{:S(2)}, u32[]{:S(2)}) collective-permute-start(bf16[144,768]{1,0:T(8,128)(2,1)S(1)} %collective-permute-done.3.refs_5_), channel_id=1, source_target_pairs={{0,128},{64,192},{128,0},{192,64},{1,129},{65,193},{129,1},{193,65... | collective-permute-start | bytes 663560 | tf_op jit(solution)/shard_map/ppermute | solution.py:193
  38.4 12.9 %collective-permute-start.5 = (bf16[144,768]{1,0:T(8,128)(2,1)S(1)}, bf16[144,768]{1,0:T(8,128)(2,1)S(1)}, u32[]{:S(2)}, u32[]{:S(2)}) collective-permute-start(bf16[144,768]{1,0:T(8,128)(2,1)S(1)} %collective-permute-done.3.refs_5_), channel_id=1, source_target_pairs={{0,64},{64,128},{128,192},{192,0},{1,65},{65,129},{129,193},{193,1... | collective-permute-start | bytes 663560 | tf_op jit(solution)/shard_map/ppermute | solution.py:193
  51.4 0.9 copy-start
  52.3 0.9 copy-start.1
  57.7 10.0 %collective-permute-start.12 = (f32[8,576]{1,0:T(8,128)S(1)}, f32[8,576]{1,0:T(8,128)S(1)}, u32[]{:S(2)}, u32[]{:S(2)}) collective-permute-start(f32[8,576]{1,0:T(8,128)S(1)} %get-tuple-element.32.refs_0_), channel_id=1, source_target_pairs={{0,16},{16,32},{32,48},{48,0},{1,17},{17,33},{33,49},{49,1},{2,18}... | collective-permute-start | bytes 55304 | tf_op jit(solution)/shard_map/ppermute | solution.py:198
  59.6 8.2 %collective-permute-start.11 = (f32[8,576]{1,0:T(8,128)S(1)}, f32[8,576]{1,0:T(8,128)S(1)}, u32[]{:S(2)}, u32[]{:S(2)}) collective-permute-start(f32[8,576]{1,0:T(8,128)S(1)} %get-tuple-element.32.refs_0_), channel_id=1, source_target_pairs={{0,32},{16,48},{32,0},{48,16},{1,33},{17,49},{33,1},{49,17},{2,34}... | collective-permute-start | bytes 55304 | tf_op jit(solution)/shard_map/ppermute | solution.py:198
  63.9 3.9 %collective-permute-start.10 = (f32[8,576]{1,0:T(8,128)S(1)}, f32[8,576]{1,0:T(8,128)S(1)}, u32[]{:S(2)}, u32[]{:S(2)}) collective-permute-start(f32[8,576]{1,0:T(8,128)S(1)} %get-tuple-element.32.refs_0_), channel_id=1, source_target_pairs={{0,48},{16,0},{32,16},{48,32},{1,49},{17,1},{33,17},{49,33},{2,50}... | collective-permute-start | bytes 55304 | tf_op jit(solution)/shard_map/ppermute | solution.py:198
  71.2 8.9 %collective-permute-start.13 = (bf16[288,768]{1,0:T(8,128)(2,1)S(1)}, bf16[288,768]{1,0:T(8,128)(2,1)S(1)}, u32[]{:S(2)}, u32[]{:S(2)}) collective-permute-start(bf16[288,768]{1,0:T(8,128)(2,1)S(1)} %get-tuple-element.39), channel_id=1, source_target_pairs={{0,192},{64,0},{128,64},{192,128},{1,193},{65,1},{129,65},{193,129... | collective-permute-start | bytes 1327112 | tf_op jit(solution)/shard_map/ppermute | solution.py:198
  71.3 11.3 %collective-permute-start.14 = (bf16[288,768]{1,0:T(8,128)(2,1)S(1)}, bf16[288,768]{1,0:T(8,128)(2,1)S(1)}, u32[]{:S(2)}, u32[]{:S(2)}) collective-permute-start(bf16[288,768]{1,0:T(8,128)(2,1)S(1)} %get-tuple-element.40), channel_id=1, source_target_pairs={{0,128},{64,192},{128,0},{192,64},{1,129},{65,193},{129,1},{193,65... | collective-permute-start | bytes 1327112 | tf_op jit(solution)/shard_map/ppermute | solution.py:198
  73.7 20.2 %collective-permute-start.15 = (bf16[288,768]{1,0:T(8,128)(2,1)S(1)}, bf16[288,768]{1,0:T(8,128)(2,1)S(1)}, u32[]{:S(2)}, u32[]{:S(2)}) collective-permute-start(bf16[288,768]{1,0:T(8,128)(2,1)S(1)} %get-tuple-element.41), channel_id=1, source_target_pairs={{0,64},{64,128},{128,192},{192,0},{1,65},{65,129},{129,193},{193,1... | collective-permute-start | bytes 1327112 | tf_op jit(solution)/shard_map/ppermute | solution.py:198
  75.6 19.9 %collective-permute-start.17 = (bf16[144,768]{1,0:T(8,128)(2,1)S(1)}, bf16[144,768]{1,0:T(8,128)(2,1)S(1)}, u32[]{:S(2)}, u32[]{:S(2)}) collective-permute-start(bf16[144,768]{1,0:T(8,128)(2,1)S(1)} %get-tuple-element.48), channel_id=1, source_target_pairs={{0,48},{16,0},{32,16},{48,32},{1,49},{17,1},{33,17},{49,33},{2,50}... | collective-permute-start | bytes 663560 | tf_op jit(solution)/shard_map/ppermute | solution.py:198
  78.4 17.1 %collective-permute-start.18 = (bf16[144,768]{1,0:T(8,128)(2,1)S(1)}, bf16[144,768]{1,0:T(8,128)(2,1)S(1)}, u32[]{:S(2)}, u32[]{:S(2)}) collective-permute-start(bf16[144,768]{1,0:T(8,128)(2,1)S(1)} %get-tuple-element.49), channel_id=1, source_target_pairs={{0,32},{16,48},{32,0},{48,16},{1,33},{17,49},{33,1},{49,17},{2,34}... | collective-permute-start | bytes 663560 | tf_op jit(solution)/shard_map/ppermute | solution.py:198
  80.1 15.4 %collective-permute-start.19 = (bf16[144,768]{1,0:T(8,128)(2,1)S(1)}, bf16[144,768]{1,0:T(8,128)(2,1)S(1)}, u32[]{:S(2)}, u32[]{:S(2)}) collective-permute-start(bf16[144,768]{1,0:T(8,128)(2,1)S(1)} %get-tuple-element.50), channel_id=1, source_target_pairs={{0,16},{16,32},{32,48},{48,0},{1,17},{17,33},{33,49},{49,1},{2,18}... | collective-permute-start | bytes 663560 | tf_op jit(solution)/shard_map/ppermute | solution.py:198
  94.1 11.1 %collective-permute-start.16 = (bf16[144,768]{1,0:T(8,128)(2,1)S(1)}, bf16[144,768]{1,0:T(8,128)(2,1)S(1)}, u32[]{:S(2)}, u32[]{:S(2)}) collective-permute-start(bf16[144,768]{1,0:T(8,128)(2,1)S(1)} %get-tuple-element.43), channel_id=1, source_target_pairs={{0,8},{8,0},{1,9},{9,1},{2,10},{10,2},{3,11},{11,3},{4,12},{12,4},... | collective-permute-start | bytes 663560 | tf_op jit(solution)/shard_map/ppermute | solution.py:284

commit v4 on v3

--- a/solution.py
+++ b/solution.py
@@ -78,40 +78,75 @@
     return pl.ds(pl.multiple_of(lax.rem(zh + groups - s, groups) * rows, 16), rows)
 
 
-def forward_kernel(heads, groups, shards, zh_ref, *refs):
-    qgs, kvs = refs[:groups], refs[groups : groups + shards]
-    pk_ref, e_ref, ot_ref, row_ref, st_ref, qs, gs, kb, vb = refs[groups + shards :]
-    rows, width = qgs[0].shape[0], qs.shape[1]
-    pk = peak_lanes(pk_ref)
-    pq, pkk, pv, pg = (pk[:, i : i + 1] for i in range(4))
-    zh = zh_ref[0]
-    for s, ref in enumerate(qgs):
-        qs[place_of(zh, groups, rows, s), :] = scaled(ref[:, :width], TOP / pq)
-        gs[place_of(zh, groups, rows, s), :] = scaled(ref[:, width:], TOP / pg)
-    for s, ref in enumerate(kvs):
-        kb[s * rows : (s + 1) * rows, :] = scaled(ref[:, :width], TOP / pkk)
-        vb[s * rows : (s + 1) * rows, :] = scaled(ref[:, width:], TOP / pv)
+def half_pass(heads, pk, qs, gs, kb, vb, e_ref):
+    pq, pkk = pk[:, 0:1], pk[:, 1:2]
     score_scale = pq * pkk / (TOP * TOP * ROOT)
-    st_ref[...] = jnp.zeros_like(st_ref)
-    row_ref[...] = jnp.zeros_like(row_ref)
+    to_power = score_scale * math.log2(math.e)
+    found = []
     for h in range(heads):
         cols = slice(h * HD, (h + 1) * HD)
-        s = mxu(kb[:, cols], qs[:, cols], NT) * score_scale
-        m = jnp.max(s, axis=0, keepdims=True)
-        e = jnp.exp(s - m)
+        s = mxu(kb[:, cols], qs[:, cols], NT)
+        peak = jnp.max(s, axis=0, keepdims=True)
+        e = jnp.exp2(s * to_power - peak * to_power)
+        m = peak * score_scale
         e_ref[h] = e
         total = jnp.sum(e, axis=0, keepdims=True)
         o = mxu(vb[:, cols], e.astype(BF16), TN) / total
-        ot_ref[cols, :] = o
+        d = jnp.sum(o * gs[:, cols].T.astype(F32), axis=0, keepdims=True)
+        found.append((m, m + jnp.log(total), d, o))
+    return found
+
+
+def load_keys(parts, pk, kb, vb):
+    rows, width = parts[0].shape[0], kb.shape[1]
+    for s, ref in enumerate(parts):
+        kb[s * rows : (s + 1) * rows, :] = scaled(ref[:, :width], TOP / pk[:, 1:2])
+        vb[s * rows : (s + 1) * rows, :] = scaled(ref[:, width:], TOP / pk[:, 2:3])
+
+
+def near_kernel(heads, groups, zh_ref, *refs):
+    qgs, near = refs[:groups], refs[groups : 2 * groups]
+    pk_ref, qs, gs, kb, vb, e_ref, ot_ref, row_ref = refs[2 * groups :]
+    rows, width = qgs[0].shape[0], qs.shape[1]
+    pk = peak_lanes(pk_ref)
+    zh = zh_ref[0]
+    for s, ref in enumerate(qgs):
+        qs[place_of(zh, groups, rows, s), :] = scaled(ref[:, :width], TOP / pk[:, 0:1])
+        gs[place_of(zh, groups, rows, s), :] = scaled(ref[:, width:], TOP / pk[:, 3:4])
+    load_keys(near, pk, kb, vb)
+    row_ref[...] = jnp.zeros_like(row_ref)
+    for h, (m, lse, d, o) in enumerate(half_pass(heads, pk, qs, gs, kb, vb, e_ref)):
+        ot_ref[h * HD : (h + 1) * HD, :] = o
+        for i, row in enumerate((m, lse, d)):
+            row_ref[3 * h + i : 3 * h + i + 1, :] = row
+
+
+def far_kernel(heads, groups, *refs):
+    far = refs[:groups]
+    pk_ref, qs, gs, ot1_ref, row1_ref, kb, vb, e_ref, ot_ref, row_ref, st_ref = refs[groups:]
+    pk = peak_lanes(pk_ref)
+    load_keys(far, pk, kb, vb)
+    row_ref[...] = jnp.zeros_like(row_ref)
+    stats = []
+    for h, (m, lse, d, o) in enumerate(half_pass(heads, pk, qs, gs, kb, vb, e_ref)):
+        cols = slice(h * HD, (h + 1) * HD)
+        lse1, d1 = (row1_ref[3 * h + i : 3 * h + i + 1, :] for i in (1, 2))
+        top = jnp.maximum(lse, lse1)
+        both = top + jnp.log(jnp.exp(lse - top) + jnp.exp(lse1 - top))
+        w, w1 = jnp.exp(lse - both), jnp.exp(lse1 - both)
+        ot_ref[cols, :] = w * o + w1 * ot1_ref[cols, :]
         row_ref[h : h + 1, :] = m
-        st_ref[2 * h : 2 * h + 1, :] = m + jnp.log(total)
-        st_ref[2 * h + 1 : 2 * h + 2, :] = jnp.sum(o * gs[:, cols].T.astype(F32), axis=0, keepdims=True)
-
-
-def middle_kernel(heads, gs, vb, dp):
+        stats += [both, w * d + w1 * d1]
+    st_ref[...] = jnp.zeros_like(st_ref)
+    for i, row in enumerate(stats):
+        st_ref[i : i + 1, :] = row
+
+
+def middle_kernel(heads, gs, vb1, vb2, dp1, dp2):
     for h in range(heads):
         cols = slice(h * HD, (h + 1) * HD)
-        dp[h] = mxu(vb[:, cols], gs[:, cols], NT)
+        for vb, dp in ((vb1, dp1), (vb2, dp2)):
+            dp[h] = mxu(vb[:, cols], gs[:, cols], NT)
 
 
 def totals(sts, h):
@@ -123,31 +158,36 @@
 
 
 def keys_kernel(heads, groups, *refs):
-    sts, (pk_ref, qs, gs, e, row_ref, dp, ds), dkvs = refs[:groups], refs[groups : groups + 7], refs[groups + 7 :]
+    sts, dkvs = refs[:groups], refs[-groups:]
+    pk_ref, qs, gs, e1, e2, row1_ref, row2_ref, dp1, dp2, ds1, ds2 = refs[groups:-groups]
     pk = peak_lanes(pk_ref)
     pq, pkk, pv, pg = (pk[:, i : i + 1] for i in range(4))
     grad_scale = pg * pv / (TOP * TOP)
     width = qs.shape[1]
-    span = e.shape[1] // groups
+    rows = e1.shape[1] // groups
     for h in range(heads):
         left = slice(h * HD, (h + 1) * HD)
         right = slice(width + h * HD, width + (h + 1) * HD)
         log_total, delta = totals(sts, h)
-        p = e[h] * jnp.exp(row_ref[h : h + 1, :] - log_total)
-        dv = mxu(p.astype(BF16), gs[:, left], NN) * (pg / TOP)
-        d = (p * (dp[h] * grad_scale - delta * grad_scale)).astype(BF16)
-        ds[h] = d
-        dk = mxu(d, qs[:, left], NN) * (pq / (TOP * ROOT))
-        for s, ref in enumerate(dkvs):
-            part = slice(s * span, (s + 1) * span)
-            ref[:, left] = dk[part].astype(BF16)
-            ref[:, right] = dv[part].astype(BF16)
+        delta = delta * grad_scale
+        q, g = qs[:, left], gs[:, left]
+        halves = ((e1, row1_ref[3 * h : 3 * h + 1, :], dp1, ds1), (e2, row2_ref[h : h + 1, :], dp2, ds2))
+        for half, (e, m, dp, ds) in enumerate(halves):
+            p = e[h] * jnp.exp(m - log_total)
+            dv = mxu(p.astype(BF16), g, NN) * (pg / TOP)
+            d = (p * (dp[h] * grad_scale - delta)).astype(BF16)
+            ds[h] = d
+            dk = mxu(d, q, NN) * (pq / (TOP * ROOT))
+            for s, ref in enumerate(dkvs):
+                part, to = slice(s * rows, (s + 1) * rows), slice(half * rows, (half + 1) * rows)
+                ref[to, left] = dk[part].astype(BF16)
+                ref[to, right] = dv[part].astype(BF16)
 
 
 def queries_kernel(heads, groups, zh_ref, *refs):
-    sts, (pk_ref, ot_ref, kb, ds) = refs[:groups], refs[groups : groups + 4]
-    oqs, oqa = refs[groups + 4 : -1], refs[-1]
-    rows, width = oqs[0].shape[0], kb.shape[1]
+    sts, (pk_ref, ot_ref, kb1, kb2, ds1, ds2) = refs[:groups], refs[groups : groups + 6]
+    oqs, oqa = refs[groups + 6 : -1], refs[-1]
+    rows, width = oqs[0].shape[0], kb1.shape[1]
     pk = peak_lanes(pk_ref)
     for h in range(heads):
         left = slice(h * HD, (h + 1) * HD)
@@ -155,7 +195,8 @@
         log_total, _ = totals(sts, h)
         weight = jnp.exp(sts[0][2 * h : 2 * h + 1, :] - log_total) * (pk[:, 2:3] / TOP)
         oqa[:, left] = (ot_ref[left, :] * weight).astype(BF16).T
-        dq = mxu(kb[:, left], ds[h], TN) * (pk[:, 1:2] / (TOP * ROOT))
+        dq = mxu(kb1[:, left], ds1[h], TN) + mxu(kb2[:, left], ds2[h], TN)
+        dq = dq * (pk[:, 1:2] / (TOP * ROOT))
         oqa[:, right] = dq.astype(BF16).T
     for s, ref in enumerate(oqs):
         ref[...] = oqa[place_of(zh_ref[0], groups, rows, s), :]
@@ -231,38 +272,47 @@
     qgs = spread(qg, "zh", groups)
     far = spread(twin, "x", sizes["x"])
     pk = lax.all_to_all(pk, axes, 0, 0, tiled=True)
-    kvs = [one for two in zip(near, far) for one in two]
-
-    square = like(F32, heads, k_rows, q_rows)
-    some_rows = like(F32, 8, q_rows)
-    e, ot, top, stats, qs, gs, kb, vb = call(
-        functools.partial(forward_kernel, heads, groups, len(kvs)),
-        "forward",
-        (square, like(F32, width, q_rows), some_rows, some_rows)
-        + (like(BF16, q_rows, width),) * 2
-        + (like(BF16, k_rows, width),) * 2,
-        (zh, *qgs, *kvs, pk),
-        flops=4 * pairs * HD,
+    half = like(BF16, q_rows, width)
+    square = like(F32, heads, q_rows, q_rows)
+    some_rows = like(F32, 16, q_rows)
+    outputs = like(F32, width, q_rows)
+    qs, gs, kb1, vb1, e1, ot1, row1 = call(
+        functools.partial(near_kernel, heads, groups),
+        "near",
+        (half,) * 4 + (square, outputs, some_rows),
+        (zh, *qgs, *near, pk),
+        flops=2 * pairs * HD,
         nbytes=4 * 2**20,
-        exps=pairs,
+        exps=pairs // 2,
         limit=FORWARD_LIMIT,
-        in_specs=[smem] + [vmem] * (groups + len(kvs) + 1),
+        in_specs=[smem] + [vmem] * (2 * groups + 1),
+    )
+    kb2, vb2, e2, ot, row2, stats = call(
+        functools.partial(far_kernel, heads, groups),
+        "far",
+        (half,) * 2 + (square, outputs, some_rows, like(F32, 8, q_rows)),
+        (*far, pk, qs, gs, ot1, row1),
+        flops=2 * pairs * HD,
+        nbytes=4 * 2**20,
+        exps=pairs // 2,
+        limit=FORWARD_LIMIT,
     )
     sts = home([stats] * groups, "zh")
-    dp = call(
+    dp1, dp2 = call(
         functools.partial(middle_kernel, heads),
         "middle",
-        square,
-        (gs, vb),
+        (square, square),
+        (gs, vb1, vb2),
         flops=2 * pairs * HD,
         nbytes=8 * 2**20,
         limit=WORK_LIMIT,
     )
-    ds, *dkvs = call(
+    edges = like(BF16, heads, q_rows, q_rows)
+    ds1, ds2, *dkvs = call(
         functools.partial(keys_kernel, heads, groups),
         "keys",
-        (like(BF16, heads, k_rows, q_rows),) + (like(BF16, k_rows // groups, 2 * width),) * groups,
-        (*sts, pk, qs, gs, e, top, dp),
+        (edges, edges) + (like(BF16, 2 * rows, 2 * width),) * groups,
+        (*sts, pk, qs, gs, e1, e2, row1, row2, dp1, dp2),
         flops=4 * pairs * HD,
         nbytes=6 * 2**20,
         limit=WORK_LIMIT,
@@ -271,12 +321,12 @@
         functools.partial(queries_kernel, heads, groups),
         "queries",
         (wide,) * groups,
-        (zh, *sts, pk, ot, kb, ds),
+        (zh, *sts, pk, ot, kb1, kb2, ds1, ds2),
         [pltpu.VMEM((q_rows, 2 * width), BF16)],
         flops=2 * pairs * HD,
         nbytes=6 * 2**20,
         limit=WORK_LIMIT,
-        in_specs=[smem] + [vmem] * (groups + 4),
+        in_specs=[smem] + [vmem] * (groups + 6),
     )
     dkvs = home(dkvs, "x")
     oqs = home(oqs, "zh")

time: 131 us -> 127 us (0.969)
  waiting for transfers between devices: 38.2 us -> 34.3 us
    ppermute x9, waiting for transfers between devices: 4.32 us -> 0.02 us  [spread(): return [x] + [lax.ppermute(x, axis, shift(n, s)) for s in range(1, n)]]
    pallas_call x8 -> x9, Pallas kernels: 14 us -> 14.9 us  [call(): pl.pallas_call(body, name=name, out_shape=out_shape, scratch_shapes=list(...]
  transfers between devices with their start and end apart: 21 -> 21, of which waited for: 5 -> 4; matrix products, arithmetic and copies ran while one was open for 0% -> 0% of each run, Pallas kernels for 2% -> 4%
where the time goes in v4:
time: 127 us
  starting transfers between devices  51.2 us (40%)
  waiting for transfers between devices  34.3 us (27%)
  blocking collectives  23.7 us (19%)
  Pallas kernels  14.9 us (12%)
  local copies, waits for them, and re-layouts  1.87 us (1%)
    all_to_all x1, blocking collectives, on_device(): tops = lax.all_to_all(tops, axes, 0, 0, tiled=True)  23.7 us
    ppermute x9, starting transfers between devices, spread(): return [x] + [lax.ppermute(x, axis, shift(n, s)) for s in range(1, n)]  20.6 us
    ppermute x9, starting transfers between devices, home(): lax.ppermute(parts[s], axis, shift(n, n - s))  18.5 us
    pallas_call x9, Pallas kernels, call(): pl.pallas_call(body, name=name, out_shape=out_shape, scratch_shapes=list(...  14.9 us
    ppermute x9, waiting for transfers between devices, home(): lax.ppermute(parts[s], axis, shift(n, n - s))  11.6 us
    all_to_all x1, starting transfers between devices, on_device(): pk = lax.all_to_all(pk, axes, 0, 0, tiled=True)  9.97 us
    ppermute x1, waiting for transfers between devices, on_device(): got = lax.ppermute(send, 'zl', shift(2, 1))  9.65 us
    all_to_all x1, waiting for transfers between devices, on_device(): pk = lax.all_to_all(pk, axes, 0, 0, tiled=True)  8.31 us
  transfers between devices with their start and end apart: 21, of which 4 were waited for; matrix products, arithmetic and copies ran while one was open for 0% of the time, Pallas kernels for 4%

profile of v4, /device:TPU:1, one launch (start us, length us, event | category | flops | bytes accessed | tf_op | source)
XLA Modules:
  0.0 126.7 jit_solution(16907909359368559820)
XLA Ops:
  0.6 2.0 %prep.1 = (bf16[144,768]{1,0:T(8,128)(2,1)}, bf16[144,768]{1,0:T(8,128)(2,1)}, f32[256,1,128]{2,1,0:T(1,128)}) custom-call(bf16[144,384]{1,0:T(8,128)(2,1)} %q_ref.1, bf16[144,384]{1,0:T(8,128)(2,1)} %k_ref.1, bf16[144,384]{1,0:T(8,128)(2,1)} %v_ref.1, bf16[144,384]{1,0:T(8,128)(2,1)} %g_ref.1), custom_call_target="tpu_custom_call" | custom-call | bytes 1048576 | tf_op jit(solution)/shard_map/prep/pallas_call | solution.py:31
  2.6 6.9 %collective-permute-start.6 = (bf16[144,768]{1,0:T(8,128)(2,1)}, bf16[144,768]{1,0:T(8,128)(2,1)S(1)}, u32[]{:S(2)}, u32[]{:S(2)}) collective-permute-start(bf16[144,768]{1,0:T(8,128)(2,1)} %get-tuple-element.39.refs_0_), channel_id=1, source_target_pairs={{0,48},{16,0},{32,16},{48,32},{1,49},{17,1},{33,17},{49,33},{2,50}... | collective-permute-start | bytes 663560 | tf_op jit(solution)/shard_map/ppermute | solution.py:234
  9.5 1.0 collective-permute-start.5
  10.5 0.9 collective-permute-start
  11.4 2.1 %collective-permute-start.4 = (bf16[144,768]{1,0:T(8,128)(2,1)}, bf16[144,768]{1,0:T(8,128)(2,1)S(1)}, u32[]{:S(2)}, u32[]{:S(2)}) collective-permute-start(bf16[144,768]{1,0:T(8,128)(2,1)} %get-tuple-element.39.refs_0_), channel_id=1, source_target_pairs={{0,16},{16,32},{32,48},{48,0},{1,17},{17,33},{33,49},{49,1},{2,18}... | collective-permute-start | bytes 663560 | tf_op jit(solution)/shard_map/ppermute | solution.py:234
  13.5 2.5 %collective-permute-start.9 = (bf16[144,768]{1,0:T(8,128)(2,1)}, bf16[144,768]{1,0:T(8,128)(2,1)S(1)}, u32[]{:S(2)}, u32[]{:S(2)}) collective-permute-start(bf16[144,768]{1,0:T(8,128)(2,1)} %get-tuple-element.37.refs_4_), channel_id=1, source_target_pairs={{0,192},{64,0},{128,64},{192,128},{1,193},{65,1},{129,65},{193,129... | collective-permute-start | bytes 663560 | tf_op jit(solution)/shard_map/ppermute | solution.py:234
  16.0 10.0 %all-to-all-start = ((f32[256,1,128]{2,1,0:T(1,128)}), f32[256,1,128]{2,1,0:T(1,128)S(1)}, u32[]{:S(2)}, u32[]{:S(2)}) async-start(f32[256,1,128]{2,1,0:T(1,128)} %get-tuple-element.38), calls=%async_computation | async-start | bytes 262144 | tf_op jit(solution)/shard_map/all_to_all | solution.py:274
  26.0 3.0 %collective-permute-start.8 = (bf16[144,768]{1,0:T(8,128)(2,1)}, bf16[144,768]{1,0:T(8,128)(2,1)S(1)}, u32[]{:S(2)}, u32[]{:S(2)}) collective-permute-start(bf16[144,768]{1,0:T(8,128)(2,1)} %get-tuple-element.37.refs_4_), channel_id=1, source_target_pairs={{0,128},{64,192},{128,0},{192,64},{1,129},{65,193},{129,1},{193,65... | collective-permute-start | bytes 663560 | tf_op jit(solution)/shard_map/ppermute | solution.py:234
  29.0 1.0 collective-permute-start.7
  30.0 4.6 %collective-permute-done.refs_0_ = bf16[144,768]{1,0:T(8,128)(2,1)S(1)} collective-permute-done((bf16[144,768]{1,0:T(8,128)(2,1)}, bf16[144,768]{1,0:T(8,128)(2,1)S(1)}, u32[]{:S(2)}, u32[]{:S(2)}) %collective-permute-start) | collective-permute-done | bytes 221216 | tf_op jit(solution)/shard_map/ppermute | solution.py:270
  34.6 2.5 %collective-permute-start.3 = (bf16[144,768]{1,0:T(8,128)(2,1)S(1)}, bf16[144,768]{1,0:T(8,128)(2,1)S(1)}, u32[]{:S(2)}, u32[]{:S(2)}) collective-permute-start(bf16[144,768]{1,0:T(8,128)(2,1)S(1)} %collective-permute-done.refs_0_), channel_id=1, source_target_pairs={{0,192},{64,0},{128,64},{192,128},{1,193},{65,1},{129,65},{193,129... | collective-permute-start | bytes 663560 | tf_op jit(solution)/shard_map/ppermute | solution.py:234
  37.1 1.3 %collective-permute-start.2 = (bf16[144,768]{1,0:T(8,128)(2,1)S(1)}, bf16[144,768]{1,0:T(8,128)(2,1)S(1)}, u32[]{:S(2)}, u32[]{:S(2)}) collective-permute-start(bf16[144,768]{1,0:T(8,128)(2,1)S(1)} %collective-permute-done.refs_0_), channel_id=1, source_target_pairs={{0,128},{64,192},{128,0},{192,64},{1,129},{65,193},{129,1},{193,65... | collective-permute-start | bytes 663560 | tf_op jit(solution)/shard_map/ppermute | solution.py:234
  38.7 8.3 %all-to-all-done.refs_8_.refs_4_ = f32[256,1,128]{2,1,0:T(1,128)S(1)} async-done(((f32[256,1,128]{2,1,0:T(1,128)}), f32[256,1,128]{2,1,0:T(1,128)S(1)}, u32[]{:S(2)}, u32[]{:S(2)}) %all-to-all-start) | async-done | bytes 131104 | tf_op jit(solution)/shard_map/all_to_all | solution.py:274
  47.1 0.9 copy-done
  48.0 0.9 copy-done.1
  48.9 2.6 %near.1 = (bf16[576,384]{1,0:T(8,128)(2,1)S(1)}, bf16[576,384]{1,0:T(8,128)(2,1)S(1)}, bf16[576,384]{1,0:T(8,128)(2,1)S(1)}, bf16[576,384]{1,0:T(8,128)(2,1)S(1)...) custom-call(s32[1]{0:T(128)} %bitcast.zh_ref, bf16[144,768]{1,0:T(8,128)(2,1)S(1)} %copy-done, ...), custom_call_target="tpu_custom_call" | custom-call | flops 509607936 | bytes 4194304 | tf_op jit(solution)/shard_map/near/pallas_call | solution.py:31
  51.6 2.4 %far.1 = (bf16[576,384]{1,0:T(8,128)(2,1)S(1)}, bf16[576,384]{1,0:T(8,128)(2,1)S(1)}, f32[3,576,576]{2,1,0:T(8,128)S(1)}, f32[384,576]{1,0:T(8,128)S(1)}, f32[16,576]{1,0:T(8,128)S(1)}, /*index=5*/f32[8,576]{1,0:T(8,128)S(1)}) custom-call(bf16[144,768]{1,0:T(8,128)(2,1)S(1)} %collective-permute-done.refs_0_, ...), custom_call_target="tpu_custom_call" | custom-call | flops 509607936 | bytes 4194304 | tf_op jit(solution)/shard_map/far/pallas_call | solution.py:31
  54.0 1.6 %collective-permute-start.12 = (f32[8,576]{1,0:T(8,128)S(1)}, f32[8,576]{1,0:T(8,128)S(1)}, u32[]{:S(2)}, u32[]{:S(2)}) collective-permute-start(f32[8,576]{1,0:T(8,128)S(1)} %get-tuple-element.44.refs_0_), channel_id=1, source_target_pairs={{0,16},{16,32},{32,48},{48,0},{1,17},{17,33},{33,49},{49,1},{2,18}... | collective-permute-start | bytes 55304 | tf_op jit(solution)/shard_map/ppermute | solution.py:239
  55.7 4.3 %collective-permute-start.11 = (f32[8,576]{1,0:T(8,128)S(1)}, f32[8,576]{1,0:T(8,128)S(1)}, u32[]{:S(2)}, u32[]{:S(2)}) collective-permute-start(f32[8,576]{1,0:T(8,128)S(1)} %get-tuple-element.44.refs_0_), channel_id=1, source_target_pairs={{0,32},{16,48},{32,0},{48,16},{1,33},{17,49},{33,1},{49,17},{2,34}... | collective-permute-start | bytes 55304 | tf_op jit(solution)/shard_map/ppermute | solution.py:239
  60.0 2.5 %collective-permute-start.10 = (f32[8,576]{1,0:T(8,128)S(1)}, f32[8,576]{1,0:T(8,128)S(1)}, u32[]{:S(2)}, u32[]{:S(2)}) collective-permute-start(f32[8,576]{1,0:T(8,128)S(1)} %get-tuple-element.44.refs_0_), channel_id=1, source_target_pairs={{0,48},{16,0},{32,16},{48,32},{1,49},{17,1},{33,17},{49,33},{2,50}... | collective-permute-start | bytes 55304 | tf_op jit(solution)/shard_map/ppermute | solution.py:239
  62.5 1.3 %middle.1 = (f32[3,576,576]{2,1,0:T(8,128)S(1)}, f32[3,576,576]{2,1,0:T(8,128)S(1)}) custom-call(bf16[576,384]{1,0:T(8,128)(2,1)S(1)} %get-tuple-element.41.refs_6_.gs, bf16[576,384]{1,0:T(8,128)(2,1)S(1)} %get-tuple-element.48.vb1, bf16[576,384]{1,0:T(8,128)(2,1)S(1)} %get-tuple-element.49.vb2), custom_call_target="tpu_custom_call" | custom-call | flops 509607936 | bytes 8388608 | tf_op jit(solution)/shard_map/middle/pallas_call | solution.py:31
  63.9 3.6 %keys.1 = (bf16[3,576,576]{2,1,0:T(8,128)(2,1)S(1)}, bf16[3,576,576]{2,1,0:T(8,128)(2,1)S(1)}, bf16[288,768]{1,0:T(8,128)(2,1)S(1)}, bf16[288,768]{1,0:T(8,128)(...) custom-call(f32[8,576]{1,0:T(8,128)S(1)} %get-tuple-element.44.refs_0_, ...), custom_call_target="tpu_custom_call" | custom-call | flops 1019215872 | bytes 6291456 | tf_op jit(solution)/shard_map/keys/pallas_call | solution.py:31
  67.6 2.4 %collective-permute-start.14 = (bf16[288,768]{1,0:T(8,128)(2,1)S(1)}, bf16[288,768]{1,0:T(8,128)(2,1)S(1)}, u32[]{:S(2)}, u32[]{:S(2)}) collective-permute-start(bf16[288,768]{1,0:T(8,128)(2,1)S(1)} %get-tuple-element.54), channel_id=1, source_target_pairs={{0,128},{64,192},{128,0},{192,64},{1,129},{65,193},{129,1},{193,65... | collective-permute-start | bytes 1327112 | tf_op jit(solution)/shard_map/ppermute | solution.py:239
  70.5 1.4 %queries.1 = (bf16[144,768]{1,0:T(8,128)(2,1)S(1)}, bf16[144,768]{1,0:T(8,128)(2,1)S(1)}, bf16[144,768]{1,0:T(8,128)(2,1)S(1)}, bf16[144,768]{1,0:T(8,128)(2,1)S(1)}) custom-call(s32[1]{0:T(128)} %bitcast.zh_ref, f32[8,576]{1,0:T(8,128)S(1)} %get-tuple-element.44.refs_0_, f32[8,576]{1,0:T(8,128)S(1)} %collective-permute-done.10.refs_1_, ...), custom_call_target="tpu_custom_call" | custom-call | flops 509607936 | bytes 6291456 | tf_op jit(solution)/shard_map/queries/pallas_call | solution.py:31
  72.0 2.8 %collective-permute-start.17 = (bf16[144,768]{1,0:T(8,128)(2,1)S(1)}, bf16[144,768]{1,0:T(8,128)(2,1)S(1)}, u32[]{:S(2)}, u32[]{:S(2)}) collective-permute-start(bf16[144,768]{1,0:T(8,128)(2,1)S(1)} %get-tuple-element.64), channel_id=1, source_target_pairs={{0,48},{16,0},{32,16},{48,32},{1,49},{17,1},{33,17},{49,33},{2,50}... | collective-permute-start | bytes 663560 | tf_op jit(solution)/shard_map/ppermute | solution.py:239
  74.8 1.7 %collective-permute-start.18 = (bf16[144,768]{1,0:T(8,128)(2,1)S(1)}, bf16[144,768]{1,0:T(8,128)(2,1)S(1)}, u32[]{:S(2)}, u32[]{:S(2)}) collective-permute-start(bf16[144,768]{1,0:T(8,128)(2,1)S(1)} %get-tuple-element.65), channel_id=1, source_target_pairs={{0,32},{16,48},{32,0},{48,16},{1,33},{17,49},{33,1},{49,17},{2,34}... | collective-permute-start | bytes 663560 | tf_op jit(solution)/shard_map/ppermute | solution.py:239
  76.5 2.5 %collective-permute-start.19 = (bf16[144,768]{1,0:T(8,128)(2,1)S(1)}, bf16[144,768]{1,0:T(8,128)(2,1)S(1)}, u32[]{:S(2)}, u32[]{:S(2)}) collective-permute-start(bf16[144,768]{1,0:T(8,128)(2,1)S(1)} %get-tuple-element.66), channel_id=1, source_target_pairs={{0,16},{16,32},{32,48},{48,0},{1,17},{17,33},{33,49},{49,1},{2,18}... | collective-permute-start | bytes 663560 | tf_op jit(solution)/shard_map/ppermute | solution.py:239
  79.0 11.6 %collective-permute-done.15.refs_3_ = bf16[288,768]{1,0:T(8,128)(2,1)S(1)} collective-permute-done((bf16[288,768]{1,0:T(8,128)(2,1)S(1)}, bf16[288,768]{1,0:T(8,128)(2,1)S(1)}, u32[]{:S(2)}, u32[]{:S(2)}) %collective-permute-start.15) | collective-permute-done | bytes 442400 | tf_op jit(solution)/shard_map/ppermute | solution.py:239
  90.8 1.2 collective-permute-start.16
  92.0 9.7 %collective-permute-done.16.got_ref = bf16[144,768]{1,0:T(8,128)(2,1)S(1)} collective-permute-done((bf16[144,768]{1,0:T(8,128)(2,1)S(1)}, bf16[144,768]{1,0:T(8,128)(2,1)S(1)}, u32[]{:S(2)}, u32[]{:S(2)}) %collective-permute-start.16) | collective-permute-done | bytes 221216 | tf_op jit(solution)/shard_map/ppermute | solution.py:334
  102.0 23.7 %all_to_all.10.pk_ref = f32[256,1,128]{2,1,0:T(1,128)S(1)} all-to-all(f32[256,1,128]{2,1,0:T(1,128)S(1)} %get-tuple-element.69), channel_id=1, replica_groups=mesh['x'=4,'zh'=4,'zl'=2,'y'=4,'c'=2] {'x','zh','zl','y','c'}, dimensions={0} | all-to-all | bytes 262144 | tf_op jit(solution)/shard_map/all_to_all | solution.py:342
  125.7 0.9 cast.1
  (24 shorter events, 1.5 us)
Async XLA Ops:
  2.6 23.4 %collective-permute-start.6 = (bf16[144,768]{1,0:T(8,128)(2,1)}, bf16[144,768]{1,0:T(8,128)(2,1)S(1)}, u32[]{:S(2)}, u32[]{:S(2)}) collective-permute-start(bf16[144,768]{1,0:T(8,128)(2,1)} %get-tuple-element.39.refs_0_), channel_id=1, source_target_pairs={{0,48},{16,0},{32,16},{48,32},{1,49},{17,1},{33,17},{49,33},{2,50}... | collective-permute-start | bytes 663560 | tf_op jit(solution)/shard_map/ppermute | solution.py:234
  9.5 19.4 %collective-permute-start.5 = (bf16[144,768]{1,0:T(8,128)(2,1)}, bf16[144,768]{1,0:T(8,128)(2,1)S(1)}, u32[]{:S(2)}, u32[]{:S(2)}) collective-permute-start(bf16[144,768]{1,0:T(8,128)(2,1)} %get-tuple-element.39.refs_0_), channel_id=1, source_target_pairs={{0,32},{16,48},{32,0},{48,16},{1,33},{17,49},{33,1},{49,17},{2,34}... | collective-permute-start | bytes 663560 | tf_op jit(solution)/shard_map/ppermute | solution.py:234
  10.5 24.1 %collective-permute-start = (bf16[144,768]{1,0:T(8,128)(2,1)}, bf16[144,768]{1,0:T(8,128)(2,1)S(1)}, u32[]{:S(2)}, u32[]{:S(2)}) collective-permute-start(bf16[144,768]{1,0:T(8,128)(2,1)} %get-tuple-element.37.refs_4_), channel_id=1, source_target_pairs={{0,8},{8,0},{1,9},{9,1},{2,10},{10,2},{3,11},{11,3},{4,12},{12,4},... | collective-permute-start | bytes 663560 | tf_op jit(solution)/shard_map/ppermute | solution.py:270
  11.4 25.7 %collective-permute-start.4 = (bf16[144,768]{1,0:T(8,128)(2,1)}, bf16[144,768]{1,0:T(8,128)(2,1)S(1)}, u32[]{:S(2)}, u32[]{:S(2)}) collective-permute-start(bf16[144,768]{1,0:T(8,128)(2,1)} %get-tuple-element.39.refs_0_), channel_id=1, source_target_pairs={{0,16},{16,32},{32,48},{48,0},{1,17},{17,33},{33,49},{49,1},{2,18}... | collective-permute-start | bytes 663560 | tf_op jit(solution)/shard_map/ppermute | solution.py:234
  13.5 24.9 %collective-permute-start.9 = (bf16[144,768]{1,0:T(8,128)(2,1)}, bf16[144,768]{1,0:T(8,128)(2,1)S(1)}, u32[]{:S(2)}, u32[]{:S(2)}) collective-permute-start(bf16[144,768]{1,0:T(8,128)(2,1)} %get-tuple-element.37.refs_4_), channel_id=1, source_target_pairs={{0,192},{64,0},{128,64},{192,128},{1,193},{65,1},{129,65},{193,129... | collective-permute-start | bytes 663560 | tf_op jit(solution)/shard_map/ppermute | solution.py:234
  16.0 31.0 %all-to-all-start = ((f32[256,1,128]{2,1,0:T(1,128)}), f32[256,1,128]{2,1,0:T(1,128)S(1)}, u32[]{:S(2)}, u32[]{:S(2)}) async-start(f32[256,1,128]{2,1,0:T(1,128)} %get-tuple-element.38), calls=%async_computation | async-start | bytes 262144 | tf_op jit(solution)/shard_map/all_to_all | solution.py:274
  26.0 12.7 %collective-permute-start.8 = (bf16[144,768]{1,0:T(8,128)(2,1)}, bf16[144,768]{1,0:T(8,128)(2,1)S(1)}, u32[]{:S(2)}, u32[]{:S(2)}) collective-permute-start(bf16[144,768]{1,0:T(8,128)(2,1)} %get-tuple-element.37.refs_4_), channel_id=1, source_target_pairs={{0,128},{64,192},{128,0},{192,64},{1,129},{65,193},{129,1},{193,65... | collective-permute-start | bytes 663560 | tf_op jit(solution)/shard_map/ppermute | solution.py:234
  29.0 9.8 %collective-permute-start.7 = (bf16[144,768]{1,0:T(8,128)(2,1)}, bf16[144,768]{1,0:T(8,128)(2,1)S(1)}, u32[]{:S(2)}, u32[]{:S(2)}) collective-permute-start(bf16[144,768]{1,0:T(8,128)(2,1)} %get-tuple-element.37.refs_4_), channel_id=1, source_target_pairs={{0,64},{64,128},{128,192},{192,0},{1,65},{65,129},{129,193},{193,1... | collective-permute-start | bytes 663560 | tf_op jit(solution)/shard_map/ppermute | solution.py:234
  34.6 16.9 %collective-permute-start.3 = (bf16[144,768]{1,0:T(8,128)(2,1)S(1)}, bf16[144,768]{1,0:T(8,128)(2,1)S(1)}, u32[]{:S(2)}, u32[]{:S(2)}) collective-permute-start(bf16[144,768]{1,0:T(8,128)(2,1)S(1)} %collective-permute-done.refs_0_), channel_id=1, source_target_pairs={{0,192},{64,0},{128,64},{192,128},{1,193},{65,1},{129,65},{193,129... | collective-permute-start | bytes 663560 | tf_op jit(solution)/shard_map/ppermute | solution.py:234
  37.1 14.5 %collective-permute-start.2 = (bf16[144,768]{1,0:T(8,128)(2,1)S(1)}, bf16[144,768]{1,0:T(8,128)(2,1)S(1)}, u32[]{:S(2)}, u32[]{:S(2)}) collective-permute-start(bf16[144,768]{1,0:T(8,128)(2,1)S(1)} %collective-permute-done.refs_0_), channel_id=1, source_target_pairs={{0,128},{64,192},{128,0},{192,64},{1,129},{65,193},{129,1},{193,65... | collective-permute-start | bytes 663560 | tf_op jit(solution)/shard_map/ppermute | solution.py:234
  38.4 13.2 %collective-permute-start.1 = (bf16[144,768]{1,0:T(8,128)(2,1)S(1)}, bf16[144,768]{1,0:T(8,128)(2,1)S(1)}, u32[]{:S(2)}, u32[]{:S(2)}) collective-permute-start(bf16[144,768]{1,0:T(8,128)(2,1)S(1)} %collective-permute-done.refs_0_), channel_id=1, source_target_pairs={{0,64},{64,128},{128,192},{192,0},{1,65},{65,129},{129,193},{193,1... | collective-permute-start | bytes 663560 | tf_op jit(solution)/shard_map/ppermute | solution.py:234
  47.1 0.9 copy-start
  48.0 0.9 copy-start.1
  54.0 9.8 %collective-permute-start.12 = (f32[8,576]{1,0:T(8,128)S(1)}, f32[8,576]{1,0:T(8,128)S(1)}, u32[]{:S(2)}, u32[]{:S(2)}) collective-permute-start(f32[8,576]{1,0:T(8,128)S(1)} %get-tuple-element.44.refs_0_), channel_id=1, source_target_pairs={{0,16},{16,32},{32,48},{48,0},{1,17},{17,33},{33,49},{49,1},{2,18}... | collective-permute-start | bytes 55304 | tf_op jit(solution)/shard_map/ppermute | solution.py:239
  55.7 8.2 %collective-permute-start.11 = (f32[8,576]{1,0:T(8,128)S(1)}, f32[8,576]{1,0:T(8,128)S(1)}, u32[]{:S(2)}, u32[]{:S(2)}) collective-permute-start(f32[8,576]{1,0:T(8,128)S(1)} %get-tuple-element.44.refs_0_), channel_id=1, source_target_pairs={{0,32},{16,48},{32,0},{48,16},{1,33},{17,49},{33,1},{49,17},{2,34}... | collective-permute-start | bytes 55304 | tf_op jit(solution)/shard_map/ppermute | solution.py:239
  60.0 3.9 %collective-permute-start.10 = (f32[8,576]{1,0:T(8,128)S(1)}, f32[8,576]{1,0:T(8,128)S(1)}, u32[]{:S(2)}, u32[]{:S(2)}) collective-permute-start(f32[8,576]{1,0:T(8,128)S(1)} %get-tuple-element.44.refs_0_), channel_id=1, source_target_pairs={{0,48},{16,0},{32,16},{48,32},{1,49},{17,1},{33,17},{49,33},{2,50}... | collective-permute-start | bytes 55304 | tf_op jit(solution)/shard_map/ppermute | solution.py:239
  67.5 9.0 %collective-permute-start.13 = (bf16[288,768]{1,0:T(8,128)(2,1)S(1)}, bf16[288,768]{1,0:T(8,128)(2,1)S(1)}, u32[]{:S(2)}, u32[]{:S(2)}) collective-permute-start(bf16[288,768]{1,0:T(8,128)(2,1)S(1)} %get-tuple-element.53), channel_id=1, source_target_pairs={{0,192},{64,0},{128,64},{192,128},{1,193},{65,1},{129,65},{193,129... | collective-permute-start | bytes 1327112 | tf_op jit(solution)/shard_map/ppermute | solution.py:239
  67.6 11.4 %collective-permute-start.14 = (bf16[288,768]{1,0:T(8,128)(2,1)S(1)}, bf16[288,768]{1,0:T(8,128)(2,1)S(1)}, u32[]{:S(2)}, u32[]{:S(2)}) collective-permute-start(bf16[288,768]{1,0:T(8,128)(2,1)S(1)} %get-tuple-element.54), channel_id=1, source_target_pairs={{0,128},{64,192},{128,0},{192,64},{1,129},{65,193},{129,1},{193,65... | collective-permute-start | bytes 1327112 | tf_op jit(solution)/shard_map/ppermute | solution.py:239
  70.0 20.6 %collective-permute-start.15 = (bf16[288,768]{1,0:T(8,128)(2,1)S(1)}, bf16[288,768]{1,0:T(8,128)(2,1)S(1)}, u32[]{:S(2)}, u32[]{:S(2)}) collective-permute-start(bf16[288,768]{1,0:T(8,128)(2,1)S(1)} %get-tuple-element.55), channel_id=1, source_target_pairs={{0,64},{64,128},{128,192},{192,0},{1,65},{65,129},{129,193},{193,1... | collective-permute-start | bytes 1327112 | tf_op jit(solution)/shard_map/ppermute | solution.py:239
  72.0 20.0 %collective-permute-start.17 = (bf16[144,768]{1,0:T(8,128)(2,1)S(1)}, bf16[144,768]{1,0:T(8,128)(2,1)S(1)}, u32[]{:S(2)}, u32[]{:S(2)}) collective-permute-start(bf16[144,768]{1,0:T(8,128)(2,1)S(1)} %get-tuple-element.64), channel_id=1, source_target_pairs={{0,48},{16,0},{32,16},{48,32},{1,49},{17,1},{33,17},{49,33},{2,50}... | collective-permute-start | bytes 663560 | tf_op jit(solution)/shard_map/ppermute | solution.py:239
  74.8 17.2 %collective-permute-start.18 = (bf16[144,768]{1,0:T(8,128)(2,1)S(1)}, bf16[144,768]{1,0:T(8,128)(2,1)S(1)}, u32[]{:S(2)}, u32[]{:S(2)}) collective-permute-start(bf16[144,768]{1,0:T(8,128)(2,1)S(1)} %get-tuple-element.65), channel_id=1, source_target_pairs={{0,32},{16,48},{32,0},{48,16},{1,33},{17,49},{33,1},{49,17},{2,34}... | collective-permute-start | bytes 663560 | tf_op jit(solution)/shard_map/ppermute | solution.py:239
  76.5 15.5 %collective-permute-start.19 = (bf16[144,768]{1,0:T(8,128)(2,1)S(1)}, bf16[144,768]{1,0:T(8,128)(2,1)S(1)}, u32[]{:S(2)}, u32[]{:S(2)}) collective-permute-start(bf16[144,768]{1,0:T(8,128)(2,1)S(1)} %get-tuple-element.66), channel_id=1, source_target_pairs={{0,16},{16,32},{32,48},{48,0},{1,17},{17,33},{33,49},{49,1},{2,18}... | collective-permute-start | bytes 663560 | tf_op jit(solution)/shard_map/ppermute | solution.py:239
  90.8 10.9 %collective-permute-start.16 = (bf16[144,768]{1,0:T(8,128)(2,1)S(1)}, bf16[144,768]{1,0:T(8,128)(2,1)S(1)}, u32[]{:S(2)}, u32[]{:S(2)}) collective-permute-start(bf16[144,768]{1,0:T(8,128)(2,1)S(1)} %get-tuple-element.57), channel_id=1, source_target_pairs={{0,8},{8,0},{1,9},{9,1},{2,10},{10,2},{3,11},{11,3},{4,12},{12,4},... | collective-permute-start | bytes 663560 | tf_op jit(solution)/shard_map/ppermute | solution.py:334

commit v5 on v4

--- a/solution.py
+++ b/solution.py
@@ -19,6 +19,7 @@
 BF16 = jnp.bfloat16
 VMEM_LIMIT = 48 * 1024 * 1024
 WORK_LIMIT = 24 * 1024 * 1024
+PEAK_ROW = 15
 FORWARD_LIMIT = 32 * 1024 * 1024
 PREP_LIMIT = 62 * 1024 * 1024
 
@@ -48,7 +49,11 @@
 
 
 def peak_lanes(ref):
-    return jnp.max(ref[...], axis=0)
+    step = ref.shape[0] // 8
+    parts = [jnp.max(ref[i * step : (i + 1) * step], axis=0) for i in range(8)]
+    while len(parts) > 1:
+        parts = [jnp.maximum(a, b) for a, b in zip(parts[::2], parts[1::2])]
+    return parts[0]
 
 
 def biggest(x):
@@ -89,9 +94,10 @@
         peak = jnp.max(s, axis=0, keepdims=True)
         e = jnp.exp2(s * to_power - peak * to_power)
         m = peak * score_scale
-        e_ref[h] = e
+        weights = e.astype(BF16)
+        e_ref[h] = weights
         total = jnp.sum(e, axis=0, keepdims=True)
-        o = mxu(vb[:, cols], e.astype(BF16), TN) / total
+        o = mxu(vb[:, cols], weights, TN) / total
         d = jnp.sum(o * gs[:, cols].T.astype(F32), axis=0, keepdims=True)
         found.append((m, m + jnp.log(total), d, o))
     return found
@@ -105,7 +111,8 @@
 
 
 def near_kernel(heads, groups, zh_ref, *refs):
-    qgs, near = refs[:groups], refs[groups : 2 * groups]
+    near = (refs[0], refs[5], refs[2], refs[3])
+    qgs = (refs[4], refs[1], refs[7], refs[6])
     pk_ref, qs, gs, kb, vb, e_ref, ot_ref, row_ref = refs[2 * groups :]
     rows, width = qgs[0].shape[0], qs.shape[1]
     pk = peak_lanes(pk_ref)
@@ -115,6 +122,7 @@
         gs[place_of(zh, groups, rows, s), :] = scaled(ref[:, width:], TOP / pk[:, 3:4])
     load_keys(near, pk, kb, vb)
     row_ref[...] = jnp.zeros_like(row_ref)
+    row_ref[PEAK_ROW : PEAK_ROW + 1, :128] = pk
     for h, (m, lse, d, o) in enumerate(half_pass(heads, pk, qs, gs, kb, vb, e_ref)):
         ot_ref[h * HD : (h + 1) * HD, :] = o
         for i, row in enumerate((m, lse, d)):
@@ -123,8 +131,8 @@
 
 def far_kernel(heads, groups, *refs):
     far = refs[:groups]
-    pk_ref, qs, gs, ot1_ref, row1_ref, kb, vb, e_ref, ot_ref, row_ref, st_ref = refs[groups:]
-    pk = peak_lanes(pk_ref)
+    qs, gs, ot1_ref, row1_ref, kb, vb, e_ref, ot_ref, row_ref, st_ref = refs[groups:]
+    pk = row1_ref[PEAK_ROW : PEAK_ROW + 1, :128]
     load_keys(far, pk, kb, vb)
     row_ref[...] = jnp.zeros_like(row_ref)
     stats = []
@@ -159,8 +167,8 @@
 
 def keys_kernel(heads, groups, *refs):
     sts, dkvs = refs[:groups], refs[-groups:]
-    pk_ref, qs, gs, e1, e2, row1_ref, row2_ref, dp1, dp2, ds1, ds2 = refs[groups:-groups]
-    pk = peak_lanes(pk_ref)
+    qs, gs, e1, e2, row1_ref, row2_ref, dp1, dp2, ds1, ds2 = refs[groups:-groups]
+    pk = row1_ref[PEAK_ROW : PEAK_ROW + 1, :128]
     pq, pkk, pv, pg = (pk[:, i : i + 1] for i in range(4))
     grad_scale = pg * pv / (TOP * TOP)
     width = qs.shape[1]
@@ -169,13 +177,13 @@
         left = slice(h * HD, (h + 1) * HD)
         right = slice(width + h * HD, width + (h + 1) * HD)
         log_total, delta = totals(sts, h)
-        delta = delta * grad_scale
-        q, g = qs[:, left], gs[:, left]
+        q, gt = qs[:, left], gs[:, left].astype(F32).T
         halves = ((e1, row1_ref[3 * h : 3 * h + 1, :], dp1, ds1), (e2, row2_ref[h : h + 1, :], dp2, ds2))
         for half, (e, m, dp, ds) in enumerate(halves):
-            p = e[h] * jnp.exp(m - log_total)
-            dv = mxu(p.astype(BF16), g, NN) * (pg / TOP)
-            d = (p * (dp[h] * grad_scale - delta)).astype(BF16)
+            share = jnp.exp(m - log_total)
+            slope = share * grad_scale
+            dv = mxu(e[h], (gt * share).astype(BF16), NT) * (pg / TOP)
+            d = (e[h].astype(F32) * (dp[h] * slope - delta * slope)).astype(BF16)
             ds[h] = d
             dk = mxu(d, q, NN) * (pq / (TOP * ROOT))
             for s, ref in enumerate(dkvs):
@@ -185,10 +193,10 @@
 
 
 def queries_kernel(heads, groups, zh_ref, *refs):
-    sts, (pk_ref, ot_ref, kb1, kb2, ds1, ds2) = refs[:groups], refs[groups : groups + 6]
+    sts, (row1_ref, ot_ref, kb1, kb2, ds1, ds2) = refs[:groups], refs[groups : groups + 6]
     oqs, oqa = refs[groups + 6 : -1], refs[-1]
     rows, width = oqs[0].shape[0], kb1.shape[1]
-    pk = peak_lanes(pk_ref)
+    pk = row1_ref[PEAK_ROW : PEAK_ROW + 1, :128]
     for h in range(heads):
         left = slice(h * HD, (h + 1) * HD)
         right = slice(width + h * HD, width + (h + 1) * HD)
@@ -202,6 +210,10 @@
         ref[...] = oqa[place_of(zh_ref[0], groups, rows, s), :]
 
 
+def relay_kernel(a_ref, b_ref, sum_ref):
+    sum_ref[...] = (a_ref[...].astype(F32) + b_ref[...].astype(F32)).astype(BF16)
+
+
 def fold_kernel(*refs):
     parts, (own_ref, send_ref) = refs[:-2], refs[-2:]
     rows = own_ref.shape[0]
@@ -209,8 +221,8 @@
     send_ref[...] = sum(r[rows:, :].astype(F32) for r in parts).astype(BF16)
 
 
-def sums_kernel(groups, own_ref, got_ref, *refs):
-    oqs, (goq_ref, gkv_ref, pk_ref) = refs[:groups], refs[groups:]
+def sums_kernel(own_ref, got_ref, *refs):
+    *oqs, goq_ref, gkv_ref, pk_ref = refs
     width = own_ref.shape[1] // 2
     goq_ref[...] = sum(r[...].astype(F32) for r in oqs)
     gkv_ref[...] = own_ref[...] + got_ref[...].astype(F32)
@@ -269,18 +281,20 @@
     )
     twin = lax.ppermute(kv, "zl", shift(2, 1))
     near = spread(kv, "x", sizes["x"])
-    qgs = spread(qg, "zh", groups)
+    qgs = [qg, lax.ppermute(qg, "zh", shift(groups, 1)), None, lax.ppermute(qg, "zh", shift(groups, groups - 1))]
+    qgs[2] = lax.ppermute(qgs[1], "zh", shift(groups, 1))
     far = spread(twin, "x", sizes["x"])
     pk = lax.all_to_all(pk, axes, 0, 0, tiled=True)
     half = like(BF16, q_rows, width)
     square = like(F32, heads, q_rows, q_rows)
+    edges = like(BF16, heads, q_rows, q_rows)
     some_rows = like(F32, 16, q_rows)
     outputs = like(F32, width, q_rows)
     qs, gs, kb1, vb1, e1, ot1, row1 = call(
         functools.partial(near_kernel, heads, groups),
         "near",
-        (half,) * 4 + (square, outputs, some_rows),
-        (zh, *qgs, *near, pk),
+        (half,) * 4 + (edges, outputs, some_rows),
+        (zh, near[0], qgs[1], near[2], near[3], qgs[0], near[1], qgs[3], qgs[2], pk),
         flops=2 * pairs * HD,
         nbytes=4 * 2**20,
         exps=pairs // 2,
@@ -290,8 +304,8 @@
     kb2, vb2, e2, ot, row2, stats = call(
         functools.partial(far_kernel, heads, groups),
         "far",
-        (half,) * 2 + (square, outputs, some_rows, like(F32, 8, q_rows)),
-        (*far, pk, qs, gs, ot1, row1),
+        (half,) * 2 + (edges, outputs, some_rows, like(F32, 8, q_rows)),
+        (*far, qs, gs, ot1, row1),
         flops=2 * pairs * HD,
         nbytes=4 * 2**20,
         exps=pairs // 2,
@@ -307,12 +321,11 @@
         nbytes=8 * 2**20,
         limit=WORK_LIMIT,
     )
-    edges = like(BF16, heads, q_rows, q_rows)
     ds1, ds2, *dkvs = call(
         functools.partial(keys_kernel, heads, groups),
         "keys",
         (edges, edges) + (like(BF16, 2 * rows, 2 * width),) * groups,
-        (*sts, pk, qs, gs, e1, e2, row1, row2, dp1, dp2),
+        (*sts, qs, gs, e1, e2, row1, row2, dp1, dp2),
         flops=4 * pairs * HD,
         nbytes=6 * 2**20,
         limit=WORK_LIMIT,
@@ -321,7 +334,7 @@
         functools.partial(queries_kernel, heads, groups),
         "queries",
         (wide,) * groups,
-        (zh, *sts, pk, ot, kb1, kb2, ds1, ds2),
+        (zh, *sts, row1, ot, kb1, kb2, ds1, ds2),
         [pltpu.VMEM((q_rows, 2 * width), BF16)],
         flops=2 * pairs * HD,
         nbytes=6 * 2**20,
@@ -329,11 +342,14 @@
         in_specs=[smem] + [vmem] * (groups + 6),
     )
     dkvs = home(dkvs, "x")
-    oqs = home(oqs, "zh")
+    ahead = lax.ppermute(oqs[2], "zh", shift(groups, groups - 1))
+    back = lax.ppermute(oqs[3], "zh", shift(groups, 1))
+    relay = call(relay_kernel, "relay", wide, (oqs[1], ahead), nbytes=2**20, limit=WORK_LIMIT)
+    oqs = [oqs[0], back, lax.ppermute(relay, "zh", shift(groups, groups - 1))]
     own, send = call(fold_kernel, "fold", (like(F32, rows, 2 * width), wide), dkvs, nbytes=2 * 2**20)
     got = lax.ppermute(send, "zl", shift(2, 1))
     goq, gkv, tops = call(
-        functools.partial(sums_kernel, groups),
+        sums_kernel,
         "sums",
         (like(F32, rows, 2 * width), like(F32, rows, 2 * width), peaks),
         (own, got, *oqs),

time: 127 us -> 119 us (0.937)
  waiting for transfers between devices: 34.3 us -> 28.9 us
  starting transfers between devices: 51.2 us -> 49.2 us
    ppermute x0 -> x6, starting transfers between devices: none -> 16.4 us  [the longest x1 6.93 us: on_device(): lax.ppermute(qg, 'zh', shift(groups, groups - 1))]
    ppermute x9 -> x6, starting transfers between devices: 20.6 us -> 7.75 us  [spread(): return [x] + [lax.ppermute(x, axis, shift(n, s)) for s in range(1, n)]]
    ppermute x0 -> x6, waiting for transfers between devices: none -> 10.8 us  [the longest x1 8.75 us: on_device(): ahead = lax.ppermute(oqs[2], 'zh', shift(groups, groups - 1))]
    ppermute x9 -> x6, waiting for transfers between devices: 11.6 us -> 4.74 us  [home(): lax.ppermute(parts[s], axis, shift(n, n - s))]
    ppermute x9 -> x6, starting transfers between devices: 18.5 us -> 12.6 us  [home(): lax.ppermute(parts[s], axis, shift(n, n - s))]
    ppermute x1, waiting for transfers between devices: 4.65 us -> 0.01 us  [on_device(): twin = lax.ppermute(kv, 'zl', shift(2, 1))]
    all_to_all x1, waiting for transfers between devices: 8.31 us -> 4.18 us  [on_device(): pk = lax.all_to_all(pk, axes, 0, 0, tiled=True)]
    ppermute x1, waiting for transfers between devices: 9.65 us -> 7.48 us  [on_device(): got = lax.ppermute(send, 'zl', shift(2, 1))]
  transfers between devices with their start and end apart: 21 -> 21, of which waited for: 4 -> 7; matrix products, arithmetic and copies ran while one was open for 0% -> 0% of each run, Pallas kernels for 4% -> 5%
where the time goes in v5:
time: 119 us
  starting transfers between devices  49.2 us (41%)
  waiting for transfers between devices  28.9 us (24%)
  blocking collectives  23.7 us (20%)
  Pallas kernels  14.4 us (12%)
  local copies, waits for them, and re-layouts  1.87 us (2%)
    all_to_all x1, blocking collectives, on_device(): tops = lax.all_to_all(tops, axes, 0, 0, tiled=True)  23.7 us
    pallas_call x10, Pallas kernels, call(): pl.pallas_call(body, name=name, out_shape=out_shape, scratch_shapes=list(...  14.4 us
    ppermute x6, starting transfers between devices, home(): lax.ppermute(parts[s], axis, shift(n, n - s))  12.6 us
    all_to_all x1, starting transfers between devices, on_device(): pk = lax.all_to_all(pk, axes, 0, 0, tiled=True)  11.7 us
    ppermute x1, waiting for transfers between devices, on_device(): ahead = lax.ppermute(oqs[2], 'zh', shift(groups, groups - 1))  8.75 us
    ppermute x6, starting transfers between devices, spread(): return [x] + [lax.ppermute(x, axis, shift(n, s)) for s in range(1, n)]  7.75 us
    ppermute x1, waiting for transfers between devices, on_device(): got = lax.ppermute(send, 'zl', shift(2, 1))  7.48 us
    ppermute x1, starting transfers between devices, on_device(): lax.ppermute(qg, 'zh', shift(groups, groups - 1))  6.93 us
  transfers between devices with their start and end apart: 21, of which 7 were waited for; matrix products, arithmetic and copies ran while one was open for 0% of the time, Pallas kernels for 5%

profile of v5, /device:TPU:1, one launch (start us, length us, event | category | flops | bytes accessed | tf_op | source)
XLA Modules:
  0.0 118.7 jit_solution(5291217886672964688)
XLA Ops:
  0.6 2.0 %prep.1 = (bf16[144,768]{1,0:T(8,128)(2,1)}, bf16[144,768]{1,0:T(8,128)(2,1)}, f32[256,1,128]{2,1,0:T(1,128)}) custom-call(bf16[144,384]{1,0:T(8,128)(2,1)} %q_ref.1, bf16[144,384]{1,0:T(8,128)(2,1)} %k_ref.1, bf16[144,384]{1,0:T(8,128)(2,1)} %v_ref.1, bf16[144,384]{1,0:T(8,128)(2,1)} %g_ref.1), custom_call_target="tpu_custom_call" | custom-call | bytes 1048576 | tf_op jit(solution)/shard_map/prep/pallas_call | solution.py:32
  2.6 6.9 %collective-permute-start.8 = (bf16[144,768]{1,0:T(8,128)(2,1)}, bf16[144,768]{1,0:T(8,128)(2,1)S(1)}, u32[]{:S(2)}, u32[]{:S(2)}) collective-permute-start(bf16[144,768]{1,0:T(8,128)(2,1)} %get-tuple-element.38.refs_4_), channel_id=1, source_target_pairs={{0,48},{16,0},{32,16},{48,32},{1,49},{17,1},{33,17},{49,33},{2,50}... | collective-permute-start | bytes 663560 | tf_op jit(solution)/shard_map/ppermute | solution.py:284
  9.5 0.7 collective-permute-start
  10.3 1.2 %collective-permute-start.7 = (bf16[144,768]{1,0:T(8,128)(2,1)}, bf16[144,768]{1,0:T(8,128)(2,1)S(1)}, u32[]{:S(2)}, u32[]{:S(2)}) collective-permute-start(bf16[144,768]{1,0:T(8,128)(2,1)} %get-tuple-element.37.refs_0_), channel_id=1, source_target_pairs={{0,64},{64,128},{128,192},{192,0},{1,65},{65,129},{129,193},{193,1... | collective-permute-start | bytes 663560 | tf_op jit(solution)/shard_map/ppermute | solution.py:246
  11.5 1.5 %collective-permute-start.6 = (bf16[144,768]{1,0:T(8,128)(2,1)}, bf16[144,768]{1,0:T(8,128)(2,1)S(1)}, u32[]{:S(2)}, u32[]{:S(2)}) collective-permute-start(bf16[144,768]{1,0:T(8,128)(2,1)} %get-tuple-element.37.refs_0_), channel_id=1, source_target_pairs={{0,192},{64,0},{128,64},{192,128},{1,193},{65,1},{129,65},{193,129... | collective-permute-start | bytes 663560 | tf_op jit(solution)/shard_map/ppermute | solution.py:246
  13.0 11.7 %all-to-all-start = ((f32[256,1,128]{2,1,0:T(1,128)}), f32[256,1,128]{2,1,0:T(1,128)S(1)}, u32[]{:S(2)}, u32[]{:S(2)}) async-start(f32[256,1,128]{2,1,0:T(1,128)} %get-tuple-element.39), calls=%async_computation | async-start | bytes 262144 | tf_op jit(solution)/shard_map/all_to_all | solution.py:287
  24.7 3.0 %collective-permute-start.5 = (bf16[144,768]{1,0:T(8,128)(2,1)}, bf16[144,768]{1,0:T(8,128)(2,1)S(1)}, u32[]{:S(2)}, u32[]{:S(2)}) collective-permute-start(bf16[144,768]{1,0:T(8,128)(2,1)} %get-tuple-element.37.refs_0_), channel_id=1, source_target_pairs={{0,128},{64,192},{128,0},{192,64},{1,129},{65,193},{129,1},{193,65... | collective-permute-start | bytes 663560 | tf_op jit(solution)/shard_map/ppermute | solution.py:246
  27.6 2.5 %collective-permute-start.9 = (bf16[144,768]{1,0:T(8,128)(2,1)S(1)}, bf16[144,768]{1,0:T(8,128)(2,1)S(1)}, u32[]{:S(2)}, u32[]{:S(2)}) collective-permute-start(bf16[144,768]{1,0:T(8,128)(2,1)S(1)} %collective-permute-done.4.refs_1_), channel_id=1, source_target_pairs={{0,16},{16,32},{32,48},{48,0},{1,17},{17,33},{33,49},{49,1},{2,18}... | collective-permute-start | bytes 663560 | tf_op jit(solution)/shard_map/ppermute | solution.py:285
  30.2 0.9 collective-permute-start.3
  31.0 1.2 %collective-permute-start.2 = (bf16[144,768]{1,0:T(8,128)(2,1)S(1)}, bf16[144,768]{1,0:T(8,128)(2,1)S(1)}, u32[]{:S(2)}, u32[]{:S(2)}) collective-permute-start(bf16[144,768]{1,0:T(8,128)(2,1)S(1)} %collective-permute-done.refs_0_), channel_id=1, source_target_pairs={{0,128},{64,192},{128,0},{192,64},{1,129},{65,193},{129,1},{193,65... | collective-permute-start | bytes 663560 | tf_op jit(solution)/shard_map/ppermute | solution.py:246
  32.3 1.1 collective-permute-done.5.refs_2_
  33.3 4.2 %all-to-all-done.refs_8_ = f32[256,1,128]{2,1,0:T(1,128)S(1)} async-done(((f32[256,1,128]{2,1,0:T(1,128)}), f32[256,1,128]{2,1,0:T(1,128)S(1)}, u32[]{:S(2)}, u32[]{:S(2)}) %all-to-all-start) | async-done | bytes 131104 | tf_op jit(solution)/shard_map/all_to_all | solution.py:287
  37.5 2.1 %collective-permute-done.9.refs_7_ = bf16[144,768]{1,0:T(8,128)(2,1)S(1)} collective-permute-done((bf16[144,768]{1,0:T(8,128)(2,1)S(1)}, bf16[144,768]{1,0:T(8,128)(2,1)S(1)}, u32[]{:S(2)}, u32[]{:S(2)}) %collective-permute-start.9) | collective-permute-done | bytes 221216 | tf_op jit(solution)/shard_map/ppermute | solution.py:285
  39.5 0.9 copy-done
  40.5 0.9 copy-done.1
  41.4 2.7 %near.1 = (bf16[576,384]{1,0:T(8,128)(2,1)S(1)}, bf16[576,384]{1,0:T(8,128)(2,1)S(1)}, bf16[576,384]{1,0:T(8,128)(2,1)S(1)}, bf16[576,384]{1,0:T(8,128)(2,1)S(1)...) custom-call(s32[1]{0:T(128)} %bitcast.zh_ref, bf16[144,768]{1,0:T(8,128)(2,1)S(1)} %copy-done.1, ...), custom_call_target="tpu_custom_call" | custom-call | flops 509607936 | bytes 4194304 | tf_op jit(solution)/shard_map/near/pallas_call | solution.py:32
  44.7 2.4 %far.1 = (bf16[576,384]{1,0:T(8,128)(2,1)S(1)}, bf16[576,384]{1,0:T(8,128)(2,1)S(1)}, bf16[3,576,576]{2,1,0:T(8,128)(2,1)S(1)}, f32[384,576]{1,0:T(8,128)S(1)}, ...) custom-call(bf16[144,768]{1,0:T(8,128)(2,1)S(1)} %collective-permute-done.refs_0_, ...), custom_call_target="tpu_custom_call" | custom-call | flops 509607936 | bytes 4194304 | tf_op jit(solution)/shard_map/far/pallas_call | solution.py:32
  47.1 3.8 %collective-permute-start.12 = (f32[8,576]{1,0:T(8,128)S(1)}, f32[8,576]{1,0:T(8,128)S(1)}, u32[]{:S(2)}, u32[]{:S(2)}) collective-permute-start(f32[8,576]{1,0:T(8,128)S(1)} %get-tuple-element.44.refs_0_), channel_id=1, source_target_pairs={{0,16},{16,32},{32,48},{48,0},{1,17},{17,33},{33,49},{49,1},{2,18}... | collective-permute-start | bytes 55304 | tf_op jit(solution)/shard_map/ppermute | solution.py:251
  50.9 3.4 %collective-permute-start.11 = (f32[8,576]{1,0:T(8,128)S(1)}, f32[8,576]{1,0:T(8,128)S(1)}, u32[]{:S(2)}, u32[]{:S(2)}) collective-permute-start(f32[8,576]{1,0:T(8,128)S(1)} %get-tuple-element.44.refs_0_), channel_id=1, source_target_pairs={{0,32},{16,48},{32,0},{48,16},{1,33},{17,49},{33,1},{49,17},{2,34}... | collective-permute-start | bytes 55304 | tf_op jit(solution)/shard_map/ppermute | solution.py:251
  54.3 3.5 %collective-permute-start.10 = (f32[8,576]{1,0:T(8,128)S(1)}, f32[8,576]{1,0:T(8,128)S(1)}, u32[]{:S(2)}, u32[]{:S(2)}) collective-permute-start(f32[8,576]{1,0:T(8,128)S(1)} %get-tuple-element.44.refs_0_), channel_id=1, source_target_pairs={{0,48},{16,0},{32,16},{48,32},{1,49},{17,1},{33,17},{49,33},{2,50}... | collective-permute-start | bytes 55304 | tf_op jit(solution)/shard_map/ppermute | solution.py:251
  57.8 1.3 %middle.1 = (f32[3,576,576]{2,1,0:T(8,128)S(1)}, f32[3,576,576]{2,1,0:T(8,128)S(1)}) custom-call(bf16[576,384]{1,0:T(8,128)(2,1)S(1)} %get-tuple-element.41.refs_5_.gs, bf16[576,384]{1,0:T(8,128)(2,1)S(1)} %get-tuple-element.48.vb1, bf16[576,384]{1,0:T(8,128)(2,1)S(1)} %get-tuple-element.49.vb2), custom_call_target="tpu_custom_call" | custom-call | flops 509607936 | bytes 8388608 | tf_op jit(solution)/shard_map/middle/pallas_call | solution.py:32
  59.2 3.1 %keys.1 = (bf16[3,576,576]{2,1,0:T(8,128)(2,1)S(1)}, bf16[3,576,576]{2,1,0:T(8,128)(2,1)S(1)}, bf16[288,768]{1,0:T(8,128)(2,1)S(1)}, bf16[288,768]{1,0:T(8,128)(...) custom-call(f32[8,576]{1,0:T(8,128)S(1)} %get-tuple-element.44.refs_0_, ...), custom_call_target="tpu_custom_call" | custom-call | flops 1019215872 | bytes 6291456 | tf_op jit(solution)/shard_map/keys/pallas_call | solution.py:32
  62.3 0.6 collective-permute-start.13
  62.9 1.2 %collective-permute-start.14 = (bf16[288,768]{1,0:T(8,128)(2,1)S(1)}, bf16[288,768]{1,0:T(8,128)(2,1)S(1)}, u32[]{:S(2)}, u32[]{:S(2)}) collective-permute-start(bf16[288,768]{1,0:T(8,128)(2,1)S(1)} %get-tuple-element.54), channel_id=1, source_target_pairs={{0,128},{64,192},{128,0},{192,64},{1,129},{65,193},{129,1},{193,65... | collective-permute-start | bytes 1327112 | tf_op jit(solution)/shard_map/ppermute | solution.py:251
  64.1 1.4 %queries.1 = (bf16[144,768]{1,0:T(8,128)(2,1)S(1)}, bf16[144,768]{1,0:T(8,128)(2,1)S(1)}, bf16[144,768]{1,0:T(8,128)(2,1)S(1)}, bf16[144,768]{1,0:T(8,128)(2,1)S(1)}) custom-call(s32[1]{0:T(128)} %bitcast.zh_ref, f32[8,576]{1,0:T(8,128)S(1)} %get-tuple-element.44.refs_0_, f32[8,576]{1,0:T(8,128)S(1)} %collective-permute-done.10.refs_1_, ...), custom_call_target="tpu_custom_call" | custom-call | flops 509607936 | bytes 6291456 | tf_op jit(solution)/shard_map/queries/pallas_call | solution.py:32
  65.5 3.6 %collective-permute-start.18 = (bf16[144,768]{1,0:T(8,128)(2,1)S(1)}, bf16[144,768]{1,0:T(8,128)(2,1)S(1)}, u32[]{:S(2)}, u32[]{:S(2)}) collective-permute-start(bf16[144,768]{1,0:T(8,128)(2,1)S(1)} %get-tuple-element.66), channel_id=1, source_target_pairs={{0,48},{16,0},{32,16},{48,32},{1,49},{17,1},{33,17},{49,33},{2,50}... | collective-permute-start | bytes 663560 | tf_op jit(solution)/shard_map/ppermute | solution.py:345
  69.1 8.8 %collective-permute-done.18.b_ref = bf16[144,768]{1,0:T(8,128)(2,1)S(1)} collective-permute-done((bf16[144,768]{1,0:T(8,128)(2,1)S(1)}, bf16[144,768]{1,0:T(8,128)(2,1)S(1)}, u32[]{:S(2)}, u32[]{:S(2)}) %collective-permute-start.18) | collective-permute-done | bytes 221216 | tf_op jit(solution)/shard_map/ppermute | solution.py:345
  77.9 3.4 %collective-permute-start.19 = (bf16[144,768]{1,0:T(8,128)(2,1)S(1)}, bf16[144,768]{1,0:T(8,128)(2,1)S(1)}, u32[]{:S(2)}, u32[]{:S(2)}) collective-permute-start(bf16[144,768]{1,0:T(8,128)(2,1)S(1)} %relay.1), channel_id=1, source_target_pairs={{0,48},{16,0},{32,16},{48,32},{1,49},{17,1},{33,17},{49,33},{2,50}... | collective-permute-start | bytes 663560 | tf_op jit(solution)/shard_map/ppermute | solution.py:348
  81.3 4.7 %collective-permute-done.15.refs_3_ = bf16[288,768]{1,0:T(8,128)(2,1)S(1)} collective-permute-done((bf16[288,768]{1,0:T(8,128)(2,1)S(1)}, bf16[288,768]{1,0:T(8,128)(2,1)S(1)}, u32[]{:S(2)}, u32[]{:S(2)}) %collective-permute-start.15) | collective-permute-done | bytes 442400 | tf_op jit(solution)/shard_map/ppermute | solution.py:251
  86.3 7.5 %collective-permute-done.16.got_ref = bf16[144,768]{1,0:T(8,128)(2,1)S(1)} collective-permute-done((bf16[144,768]{1,0:T(8,128)(2,1)S(1)}, bf16[144,768]{1,0:T(8,128)(2,1)S(1)}, u32[]{:S(2)}, u32[]{:S(2)}) %collective-permute-start.16) | collective-permute-done | bytes 221216 | tf_op jit(solution)/shard_map/ppermute | solution.py:350
  94.1 23.7 %all_to_all.10.pk_ref = f32[256,1,128]{2,1,0:T(1,128)S(1)} all-to-all(f32[256,1,128]{2,1,0:T(1,128)S(1)} %get-tuple-element.69), channel_id=1, replica_groups=mesh['x'=4,'zh'=4,'zl'=2,'y'=4,'c'=2] {'x','zh','zl','y','c'}, dimensions={0} | all-to-all | bytes 262144 | tf_op jit(solution)/shard_map/all_to_all | solution.py:358
  117.8 0.9 cast.1
  (25 shorter events, 1.3 us)
Async XLA Ops:
  2.6 22.0 %collective-permute-start.8 = (bf16[144,768]{1,0:T(8,128)(2,1)}, bf16[144,768]{1,0:T(8,128)(2,1)S(1)}, u32[]{:S(2)}, u32[]{:S(2)}) collective-permute-start(bf16[144,768]{1,0:T(8,128)(2,1)} %get-tuple-element.38.refs_4_), channel_id=1, source_target_pairs={{0,48},{16,0},{32,16},{48,32},{1,49},{17,1},{33,17},{49,33},{2,50}... | collective-permute-start | bytes 663560 | tf_op jit(solution)/shard_map/ppermute | solution.py:284
  9.5 18.1 %collective-permute-start.4 = (bf16[144,768]{1,0:T(8,128)(2,1)}, bf16[144,768]{1,0:T(8,128)(2,1)S(1)}, u32[]{:S(2)}, u32[]{:S(2)}) collective-permute-start(bf16[144,768]{1,0:T(8,128)(2,1)} %get-tuple-element.38.refs_4_), channel_id=1, source_target_pairs={{0,16},{16,32},{32,48},{48,0},{1,17},{17,33},{33,49},{49,1},{2,18}... | collective-permute-start | bytes 663560 | tf_op jit(solution)/shard_map/ppermute | solution.py:284
  9.5 20.6 %collective-permute-start = (bf16[144,768]{1,0:T(8,128)(2,1)}, bf16[144,768]{1,0:T(8,128)(2,1)S(1)}, u32[]{:S(2)}, u32[]{:S(2)}) collective-permute-start(bf16[144,768]{1,0:T(8,128)(2,1)} %get-tuple-element.37.refs_0_), channel_id=1, source_target_pairs={{0,8},{8,0},{1,9},{9,1},{2,10},{10,2},{3,11},{11,3},{4,12},{12,4},... | collective-permute-start | bytes 663560 | tf_op jit(solution)/shard_map/ppermute | solution.py:282
  10.3 20.7 %collective-permute-start.7 = (bf16[144,768]{1,0:T(8,128)(2,1)}, bf16[144,768]{1,0:T(8,128)(2,1)S(1)}, u32[]{:S(2)}, u32[]{:S(2)}) collective-permute-start(bf16[144,768]{1,0:T(8,128)(2,1)} %get-tuple-element.37.refs_0_), channel_id=1, source_target_pairs={{0,64},{64,128},{128,192},{192,0},{1,65},{65,129},{129,193},{193,1... | collective-permute-start | bytes 663560 | tf_op jit(solution)/shard_map/ppermute | solution.py:246
  11.5 20.8 %collective-permute-start.6 = (bf16[144,768]{1,0:T(8,128)(2,1)}, bf16[144,768]{1,0:T(8,128)(2,1)S(1)}, u32[]{:S(2)}, u32[]{:S(2)}) collective-permute-start(bf16[144,768]{1,0:T(8,128)(2,1)} %get-tuple-element.37.refs_0_), channel_id=1, source_target_pairs={{0,192},{64,0},{128,64},{192,128},{1,193},{65,1},{129,65},{193,129... | collective-permute-start | bytes 663560 | tf_op jit(solution)/shard_map/ppermute | solution.py:246
  13.0 24.5 %all-to-all-start = ((f32[256,1,128]{2,1,0:T(1,128)}), f32[256,1,128]{2,1,0:T(1,128)S(1)}, u32[]{:S(2)}, u32[]{:S(2)}) async-start(f32[256,1,128]{2,1,0:T(1,128)} %get-tuple-element.39), calls=%async_computation | async-start | bytes 262144 | tf_op jit(solution)/shard_map/all_to_all | solution.py:287
  24.7 8.6 %collective-permute-start.5 = (bf16[144,768]{1,0:T(8,128)(2,1)}, bf16[144,768]{1,0:T(8,128)(2,1)S(1)}, u32[]{:S(2)}, u32[]{:S(2)}) collective-permute-start(bf16[144,768]{1,0:T(8,128)(2,1)} %get-tuple-element.37.refs_0_), channel_id=1, source_target_pairs={{0,128},{64,192},{128,0},{192,64},{1,129},{65,193},{129,1},{193,65... | collective-permute-start | bytes 663560 | tf_op jit(solution)/shard_map/ppermute | solution.py:246
  27.6 11.9 %collective-permute-start.9 = (bf16[144,768]{1,0:T(8,128)(2,1)S(1)}, bf16[144,768]{1,0:T(8,128)(2,1)S(1)}, u32[]{:S(2)}, u32[]{:S(2)}) collective-permute-start(bf16[144,768]{1,0:T(8,128)(2,1)S(1)} %collective-permute-done.4.refs_1_), channel_id=1, source_target_pairs={{0,16},{16,32},{32,48},{48,0},{1,17},{17,33},{33,49},{49,1},{2,18}... | collective-permute-start | bytes 663560 | tf_op jit(solution)/shard_map/ppermute | solution.py:285
  30.2 14.0 %collective-permute-start.3 = (bf16[144,768]{1,0:T(8,128)(2,1)S(1)}, bf16[144,768]{1,0:T(8,128)(2,1)S(1)}, u32[]{:S(2)}, u32[]{:S(2)}) collective-permute-start(bf16[144,768]{1,0:T(8,128)(2,1)S(1)} %collective-permute-done.refs_0_), channel_id=1, source_target_pairs={{0,192},{64,0},{128,64},{192,128},{1,193},{65,1},{129,65},{193,129... | collective-permute-start | bytes 663560 | tf_op jit(solution)/shard_map/ppermute | solution.py:246
  31.0 13.1 %collective-permute-start.2 = (bf16[144,768]{1,0:T(8,128)(2,1)S(1)}, bf16[144,768]{1,0:T(8,128)(2,1)S(1)}, u32[]{:S(2)}, u32[]{:S(2)}) collective-permute-start(bf16[144,768]{1,0:T(8,128)(2,1)S(1)} %collective-permute-done.refs_0_), channel_id=1, source_target_pairs={{0,128},{64,192},{128,0},{192,64},{1,129},{65,193},{129,1},{193,65... | collective-permute-start | bytes 663560 | tf_op jit(solution)/shard_map/ppermute | solution.py:246
  32.2 12.5 %collective-permute-start.1 = (bf16[144,768]{1,0:T(8,128)(2,1)S(1)}, bf16[144,768]{1,0:T(8,128)(2,1)S(1)}, u32[]{:S(2)}, u32[]{:S(2)}) collective-permute-start(bf16[144,768]{1,0:T(8,128)(2,1)S(1)} %collective-permute-done.refs_0_), channel_id=1, source_target_pairs={{0,64},{64,128},{128,192},{192,0},{1,65},{65,129},{129,193},{193,1... | collective-permute-start | bytes 663560 | tf_op jit(solution)/shard_map/ppermute | solution.py:246
  39.5 0.9 copy-start
  40.5 0.9 copy-start.1
  47.1 12.0 %collective-permute-start.12 = (f32[8,576]{1,0:T(8,128)S(1)}, f32[8,576]{1,0:T(8,128)S(1)}, u32[]{:S(2)}, u32[]{:S(2)}) collective-permute-start(f32[8,576]{1,0:T(8,128)S(1)} %get-tuple-element.44.refs_0_), channel_id=1, source_target_pairs={{0,16},{16,32},{32,48},{48,0},{1,17},{17,33},{33,49},{49,1},{2,18}... | collective-permute-start | bytes 55304 | tf_op jit(solution)/shard_map/ppermute | solution.py:251
  50.9 8.2 %collective-permute-start.11 = (f32[8,576]{1,0:T(8,128)S(1)}, f32[8,576]{1,0:T(8,128)S(1)}, u32[]{:S(2)}, u32[]{:S(2)}) collective-permute-start(f32[8,576]{1,0:T(8,128)S(1)} %get-tuple-element.44.refs_0_), channel_id=1, source_target_pairs={{0,32},{16,48},{32,0},{48,16},{1,33},{17,49},{33,1},{49,17},{2,34}... | collective-permute-start | bytes 55304 | tf_op jit(solution)/shard_map/ppermute | solution.py:251
  54.3 4.8 %collective-permute-start.10 = (f32[8,576]{1,0:T(8,128)S(1)}, f32[8,576]{1,0:T(8,128)S(1)}, u32[]{:S(2)}, u32[]{:S(2)}) collective-permute-start(f32[8,576]{1,0:T(8,128)S(1)} %get-tuple-element.44.refs_0_), channel_id=1, source_target_pairs={{0,48},{16,0},{32,16},{48,32},{1,49},{17,1},{33,17},{49,33},{2,50}... | collective-permute-start | bytes 55304 | tf_op jit(solution)/shard_map/ppermute | solution.py:251
  62.3 19.0 %collective-permute-start.13 = (bf16[288,768]{1,0:T(8,128)(2,1)S(1)}, bf16[288,768]{1,0:T(8,128)(2,1)S(1)}, u32[]{:S(2)}, u32[]{:S(2)}) collective-permute-start(bf16[288,768]{1,0:T(8,128)(2,1)S(1)} %get-tuple-element.53), channel_id=1, source_target_pairs={{0,192},{64,0},{128,64},{192,128},{1,193},{65,1},{129,65},{193,129... | collective-permute-start | bytes 1327112 | tf_op jit(solution)/shard_map/ppermute | solution.py:251
  62.9 18.3 %collective-permute-start.14 = (bf16[288,768]{1,0:T(8,128)(2,1)S(1)}, bf16[288,768]{1,0:T(8,128)(2,1)S(1)}, u32[]{:S(2)}, u32[]{:S(2)}) collective-permute-start(bf16[288,768]{1,0:T(8,128)(2,1)S(1)} %get-tuple-element.54), channel_id=1, source_target_pairs={{0,128},{64,192},{128,0},{192,64},{1,129},{65,193},{129,1},{193,65... | collective-permute-start | bytes 1327112 | tf_op jit(solution)/shard_map/ppermute | solution.py:251
  64.1 21.9 %collective-permute-start.15 = (bf16[288,768]{1,0:T(8,128)(2,1)S(1)}, bf16[288,768]{1,0:T(8,128)(2,1)S(1)}, u32[]{:S(2)}, u32[]{:S(2)}) collective-permute-start(bf16[288,768]{1,0:T(8,128)(2,1)S(1)} %get-tuple-element.55), channel_id=1, source_target_pairs={{0,64},{64,128},{128,192},{192,0},{1,65},{65,129},{129,193},{193,1... | collective-permute-start | bytes 1327112 | tf_op jit(solution)/shard_map/ppermute | solution.py:251
  65.5 12.3 %collective-permute-start.18 = (bf16[144,768]{1,0:T(8,128)(2,1)S(1)}, bf16[144,768]{1,0:T(8,128)(2,1)S(1)}, u32[]{:S(2)}, u32[]{:S(2)}) collective-permute-start(bf16[144,768]{1,0:T(8,128)(2,1)S(1)} %get-tuple-element.66), channel_id=1, source_target_pairs={{0,48},{16,0},{32,16},{48,32},{1,49},{17,1},{33,17},{49,33},{2,50}... | collective-permute-start | bytes 663560 | tf_op jit(solution)/shard_map/ppermute | solution.py:345
  69.1 17.2 %collective-permute-start.17 = (bf16[144,768]{1,0:T(8,128)(2,1)S(1)}, bf16[144,768]{1,0:T(8,128)(2,1)S(1)}, u32[]{:S(2)}, u32[]{:S(2)}) collective-permute-start(bf16[144,768]{1,0:T(8,128)(2,1)S(1)} %get-tuple-element.64), channel_id=1, source_target_pairs={{0,16},{16,32},{32,48},{48,0},{1,17},{17,33},{33,49},{49,1},{2,18}... | collective-permute-start | bytes 663560 | tf_op jit(solution)/shard_map/ppermute | solution.py:346
  77.9 8.4 %collective-permute-start.19 = (bf16[144,768]{1,0:T(8,128)(2,1)S(1)}, bf16[144,768]{1,0:T(8,128)(2,1)S(1)}, u32[]{:S(2)}, u32[]{:S(2)}) collective-permute-start(bf16[144,768]{1,0:T(8,128)(2,1)S(1)} %relay.1), channel_id=1, source_target_pairs={{0,48},{16,0},{32,16},{48,32},{1,49},{17,1},{33,17},{49,33},{2,50}... | collective-permute-start | bytes 663560 | tf_op jit(solution)/shard_map/ppermute | solution.py:348
  86.2 7.6 %collective-permute-start.16 = (bf16[144,768]{1,0:T(8,128)(2,1)S(1)}, bf16[144,768]{1,0:T(8,128)(2,1)S(1)}, u32[]{:S(2)}, u32[]{:S(2)}) collective-permute-start(bf16[144,768]{1,0:T(8,128)(2,1)S(1)} %get-tuple-element.57), channel_id=1, source_target_pairs={{0,8},{8,0},{1,9},{9,1},{2,10},{10,2},{3,11},{11,3},{4,12},{12,4},... | collective-permute-start | bytes 663560 | tf_op jit(solution)/shard_map/ppermute | solution.py:350

commit v6 on v5

--- a/solution.py
+++ b/solution.py
@@ -79,8 +79,9 @@
     pk_ref[...] = jnp.broadcast_to(row[None], pk_ref.shape)
 
 
-def place_of(zh, groups, rows, s):
-    return pl.ds(pl.multiple_of(lax.rem(zh + groups - s, groups) * rows, 16), rows)
+def place_of(at_ref, groups, rows, s):
+    where = lax.rem(at_ref[0] + 2 * groups - at_ref[1] * s, groups)
+    return pl.ds(pl.multiple_of(where * rows, 16), rows)
 
 
 def half_pass(heads, pk, qs, gs, kb, vb, e_ref):
@@ -110,16 +111,15 @@
         vb[s * rows : (s + 1) * rows, :] = scaled(ref[:, width:], TOP / pk[:, 2:3])
 
 
-def near_kernel(heads, groups, zh_ref, *refs):
+def near_kernel(heads, groups, at_ref, *refs):
     near = (refs[0], refs[5], refs[2], refs[3])
     qgs = (refs[4], refs[1], refs[7], refs[6])
     pk_ref, qs, gs, kb, vb, e_ref, ot_ref, row_ref = refs[2 * groups :]
     rows, width = qgs[0].shape[0], qs.shape[1]
     pk = peak_lanes(pk_ref)
-    zh = zh_ref[0]
     for s, ref in enumerate(qgs):
-        qs[place_of(zh, groups, rows, s), :] = scaled(ref[:, :width], TOP / pk[:, 0:1])
-        gs[place_of(zh, groups, rows, s), :] = scaled(ref[:, width:], TOP / pk[:, 3:4])
+        qs[place_of(at_ref, groups, rows, s), :] = scaled(ref[:, :width], TOP / pk[:, 0:1])
+        gs[place_of(at_ref, groups, rows, s), :] = scaled(ref[:, width:], TOP / pk[:, 3:4])
     load_keys(near, pk, kb, vb)
     row_ref[...] = jnp.zeros_like(row_ref)
     row_ref[PEAK_ROW : PEAK_ROW + 1, :128] = pk
@@ -192,7 +192,7 @@
                 ref[to, right] = dv[part].astype(BF16)
 
 
-def queries_kernel(heads, groups, zh_ref, *refs):
+def queries_kernel(heads, groups, at_ref, *refs):
     sts, (row1_ref, ot_ref, kb1, kb2, ds1, ds2) = refs[:groups], refs[groups : groups + 6]
     oqs, oqa = refs[groups + 6 : -1], refs[-1]
     rows, width = oqs[0].shape[0], kb1.shape[1]
@@ -207,7 +207,7 @@
         dq = dq * (pk[:, 1:2] / (TOP * ROOT))
         oqa[:, right] = dq.astype(BF16).T
     for s, ref in enumerate(oqs):
-        ref[...] = oqa[place_of(zh_ref[0], groups, rows, s), :]
+        ref[...] = oqa[place_of(at_ref, groups, rows, s), :]
 
 
 def relay_kernel(a_ref, b_ref, sum_ref):
@@ -244,6 +244,11 @@
 
 def spread(x, axis, n):
     return [x] + [lax.ppermute(x, axis, shift(n, s)) for s in range(1, n)]
+
+
+def turn(x, n, s):
+    pairs = [(2 * i + c, 2 * ((i + (s if c == 0 else -s)) % n) + c) for i in range(n) for c in range(2)]
+    return lax.ppermute(x, ("zh", "c"), pairs)
 
 
 def home(parts, axis):
@@ -264,7 +269,8 @@
     pairs = q_rows * k_rows * heads
     peaks = like(F32, everyone, 1, 128)
     wide = like(BF16, rows, 2 * width)
-    zh = lax.axis_index("zh").astype(jnp.int32).reshape(1)
+    step = 1 - 2 * lax.axis_index("c")
+    at = jnp.stack([lax.axis_index("zh"), step]).astype(jnp.int32)
     smem = pl.BlockSpec(memory_space=pltpu.SMEM)
     vmem = pl.BlockSpec(memory_space=pltpu.VMEM)
     hbm = pl.BlockSpec(memory_space=pltpu.HBM)
@@ -281,8 +287,8 @@
     )
     twin = lax.ppermute(kv, "zl", shift(2, 1))
     near = spread(kv, "x", sizes["x"])
-    qgs = [qg, lax.ppermute(qg, "zh", shift(groups, 1)), None, lax.ppermute(qg, "zh", shift(groups, groups - 1))]
-    qgs[2] = lax.ppermute(qgs[1], "zh", shift(groups, 1))
+    qgs = [qg, turn(qg, groups, 1), None, turn(qg, groups, -1)]
+    qgs[2] = turn(qgs[1], groups, 1)
     far = spread(twin, "x", sizes["x"])
     pk = lax.all_to_all(pk, axes, 0, 0, tiled=True)
     half = like(BF16, q_rows, width)
@@ -294,7 +300,7 @@
         functools.partial(near_kernel, heads, groups),
         "near",
         (half,) * 4 + (edges, outputs, some_rows),
-        (zh, near[0], qgs[1], near[2], near[3], qgs[0], near[1], qgs[3], qgs[2], pk),
+        (at, near[0], qgs[1], near[2], near[3], qgs[0], near[1], qgs[3], qgs[2], pk),
         flops=2 * pairs * HD,
         nbytes=4 * 2**20,
         exps=pairs // 2,
@@ -334,7 +340,7 @@
         functools.partial(queries_kernel, heads, groups),
         "queries",
         (wide,) * groups,
-        (zh, *sts, row1, ot, kb1, kb2, ds1, ds2),
+        (at, *sts, row1, ot, kb1, kb2, ds1, ds2),
         [pltpu.VMEM((q_rows, 2 * width), BF16)],
         flops=2 * pairs * HD,
         nbytes=6 * 2**20,
@@ -342,10 +348,10 @@
         in_specs=[smem] + [vmem] * (groups + 6),
     )
     dkvs = home(dkvs, "x")
-    ahead = lax.ppermute(oqs[2], "zh", shift(groups, groups - 1))
-    back = lax.ppermute(oqs[3], "zh", shift(groups, 1))
+    ahead = turn(oqs[2], groups, -1)
+    back = turn(oqs[3], groups, 1)
     relay = call(relay_kernel, "relay", wide, (oqs[1], ahead), nbytes=2**20, limit=WORK_LIMIT)
-    oqs = [oqs[0], back, lax.ppermute(relay, "zh", shift(groups, groups - 1))]
+    oqs = [oqs[0], back, turn(relay, groups, -1)]
     own, send = call(fold_kernel, "fold", (like(F32, rows, 2 * width), wide), dkvs, nbytes=2 * 2**20)
     got = lax.ppermute(send, "zl", shift(2, 1))
     goq, gkv, tops = call(

time: 119 us -> 118 us (level)
  starting transfers between devices: 49.2 us -> 47 us
    ppermute x6, waiting for transfers between devices: 4.74 us -> 9.62 us  [home(): lax.ppermute(parts[s], axis, shift(n, n - s))]
    ppermute x6, waiting for transfers between devices: 10.8 us -> 6.49 us  [turn(): return lax.ppermute(x, ('zh', 'c'), pairs)]
    ppermute x6, starting transfers between devices: 12.6 us -> 10.5 us  [home(): lax.ppermute(parts[s], axis, shift(n, n - s))]
    ppermute x6, waiting for transfers between devices: 1.65 us -> 3.55 us  [spread(): return [x] + [lax.ppermute(x, axis, shift(n, s)) for s in range(1, n)]]
    all_to_all x1, waiting for transfers between devices: 4.18 us -> 2.88 us  [on_device(): pk = lax.all_to_all(pk, axes, 0, 0, tiled=True)]
  transfers between devices with their start and end apart: 21 -> 21, of which waited for: 7 -> 7; matrix products, arithmetic and copies ran while one was open for 0% -> 0% of each run, Pallas kernels for 5% -> 6%
where the time goes in v6:
time: 118 us
  starting transfers between devices  47 us (40%)
  waiting for transfers between devices  29.2 us (25%)
  blocking collectives  23.3 us (20%)
  Pallas kernels  15.5 us (13%)
  local copies, waits for them, and re-layouts  1.87 us (2%)
    all_to_all x1, blocking collectives, on_device(): tops = lax.all_to_all(tops, axes, 0, 0, tiled=True)  23.3 us
    ppermute x6, starting transfers between devices, turn(): return lax.ppermute(x, ('zh', 'c'), pairs)  16.2 us
    pallas_call x10, Pallas kernels, call(): pl.pallas_call(body, name=name, out_shape=out_shape, scratch_shapes=list(...  15.5 us
    all_to_all x1, starting transfers between devices, on_device(): pk = lax.all_to_all(pk, axes, 0, 0, tiled=True)  11.6 us
    ppermute x6, starting transfers between devices, home(): lax.ppermute(parts[s], axis, shift(n, n - s))  10.5 us
    ppermute x6, waiting for transfers between devices, home(): lax.ppermute(parts[s], axis, shift(n, n - s))  9.62 us
    ppermute x6, starting transfers between devices, spread(): return [x] + [lax.ppermute(x, axis, shift(n, s)) for s in range(1, n)]  7.75 us
    ppermute x1, waiting for transfers between devices, on_device(): got = lax.ppermute(send, 'zl', shift(2, 1))  6.69 us
  transfers between devices with their start and end apart: 21, of which 7 were waited for; matrix products, arithmetic and copies ran while one was open for 0% of the time, Pallas kernels for 6%

profile of v6, /device:TPU:1, one launch (start us, length us, event | category | flops | bytes accessed | tf_op | source)
XLA Modules:
  0.0 117.7 jit_solution(14085211246660725374)
XLA Ops:
  0.6 2.0 %prep.1 = (bf16[144,768]{1,0:T(8,128)(2,1)}, bf16[144,768]{1,0:T(8,128)(2,1)}, f32[256,1,128]{2,1,0:T(1,128)}) custom-call(bf16[144,384]{1,0:T(8,128)(2,1)} %q_ref.1, bf16[144,384]{1,0:T(8,128)(2,1)} %k_ref.1, bf16[144,384]{1,0:T(8,128)(2,1)} %v_ref.1, bf16[144,384]{1,0:T(8,128)(2,1)} %g_ref.1), custom_call_target="tpu_custom_call" | custom-call | bytes 1048576 | tf_op jit(solution)/shard_map/prep/pallas_call | solution.py:32
  2.6 3.9 %collective-permute-start.8 = (bf16[144,768]{1,0:T(8,128)(2,1)}, bf16[144,768]{1,0:T(8,128)(2,1)S(1)}, u32[]{:S(2)}, u32[]{:S(2)}) collective-permute-start(bf16[144,768]{1,0:T(8,128)(2,1)} %get-tuple-element.38.refs_4_), channel_id=1, source_target_pairs={{0,48},{1,17},{16,0},{17,33},{32,16},{33,49},{48,32},{49,1},{2,50}... | collective-permute-start | bytes 663560 | tf_op jit(solution)/shard_map/ppermute | solution.py:251
  6.5 3.1 %collective-permute-start.4 = (bf16[144,768]{1,0:T(8,128)(2,1)}, bf16[144,768]{1,0:T(8,128)(2,1)S(1)}, u32[]{:S(2)}, u32[]{:S(2)}) collective-permute-start(bf16[144,768]{1,0:T(8,128)(2,1)} %get-tuple-element.38.refs_4_), channel_id=1, source_target_pairs={{0,16},{1,49},{16,32},{17,1},{32,48},{33,17},{48,0},{49,33},{2,18}... | collective-permute-start | bytes 663560 | tf_op jit(solution)/shard_map/ppermute | solution.py:251
  9.6 0.7 collective-permute-start
  10.4 1.2 %collective-permute-start.7 = (bf16[144,768]{1,0:T(8,128)(2,1)}, bf16[144,768]{1,0:T(8,128)(2,1)S(1)}, u32[]{:S(2)}, u32[]{:S(2)}) collective-permute-start(bf16[144,768]{1,0:T(8,128)(2,1)} %get-tuple-element.37.refs_0_), channel_id=1, source_target_pairs={{0,64},{64,128},{128,192},{192,0},{1,65},{65,129},{129,193},{193,1... | collective-permute-start | bytes 663560 | tf_op jit(solution)/shard_map/ppermute | solution.py:246
  11.6 1.5 %collective-permute-start.6 = (bf16[144,768]{1,0:T(8,128)(2,1)}, bf16[144,768]{1,0:T(8,128)(2,1)S(1)}, u32[]{:S(2)}, u32[]{:S(2)}) collective-permute-start(bf16[144,768]{1,0:T(8,128)(2,1)} %get-tuple-element.37.refs_0_), channel_id=1, source_target_pairs={{0,192},{64,0},{128,64},{192,128},{1,193},{65,1},{129,65},{193,129... | collective-permute-start | bytes 663560 | tf_op jit(solution)/shard_map/ppermute | solution.py:246
  13.0 11.6 %all-to-all-start = ((f32[256,1,128]{2,1,0:T(1,128)}), f32[256,1,128]{2,1,0:T(1,128)S(1)}, u32[]{:S(2)}, u32[]{:S(2)}) async-start(f32[256,1,128]{2,1,0:T(1,128)} %get-tuple-element.39), calls=%async_computation | async-start | bytes 262144 | tf_op jit(solution)/shard_map/all_to_all | solution.py:293
  24.7 3.0 %collective-permute-start.5 = (bf16[144,768]{1,0:T(8,128)(2,1)}, bf16[144,768]{1,0:T(8,128)(2,1)S(1)}, u32[]{:S(2)}, u32[]{:S(2)}) collective-permute-start(bf16[144,768]{1,0:T(8,128)(2,1)} %get-tuple-element.37.refs_0_), channel_id=1, source_target_pairs={{0,128},{64,192},{128,0},{192,64},{1,129},{65,193},{129,1},{193,65... | collective-permute-start | bytes 663560 | tf_op jit(solution)/shard_map/ppermute | solution.py:246
  27.6 4.8 %collective-permute-start.9 = (bf16[144,768]{1,0:T(8,128)(2,1)S(1)}, bf16[144,768]{1,0:T(8,128)(2,1)S(1)}, u32[]{:S(2)}, u32[]{:S(2)}) collective-permute-start(bf16[144,768]{1,0:T(8,128)(2,1)S(1)} %collective-permute-done.4.refs_1_), channel_id=1, source_target_pairs={{0,16},{1,49},{16,32},{17,1},{32,48},{33,17},{48,0},{49,33},{2,18}... | collective-permute-start | bytes 663560 | tf_op jit(solution)/shard_map/ppermute | solution.py:251
  32.4 0.9 collective-permute-start.3
  33.3 1.2 %collective-permute-start.2 = (bf16[144,768]{1,0:T(8,128)(2,1)S(1)}, bf16[144,768]{1,0:T(8,128)(2,1)S(1)}, u32[]{:S(2)}, u32[]{:S(2)}) collective-permute-start(bf16[144,768]{1,0:T(8,128)(2,1)S(1)} %collective-permute-done.refs_0_), channel_id=1, source_target_pairs={{0,128},{64,192},{128,0},{192,64},{1,129},{65,193},{129,1},{193,65... | collective-permute-start | bytes 663560 | tf_op jit(solution)/shard_map/ppermute | solution.py:246
  34.6 2.9 %all-to-all-done.refs_8_ = f32[256,1,128]{2,1,0:T(1,128)S(1)} async-done(((f32[256,1,128]{2,1,0:T(1,128)}), f32[256,1,128]{2,1,0:T(1,128)S(1)}, u32[]{:S(2)}, u32[]{:S(2)}) %all-to-all-start) | async-done | bytes 131104 | tf_op jit(solution)/shard_map/all_to_all | solution.py:293
  37.7 0.9 copy-done
  38.6 0.9 copy-done.1
  39.6 3.2 %near.1 = (bf16[576,384]{1,0:T(8,128)(2,1)S(1)}, bf16[576,384]{1,0:T(8,128)(2,1)S(1)}, bf16[576,384]{1,0:T(8,128)(2,1)S(1)}, bf16[576,384]{1,0:T(8,128)(2,1)S(1)...) custom-call(s32[2]{0:T(128)S(1)} %pad_add_fusion.at_ref, ...), custom_call_target="tpu_custom_call" | custom-call | flops 509607936 | bytes 4194304 | tf_op jit(solution)/shard_map/near/pallas_call | solution.py:32
  42.8 3.5 %collective-permute-done.1.refs_1_ = bf16[144,768]{1,0:T(8,128)(2,1)S(1)} collective-permute-done((bf16[144,768]{1,0:T(8,128)(2,1)S(1)}, bf16[144,768]{1,0:T(8,128)(2,1)S(1)}, u32[]{:S(2)}, u32[]{:S(2)}) %collective-permute-start.1) | collective-permute-done | bytes 221216 | tf_op jit(solution)/shard_map/ppermute | solution.py:246
  46.3 2.4 %far.1 = (bf16[576,384]{1,0:T(8,128)(2,1)S(1)}, bf16[576,384]{1,0:T(8,128)(2,1)S(1)}, bf16[3,576,576]{2,1,0:T(8,128)(2,1)S(1)}, f32[384,576]{1,0:T(8,128)S(1)}, ...) custom-call(bf16[144,768]{1,0:T(8,128)(2,1)S(1)} %collective-permute-done.refs_0_, ...), custom_call_target="tpu_custom_call" | custom-call | flops 509607936 | bytes 4194304 | tf_op jit(solution)/shard_map/far/pallas_call | solution.py:32
  48.9 4.5 %collective-permute-start.11 = (f32[8,576]{1,0:T(8,128)S(1)}, f32[8,576]{1,0:T(8,128)S(1)}, u32[]{:S(2)}, u32[]{:S(2)}) collective-permute-start(f32[8,576]{1,0:T(8,128)S(1)} %get-tuple-element.44.refs_0_), channel_id=1, source_target_pairs={{0,32},{16,48},{32,0},{48,16},{1,33},{17,49},{33,1},{49,17},{2,34}... | collective-permute-start | bytes 55304 | tf_op jit(solution)/shard_map/ppermute | solution.py:256
  53.3 2.5 %collective-permute-start.10 = (f32[8,576]{1,0:T(8,128)S(1)}, f32[8,576]{1,0:T(8,128)S(1)}, u32[]{:S(2)}, u32[]{:S(2)}) collective-permute-start(f32[8,576]{1,0:T(8,128)S(1)} %get-tuple-element.44.refs_0_), channel_id=1, source_target_pairs={{0,48},{16,0},{32,16},{48,32},{1,49},{17,1},{33,17},{49,33},{2,50}... | collective-permute-start | bytes 55304 | tf_op jit(solution)/shard_map/ppermute | solution.py:256
  55.8 1.3 %middle.1 = (f32[3,576,576]{2,1,0:T(8,128)S(1)}, f32[3,576,576]{2,1,0:T(8,128)S(1)}) custom-call(bf16[576,384]{1,0:T(8,128)(2,1)S(1)} %get-tuple-element.41.refs_5_.gs, bf16[576,384]{1,0:T(8,128)(2,1)S(1)} %get-tuple-element.48.vb1, bf16[576,384]{1,0:T(8,128)(2,1)S(1)} %get-tuple-element.49.vb2), custom_call_target="tpu_custom_call" | custom-call | flops 509607936 | bytes 8388608 | tf_op jit(solution)/shard_map/middle/pallas_call | solution.py:32
  57.2 3.1 %keys.1 = (bf16[3,576,576]{2,1,0:T(8,128)(2,1)S(1)}, bf16[3,576,576]{2,1,0:T(8,128)(2,1)S(1)}, bf16[288,768]{1,0:T(8,128)(2,1)S(1)}, bf16[288,768]{1,0:T(8,128)(...) custom-call(f32[8,576]{1,0:T(8,128)S(1)} %get-tuple-element.44.refs_0_, ...), custom_call_target="tpu_custom_call" | custom-call | flops 1019215872 | bytes 6291456 | tf_op jit(solution)/shard_map/keys/pallas_call | solution.py:32
  60.3 2.0 %collective-permute-start.13 = (bf16[288,768]{1,0:T(8,128)(2,1)S(1)}, bf16[288,768]{1,0:T(8,128)(2,1)S(1)}, u32[]{:S(2)}, u32[]{:S(2)}) collective-permute-start(bf16[288,768]{1,0:T(8,128)(2,1)S(1)} %get-tuple-element.53), channel_id=1, source_target_pairs={{0,192},{64,0},{128,64},{192,128},{1,193},{65,1},{129,65},{193,129... | collective-permute-start | bytes 1327112 | tf_op jit(solution)/shard_map/ppermute | solution.py:256
  62.3 0.9 collective-permute-start.14
  63.8 1.9 %queries.1 = (bf16[144,768]{1,0:T(8,128)(2,1)S(1)}, bf16[144,768]{1,0:T(8,128)(2,1)S(1)}, bf16[144,768]{1,0:T(8,128)(2,1)S(1)}, bf16[144,768]{1,0:T(8,128)(2,1)S(1)}) custom-call(s32[2]{0:T(128)S(1)} %pad_add_fusion.at_ref, f32[8,576]{1,0:T(8,128)S(1)} %get-tuple-element.44.refs_0_, f32[8,576]{1,0:T(8,128)S(1)} %collective-permute-done.10.refs_1_, ...), custom_call_target="tpu_custom_call" | custom-call | flops 509607936 | bytes 6291456 | tf_op jit(solution)/shard_map/queries/pallas_call | solution.py:32
  65.7 2.1 %collective-permute-start.18 = (bf16[144,768]{1,0:T(8,128)(2,1)S(1)}, bf16[144,768]{1,0:T(8,128)(2,1)S(1)}, u32[]{:S(2)}, u32[]{:S(2)}) collective-permute-start(bf16[144,768]{1,0:T(8,128)(2,1)S(1)} %get-tuple-element.66), channel_id=1, source_target_pairs={{0,48},{1,17},{16,0},{17,33},{32,16},{33,49},{48,32},{49,1},{2,50}... | collective-permute-start | bytes 663560 | tf_op jit(solution)/shard_map/ppermute | solution.py:251
  67.8 1.6 %collective-permute-start.17 = (bf16[144,768]{1,0:T(8,128)(2,1)S(1)}, bf16[144,768]{1,0:T(8,128)(2,1)S(1)}, u32[]{:S(2)}, u32[]{:S(2)}) collective-permute-start(bf16[144,768]{1,0:T(8,128)(2,1)S(1)} %get-tuple-element.64), channel_id=1, source_target_pairs={{0,16},{1,49},{16,32},{17,1},{32,48},{33,17},{48,0},{49,33},{2,18}... | collective-permute-start | bytes 663560 | tf_op jit(solution)/shard_map/ppermute | solution.py:251
  69.4 5.6 %collective-permute-done.18.b_ref = bf16[144,768]{1,0:T(8,128)(2,1)S(1)} collective-permute-done((bf16[144,768]{1,0:T(8,128)(2,1)S(1)}, bf16[144,768]{1,0:T(8,128)(2,1)S(1)}, u32[]{:S(2)}, u32[]{:S(2)}) %collective-permute-start.18) | collective-permute-done | bytes 221216 | tf_op jit(solution)/shard_map/ppermute | solution.py:251
  75.0 0.7 collective-permute-start.19
  75.8 9.6 %collective-permute-done.15.refs_3_ = bf16[288,768]{1,0:T(8,128)(2,1)S(1)} collective-permute-done((bf16[288,768]{1,0:T(8,128)(2,1)S(1)}, bf16[288,768]{1,0:T(8,128)(2,1)S(1)}, u32[]{:S(2)}, u32[]{:S(2)}) %collective-permute-start.15) | collective-permute-done | bytes 442400 | tf_op jit(solution)/shard_map/ppermute | solution.py:256
  86.5 6.7 %collective-permute-done.16.got_ref = bf16[144,768]{1,0:T(8,128)(2,1)S(1)} collective-permute-done((bf16[144,768]{1,0:T(8,128)(2,1)S(1)}, bf16[144,768]{1,0:T(8,128)(2,1)S(1)}, u32[]{:S(2)}, u32[]{:S(2)}) %collective-permute-start.16) | collective-permute-done | bytes 221216 | tf_op jit(solution)/shard_map/ppermute | solution.py:356
  93.5 23.3 %all_to_all.10.pk_ref = f32[256,1,128]{2,1,0:T(1,128)S(1)} all-to-all(f32[256,1,128]{2,1,0:T(1,128)S(1)} %get-tuple-element.69), channel_id=1, replica_groups=mesh['x'=4,'zh'=4,'zl'=2,'y'=4,'c'=2] {'x','zh','zl','y','c'}, dimensions={0} | all-to-all | bytes 262144 | tf_op jit(solution)/shard_map/all_to_all | solution.py:364
  116.8 0.9 cast.1
  (26 shorter events, 2.4 us)
Async XLA Ops:
  2.6 22.0 %collective-permute-start.8 = (bf16[144,768]{1,0:T(8,128)(2,1)}, bf16[144,768]{1,0:T(8,128)(2,1)S(1)}, u32[]{:S(2)}, u32[]{:S(2)}) collective-permute-start(bf16[144,768]{1,0:T(8,128)(2,1)} %get-tuple-element.38.refs_4_), channel_id=1, source_target_pairs={{0,48},{1,17},{16,0},{17,33},{32,16},{33,49},{48,32},{49,1},{2,50}... | collective-permute-start | bytes 663560 | tf_op jit(solution)/shard_map/ppermute | solution.py:251
  6.5 21.1 %collective-permute-start.4 = (bf16[144,768]{1,0:T(8,128)(2,1)}, bf16[144,768]{1,0:T(8,128)(2,1)S(1)}, u32[]{:S(2)}, u32[]{:S(2)}) collective-permute-start(bf16[144,768]{1,0:T(8,128)(2,1)} %get-tuple-element.38.refs_4_), channel_id=1, source_target_pairs={{0,16},{1,49},{16,32},{17,1},{32,48},{33,17},{48,0},{49,33},{2,18}... | collective-permute-start | bytes 663560 | tf_op jit(solution)/shard_map/ppermute | solution.py:251
  9.6 22.8 %collective-permute-start = (bf16[144,768]{1,0:T(8,128)(2,1)}, bf16[144,768]{1,0:T(8,128)(2,1)S(1)}, u32[]{:S(2)}, u32[]{:S(2)}) collective-permute-start(bf16[144,768]{1,0:T(8,128)(2,1)} %get-tuple-element.37.refs_0_), channel_id=1, source_target_pairs={{0,8},{8,0},{1,9},{9,1},{2,10},{10,2},{3,11},{11,3},{4,12},{12,4},... | collective-permute-start | bytes 663560 | tf_op jit(solution)/shard_map/ppermute | solution.py:288
  10.4 22.9 %collective-permute-start.7 = (bf16[144,768]{1,0:T(8,128)(2,1)}, bf16[144,768]{1,0:T(8,128)(2,1)S(1)}, u32[]{:S(2)}, u32[]{:S(2)}) collective-permute-start(bf16[144,768]{1,0:T(8,128)(2,1)} %get-tuple-element.37.refs_0_), channel_id=1, source_target_pairs={{0,64},{64,128},{128,192},{192,0},{1,65},{65,129},{129,193},{193,1... | collective-permute-start | bytes 663560 | tf_op jit(solution)/shard_map/ppermute | solution.py:246
  11.6 23.0 %collective-permute-start.6 = (bf16[144,768]{1,0:T(8,128)(2,1)}, bf16[144,768]{1,0:T(8,128)(2,1)S(1)}, u32[]{:S(2)}, u32[]{:S(2)}) collective-permute-start(bf16[144,768]{1,0:T(8,128)(2,1)} %get-tuple-element.37.refs_0_), channel_id=1, source_target_pairs={{0,192},{64,0},{128,64},{192,128},{1,193},{65,1},{129,65},{193,129... | collective-permute-start | bytes 663560 | tf_op jit(solution)/shard_map/ppermute | solution.py:246
  13.0 24.5 %all-to-all-start = ((f32[256,1,128]{2,1,0:T(1,128)}), f32[256,1,128]{2,1,0:T(1,128)S(1)}, u32[]{:S(2)}, u32[]{:S(2)}) async-start(f32[256,1,128]{2,1,0:T(1,128)} %get-tuple-element.39), calls=%async_computation | async-start | bytes 262144 | tf_op jit(solution)/shard_map/all_to_all | solution.py:293
  24.7 10.0 %collective-permute-start.5 = (bf16[144,768]{1,0:T(8,128)(2,1)}, bf16[144,768]{1,0:T(8,128)(2,1)S(1)}, u32[]{:S(2)}, u32[]{:S(2)}) collective-permute-start(bf16[144,768]{1,0:T(8,128)(2,1)} %get-tuple-element.37.refs_0_), channel_id=1, source_target_pairs={{0,128},{64,192},{128,0},{192,64},{1,129},{65,193},{129,1},{193,65... | collective-permute-start | bytes 663560 | tf_op jit(solution)/shard_map/ppermute | solution.py:246
  27.6 10.0 %collective-permute-start.9 = (bf16[144,768]{1,0:T(8,128)(2,1)S(1)}, bf16[144,768]{1,0:T(8,128)(2,1)S(1)}, u32[]{:S(2)}, u32[]{:S(2)}) collective-permute-start(bf16[144,768]{1,0:T(8,128)(2,1)S(1)} %collective-permute-done.4.refs_1_), channel_id=1, source_target_pairs={{0,16},{1,49},{16,32},{17,1},{32,48},{33,17},{48,0},{49,33},{2,18}... | collective-permute-start | bytes 663560 | tf_op jit(solution)/shard_map/ppermute | solution.py:251
  32.4 10.3 %collective-permute-start.3 = (bf16[144,768]{1,0:T(8,128)(2,1)S(1)}, bf16[144,768]{1,0:T(8,128)(2,1)S(1)}, u32[]{:S(2)}, u32[]{:S(2)}) collective-permute-start(bf16[144,768]{1,0:T(8,128)(2,1)S(1)} %collective-permute-done.refs_0_), channel_id=1, source_target_pairs={{0,192},{64,0},{128,64},{192,128},{1,193},{65,1},{129,65},{193,129... | collective-permute-start | bytes 663560 | tf_op jit(solution)/shard_map/ppermute | solution.py:246
  33.3 9.5 %collective-permute-start.2 = (bf16[144,768]{1,0:T(8,128)(2,1)S(1)}, bf16[144,768]{1,0:T(8,128)(2,1)S(1)}, u32[]{:S(2)}, u32[]{:S(2)}) collective-permute-start(bf16[144,768]{1,0:T(8,128)(2,1)S(1)} %collective-permute-done.refs_0_), channel_id=1, source_target_pairs={{0,128},{64,192},{128,0},{192,64},{1,129},{65,193},{129,1},{193,65... | collective-permute-start | bytes 663560 | tf_op jit(solution)/shard_map/ppermute | solution.py:246
  34.5 11.8 %collective-permute-start.1 = (bf16[144,768]{1,0:T(8,128)(2,1)S(1)}, bf16[144,768]{1,0:T(8,128)(2,1)S(1)}, u32[]{:S(2)}, u32[]{:S(2)}) collective-permute-start(bf16[144,768]{1,0:T(8,128)(2,1)S(1)} %collective-permute-done.refs_0_), channel_id=1, source_target_pairs={{0,64},{64,128},{128,192},{192,0},{1,65},{65,129},{129,193},{193,1... | collective-permute-start | bytes 663560 | tf_op jit(solution)/shard_map/ppermute | solution.py:246
  37.7 0.9 copy-start
  38.6 0.9 copy-start.1
  48.8 8.4 %collective-permute-start.12 = (f32[8,576]{1,0:T(8,128)S(1)}, f32[8,576]{1,0:T(8,128)S(1)}, u32[]{:S(2)}, u32[]{:S(2)}) collective-permute-start(f32[8,576]{1,0:T(8,128)S(1)} %get-tuple-element.44.refs_0_), channel_id=1, source_target_pairs={{0,16},{16,32},{32,48},{48,0},{1,17},{17,33},{33,49},{49,1},{2,18}... | collective-permute-start | bytes 55304 | tf_op jit(solution)/shard_map/ppermute | solution.py:256
  48.9 8.3 %collective-permute-start.11 = (f32[8,576]{1,0:T(8,128)S(1)}, f32[8,576]{1,0:T(8,128)S(1)}, u32[]{:S(2)}, u32[]{:S(2)}) collective-permute-start(f32[8,576]{1,0:T(8,128)S(1)} %get-tuple-element.44.refs_0_), channel_id=1, source_target_pairs={{0,32},{16,48},{32,0},{48,16},{1,33},{17,49},{33,1},{49,17},{2,34}... | collective-permute-start | bytes 55304 | tf_op jit(solution)/shard_map/ppermute | solution.py:256
  53.3 3.9 %collective-permute-start.10 = (f32[8,576]{1,0:T(8,128)S(1)}, f32[8,576]{1,0:T(8,128)S(1)}, u32[]{:S(2)}, u32[]{:S(2)}) collective-permute-start(f32[8,576]{1,0:T(8,128)S(1)} %get-tuple-element.44.refs_0_), channel_id=1, source_target_pairs={{0,48},{16,0},{32,16},{48,32},{1,49},{17,1},{33,17},{49,33},{2,50}... | collective-permute-start | bytes 55304 | tf_op jit(solution)/shard_map/ppermute | solution.py:256
  60.3 15.5 %collective-permute-start.13 = (bf16[288,768]{1,0:T(8,128)(2,1)S(1)}, bf16[288,768]{1,0:T(8,128)(2,1)S(1)}, u32[]{:S(2)}, u32[]{:S(2)}) collective-permute-start(bf16[288,768]{1,0:T(8,128)(2,1)S(1)} %get-tuple-element.53), channel_id=1, source_target_pairs={{0,192},{64,0},{128,64},{192,128},{1,193},{65,1},{129,65},{193,129... | collective-permute-start | bytes 1327112 | tf_op jit(solution)/shard_map/ppermute | solution.py:256
  62.3 13.5 %collective-permute-start.14 = (bf16[288,768]{1,0:T(8,128)(2,1)S(1)}, bf16[288,768]{1,0:T(8,128)(2,1)S(1)}, u32[]{:S(2)}, u32[]{:S(2)}) collective-permute-start(bf16[288,768]{1,0:T(8,128)(2,1)S(1)} %get-tuple-element.54), channel_id=1, source_target_pairs={{0,128},{64,192},{128,0},{192,64},{1,129},{65,193},{129,1},{193,65... | collective-permute-start | bytes 1327112 | tf_op jit(solution)/shard_map/ppermute | solution.py:256
  63.2 22.2 %collective-permute-start.15 = (bf16[288,768]{1,0:T(8,128)(2,1)S(1)}, bf16[288,768]{1,0:T(8,128)(2,1)S(1)}, u32[]{:S(2)}, u32[]{:S(2)}) collective-permute-start(bf16[288,768]{1,0:T(8,128)(2,1)S(1)} %get-tuple-element.55), channel_id=1, source_target_pairs={{0,64},{64,128},{128,192},{192,0},{1,65},{65,129},{129,193},{193,1... | collective-permute-start | bytes 1327112 | tf_op jit(solution)/shard_map/ppermute | solution.py:256
  65.7 9.3 %collective-permute-start.18 = (bf16[144,768]{1,0:T(8,128)(2,1)S(1)}, bf16[144,768]{1,0:T(8,128)(2,1)S(1)}, u32[]{:S(2)}, u32[]{:S(2)}) collective-permute-start(bf16[144,768]{1,0:T(8,128)(2,1)S(1)} %get-tuple-element.66), channel_id=1, source_target_pairs={{0,48},{1,17},{16,0},{17,33},{32,16},{33,49},{48,32},{49,1},{2,50}... | collective-permute-start | bytes 663560 | tf_op jit(solution)/shard_map/ppermute | solution.py:251
  67.8 18.0 %collective-permute-start.17 = (bf16[144,768]{1,0:T(8,128)(2,1)S(1)}, bf16[144,768]{1,0:T(8,128)(2,1)S(1)}, u32[]{:S(2)}, u32[]{:S(2)}) collective-permute-start(bf16[144,768]{1,0:T(8,128)(2,1)S(1)} %get-tuple-element.64), channel_id=1, source_target_pairs={{0,16},{1,49},{16,32},{17,1},{32,48},{33,17},{48,0},{49,33},{2,18}... | collective-permute-start | bytes 663560 | tf_op jit(solution)/shard_map/ppermute | solution.py:251
  75.0 11.5 %collective-permute-start.19 = (bf16[144,768]{1,0:T(8,128)(2,1)S(1)}, bf16[144,768]{1,0:T(8,128)(2,1)S(1)}, u32[]{:S(2)}, u32[]{:S(2)}) collective-permute-start(bf16[144,768]{1,0:T(8,128)(2,1)S(1)} %relay.1), channel_id=1, source_target_pairs={{0,48},{1,17},{16,0},{17,33},{32,16},{33,49},{48,32},{49,1},{2,50}... | collective-permute-start | bytes 663560 | tf_op jit(solution)/shard_map/ppermute | solution.py:251
  85.6 7.6 %collective-permute-start.16 = (bf16[144,768]{1,0:T(8,128)(2,1)S(1)}, bf16[144,768]{1,0:T(8,128)(2,1)S(1)}, u32[]{:S(2)}, u32[]{:S(2)}) collective-permute-start(bf16[144,768]{1,0:T(8,128)(2,1)S(1)} %get-tuple-element.57), channel_id=1, source_target_pairs={{0,8},{8,0},{1,9},{9,1},{2,10},{10,2},{3,11},{11,3},{4,12},{12,4},... | collective-permute-start | bytes 663560 | tf_op jit(solution)/shard_map/ppermute | solution.py:356

commit v7 on v6

--- a/solution.py
+++ b/solution.py
@@ -246,9 +246,9 @@
     return [x] + [lax.ppermute(x, axis, shift(n, s)) for s in range(1, n)]
 
 
-def turn(x, n, s):
+def turn(x, n, s, axis="zh"):
     pairs = [(2 * i + c, 2 * ((i + (s if c == 0 else -s)) % n) + c) for i in range(n) for c in range(2)]
-    return lax.ppermute(x, ("zh", "c"), pairs)
+    return lax.ppermute(x, (axis, "c"), pairs)
 
 
 def home(parts, axis):
@@ -286,10 +286,12 @@
         in_specs=[hbm] * 4,
     )
     twin = lax.ppermute(kv, "zl", shift(2, 1))
-    near = spread(kv, "x", sizes["x"])
+    nx = sizes["x"]
+    near = [kv, turn(kv, nx, 1, "x"), None, turn(kv, nx, -1, "x")]
+    near[2] = turn(kv, nx, 2, "x")
     qgs = [qg, turn(qg, groups, 1), None, turn(qg, groups, -1)]
     qgs[2] = turn(qgs[1], groups, 1)
-    far = spread(twin, "x", sizes["x"])
+    far = [twin] + [turn(twin, nx, s, "x") for s in range(1, nx)]
     pk = lax.all_to_all(pk, axes, 0, 0, tiled=True)
     half = like(BF16, q_rows, width)
     square = like(F32, heads, q_rows, q_rows)
@@ -347,7 +349,7 @@
         limit=WORK_LIMIT,
         in_specs=[smem] + [vmem] * (groups + 6),
     )
-    dkvs = home(dkvs, "x")
+    dkvs = [dkvs[0]] + [turn(dkvs[s], nx, -s, "x") for s in range(1, nx)]
     ahead = turn(oqs[2], groups, -1)
     back = turn(oqs[3], groups, 1)
     relay = call(relay_kernel, "relay", wide, (oqs[1], ahead), nbytes=2**20, limit=WORK_LIMIT)

time: 118 us -> 117 us (level)
  waiting for transfers between devices: 29.2 us -> 27 us
  starting transfers between devices: 47 us -> 49 us
    ppermute x6 -> x3, waiting for transfers between devices: 9.62 us -> 0.79 us  [home(): lax.ppermute(parts[s], axis, shift(n, n - s))]
    ppermute x12 -> x15, waiting for transfers between devices: 10 us -> 17.7 us  [turn(): return lax.ppermute(x, (axis, 'c'), pairs)]
    ppermute x12 -> x15, starting transfers between devices: 23.9 us -> 28.4 us  [turn(): return lax.ppermute(x, (axis, 'c'), pairs)]
    ppermute x6 -> x3, starting transfers between devices: 10.5 us -> 7.94 us  [home(): lax.ppermute(parts[s], axis, shift(n, n - s))]
  transfers between devices with their start and end apart: 21 -> 21, of which waited for: 7 -> 9; matrix products, arithmetic and copies ran while one was open for 0% -> 0% of each run, Pallas kernels for 6% -> 6%
where the time goes in v7:
time: 117 us
  starting transfers between devices  49 us (42%)
  waiting for transfers between devices  27 us (23%)
  blocking collectives  22.9 us (20%)
  Pallas kernels  15.5 us (13%)
  local copies, waits for them, and re-layouts  1.87 us (2%)
    ppermute x15, starting transfers between devices, turn(): return lax.ppermute(x, (axis, 'c'), pairs)  28.4 us
    all_to_all x1, blocking collectives, on_device(): tops = lax.all_to_all(tops, axes, 0, 0, tiled=True)  22.9 us
    ppermute x15, waiting for transfers between devices, turn(): return lax.ppermute(x, (axis, 'c'), pairs)  17.7 us
    pallas_call x10, Pallas kernels, call(): pl.pallas_call(body, name=name, out_shape=out_shape, scratch_shapes=list(...  15.5 us
    all_to_all x1, starting transfers between devices, on_device(): pk = lax.all_to_all(pk, axes, 0, 0, tiled=True)  11.8 us
    ppermute x3, starting transfers between devices, home(): lax.ppermute(parts[s], axis, shift(n, n - s))  7.94 us
    ppermute x1, waiting for transfers between devices, on_device(): got = lax.ppermute(send, 'zl', shift(2, 1))  6.47 us
  transfers between devices with their start and end apart: 21, of which 9 were waited for; matrix products, arithmetic and copies ran while one was open for 0% of the time, Pallas kernels for 6%

profile of v7, /device:TPU:1, one launch (start us, length us, event | category | flops | bytes accessed | tf_op | source)
XLA Modules:
  0.0 117.0 jit_solution(7231710124784625333)
XLA Ops:
  0.6 2.0 %prep.1 = (bf16[144,768]{1,0:T(8,128)(2,1)}, bf16[144,768]{1,0:T(8,128)(2,1)}, f32[256,1,128]{2,1,0:T(1,128)}) custom-call(bf16[144,384]{1,0:T(8,128)(2,1)} %q_ref.1, bf16[144,384]{1,0:T(8,128)(2,1)} %k_ref.1, bf16[144,384]{1,0:T(8,128)(2,1)} %v_ref.1, bf16[144,384]{1,0:T(8,128)(2,1)} %g_ref.1), custom_call_target="tpu_custom_call" | custom-call | bytes 1048576 | tf_op jit(solution)/shard_map/prep/pallas_call | solution.py:32
  2.6 3.9 %collective-permute-start.8 = (bf16[144,768]{1,0:T(8,128)(2,1)}, bf16[144,768]{1,0:T(8,128)(2,1)S(1)}, u32[]{:S(2)}, u32[]{:S(2)}) collective-permute-start(bf16[144,768]{1,0:T(8,128)(2,1)} %get-tuple-element.38.refs_4_), channel_id=1, source_target_pairs={{0,48},{1,17},{16,0},{17,33},{32,16},{33,49},{48,32},{49,1},{2,50}... | collective-permute-start | bytes 663560 | tf_op jit(solution)/shard_map/ppermute | solution.py:251
  6.5 3.1 %collective-permute-start.4 = (bf16[144,768]{1,0:T(8,128)(2,1)}, bf16[144,768]{1,0:T(8,128)(2,1)S(1)}, u32[]{:S(2)}, u32[]{:S(2)}) collective-permute-start(bf16[144,768]{1,0:T(8,128)(2,1)} %get-tuple-element.38.refs_4_), channel_id=1, source_target_pairs={{0,16},{1,49},{16,32},{17,1},{32,48},{33,17},{48,0},{49,33},{2,18}... | collective-permute-start | bytes 663560 | tf_op jit(solution)/shard_map/ppermute | solution.py:251
  10.4 2.5 %collective-permute-start.7 = (bf16[144,768]{1,0:T(8,128)(2,1)}, bf16[144,768]{1,0:T(8,128)(2,1)S(1)}, u32[]{:S(2)}, u32[]{:S(2)}) collective-permute-start(bf16[144,768]{1,0:T(8,128)(2,1)} %get-tuple-element.37.refs_0_), channel_id=1, source_target_pairs={{0,64},{1,193},{64,128},{65,1},{128,192},{129,65},{192,0},{193,129... | collective-permute-start | bytes 663560 | tf_op jit(solution)/shard_map/ppermute | solution.py:251
  12.9 11.8 %all-to-all-start = ((f32[256,1,128]{2,1,0:T(1,128)}), f32[256,1,128]{2,1,0:T(1,128)S(1)}, u32[]{:S(2)}, u32[]{:S(2)}) async-start(f32[256,1,128]{2,1,0:T(1,128)} %get-tuple-element.39), calls=%async_computation | async-start | bytes 262144 | tf_op jit(solution)/shard_map/all_to_all | solution.py:295
  24.7 3.0 %collective-permute-start.5 = (bf16[144,768]{1,0:T(8,128)(2,1)}, bf16[144,768]{1,0:T(8,128)(2,1)S(1)}, u32[]{:S(2)}, u32[]{:S(2)}) collective-permute-start(bf16[144,768]{1,0:T(8,128)(2,1)} %get-tuple-element.37.refs_0_), channel_id=1, source_target_pairs={{0,128},{1,129},{64,192},{65,193},{128,0},{129,1},{192,64},{193,65... | collective-permute-start | bytes 663560 | tf_op jit(solution)/shard_map/ppermute | solution.py:251
  27.6 4.8 %collective-permute-start.9 = (bf16[144,768]{1,0:T(8,128)(2,1)S(1)}, bf16[144,768]{1,0:T(8,128)(2,1)S(1)}, u32[]{:S(2)}, u32[]{:S(2)}) collective-permute-start(bf16[144,768]{1,0:T(8,128)(2,1)S(1)} %collective-permute-done.4.refs_1_), channel_id=1, source_target_pairs={{0,16},{1,49},{16,32},{17,1},{32,48},{33,17},{48,0},{49,33},{2,18}... | collective-permute-start | bytes 663560 | tf_op jit(solution)/shard_map/ppermute | solution.py:251
  32.7 1.8 %collective-permute-start.2 = (bf16[144,768]{1,0:T(8,128)(2,1)S(1)}, bf16[144,768]{1,0:T(8,128)(2,1)S(1)}, u32[]{:S(2)}, u32[]{:S(2)}) collective-permute-start(bf16[144,768]{1,0:T(8,128)(2,1)S(1)} %collective-permute-done.refs_0_), channel_id=1, source_target_pairs={{0,128},{1,129},{64,192},{65,193},{128,0},{129,1},{192,64},{193,65... | collective-permute-start | bytes 663560 | tf_op jit(solution)/shard_map/ppermute | solution.py:251
  34.5 0.9 collective-permute-start.1
  35.5 2.0 %all-to-all-done.refs_8_ = f32[256,1,128]{2,1,0:T(1,128)S(1)} async-done(((f32[256,1,128]{2,1,0:T(1,128)}), f32[256,1,128]{2,1,0:T(1,128)S(1)}, u32[]{:S(2)}, u32[]{:S(2)}) %all-to-all-start) | async-done | bytes 131104 | tf_op jit(solution)/shard_map/all_to_all | solution.py:295
  37.7 0.9 copy-done
  38.6 0.9 copy-done.1
  39.6 3.2 %near.1 = (bf16[576,384]{1,0:T(8,128)(2,1)S(1)}, bf16[576,384]{1,0:T(8,128)(2,1)S(1)}, bf16[576,384]{1,0:T(8,128)(2,1)S(1)}, bf16[576,384]{1,0:T(8,128)(2,1)S(1)...) custom-call(s32[2]{0:T(128)S(1)} %pad_add_fusion.at_ref, ...), custom_call_target="tpu_custom_call" | custom-call | flops 509607936 | bytes 4194304 | tf_op jit(solution)/shard_map/near/pallas_call | solution.py:32
  42.8 1.8 %collective-permute-done.3.refs_3_ = bf16[144,768]{1,0:T(8,128)(2,1)S(1)} collective-permute-done((bf16[144,768]{1,0:T(8,128)(2,1)S(1)}, bf16[144,768]{1,0:T(8,128)(2,1)S(1)}, u32[]{:S(2)}, u32[]{:S(2)}) %collective-permute-start.3) | collective-permute-done | bytes 221216 | tf_op jit(solution)/shard_map/ppermute | solution.py:251
  44.6 2.4 %far.1 = (bf16[576,384]{1,0:T(8,128)(2,1)S(1)}, bf16[576,384]{1,0:T(8,128)(2,1)S(1)}, bf16[3,576,576]{2,1,0:T(8,128)(2,1)S(1)}, f32[384,576]{1,0:T(8,128)S(1)}, ...) custom-call(bf16[144,768]{1,0:T(8,128)(2,1)S(1)} %collective-permute-done.refs_0_, ...), custom_call_target="tpu_custom_call" | custom-call | flops 509607936 | bytes 4194304 | tf_op jit(solution)/shard_map/far/pallas_call | solution.py:32
  47.0 1.4 %collective-permute-start.12 = (f32[8,576]{1,0:T(8,128)S(1)}, f32[8,576]{1,0:T(8,128)S(1)}, u32[]{:S(2)}, u32[]{:S(2)}) collective-permute-start(f32[8,576]{1,0:T(8,128)S(1)} %get-tuple-element.44.refs_0_), channel_id=1, source_target_pairs={{0,16},{16,32},{32,48},{48,0},{1,17},{17,33},{33,49},{49,1},{2,18}... | collective-permute-start | bytes 55304 | tf_op jit(solution)/shard_map/ppermute | solution.py:256
  48.5 4.1 %collective-permute-start.11 = (f32[8,576]{1,0:T(8,128)S(1)}, f32[8,576]{1,0:T(8,128)S(1)}, u32[]{:S(2)}, u32[]{:S(2)}) collective-permute-start(f32[8,576]{1,0:T(8,128)S(1)} %get-tuple-element.44.refs_0_), channel_id=1, source_target_pairs={{0,32},{16,48},{32,0},{48,16},{1,33},{17,49},{33,1},{49,17},{2,34}... | collective-permute-start | bytes 55304 | tf_op jit(solution)/shard_map/ppermute | solution.py:256
  52.6 2.4 %collective-permute-start.10 = (f32[8,576]{1,0:T(8,128)S(1)}, f32[8,576]{1,0:T(8,128)S(1)}, u32[]{:S(2)}, u32[]{:S(2)}) collective-permute-start(f32[8,576]{1,0:T(8,128)S(1)} %get-tuple-element.44.refs_0_), channel_id=1, source_target_pairs={{0,48},{16,0},{32,16},{48,32},{1,49},{17,1},{33,17},{49,33},{2,50}... | collective-permute-start | bytes 55304 | tf_op jit(solution)/shard_map/ppermute | solution.py:256
  55.0 1.3 %middle.1 = (f32[3,576,576]{2,1,0:T(8,128)S(1)}, f32[3,576,576]{2,1,0:T(8,128)S(1)}) custom-call(bf16[576,384]{1,0:T(8,128)(2,1)S(1)} %get-tuple-element.41.refs_5_.gs, bf16[576,384]{1,0:T(8,128)(2,1)S(1)} %get-tuple-element.48.vb1, bf16[576,384]{1,0:T(8,128)(2,1)S(1)} %get-tuple-element.49.vb2), custom_call_target="tpu_custom_call" | custom-call | flops 509607936 | bytes 8388608 | tf_op jit(solution)/shard_map/middle/pallas_call | solution.py:32
  57.1 3.1 %keys.1 = (bf16[3,576,576]{2,1,0:T(8,128)(2,1)S(1)}, bf16[3,576,576]{2,1,0:T(8,128)(2,1)S(1)}, bf16[288,768]{1,0:T(8,128)(2,1)S(1)}, bf16[288,768]{1,0:T(8,128)(...) custom-call(f32[8,576]{1,0:T(8,128)S(1)} %get-tuple-element.44.refs_0_, ...), custom_call_target="tpu_custom_call" | custom-call | flops 1019215872 | bytes 6291456 | tf_op jit(solution)/shard_map/keys/pallas_call | solution.py:32
  61.1 2.5 %collective-permute-start.14 = (bf16[288,768]{1,0:T(8,128)(2,1)S(1)}, bf16[288,768]{1,0:T(8,128)(2,1)S(1)}, u32[]{:S(2)}, u32[]{:S(2)}) collective-permute-start(bf16[288,768]{1,0:T(8,128)(2,1)S(1)} %get-tuple-element.54), channel_id=1, source_target_pairs={{0,128},{1,129},{64,192},{65,193},{128,0},{129,1},{192,64},{193,65... | collective-permute-start | bytes 1327112 | tf_op jit(solution)/shard_map/ppermute | solution.py:251
  63.6 1.1 collective-permute-start.15
  64.7 1.9 %queries.1 = (bf16[144,768]{1,0:T(8,128)(2,1)S(1)}, bf16[144,768]{1,0:T(8,128)(2,1)S(1)}, bf16[144,768]{1,0:T(8,128)(2,1)S(1)}, bf16[144,768]{1,0:T(8,128)(2,1)S(1)}) custom-call(s32[2]{0:T(128)S(1)} %pad_add_fusion.at_ref, f32[8,576]{1,0:T(8,128)S(1)} %get-tuple-element.44.refs_0_, f32[8,576]{1,0:T(8,128)S(1)} %collective-permute-done.10.refs_1_, ...), custom_call_target="tpu_custom_call" | custom-call | flops 509607936 | bytes 6291456 | tf_op jit(solution)/shard_map/queries/pallas_call | solution.py:32
  66.6 1.3 %collective-permute-start.18 = (bf16[144,768]{1,0:T(8,128)(2,1)S(1)}, bf16[144,768]{1,0:T(8,128)(2,1)S(1)}, u32[]{:S(2)}, u32[]{:S(2)}) collective-permute-start(bf16[144,768]{1,0:T(8,128)(2,1)S(1)} %get-tuple-element.66), channel_id=1, source_target_pairs={{0,48},{1,17},{16,0},{17,33},{32,16},{33,49},{48,32},{49,1},{2,50}... | collective-permute-start | bytes 663560 | tf_op jit(solution)/shard_map/ppermute | solution.py:251
  67.9 2.3 %collective-permute-start.17 = (bf16[144,768]{1,0:T(8,128)(2,1)S(1)}, bf16[144,768]{1,0:T(8,128)(2,1)S(1)}, u32[]{:S(2)}, u32[]{:S(2)}) collective-permute-start(bf16[144,768]{1,0:T(8,128)(2,1)S(1)} %get-tuple-element.64), channel_id=1, source_target_pairs={{0,16},{1,49},{16,32},{17,1},{32,48},{33,17},{48,0},{49,33},{2,18}... | collective-permute-start | bytes 663560 | tf_op jit(solution)/shard_map/ppermute | solution.py:251
  70.2 5.2 %collective-permute-done.18.b_ref = bf16[144,768]{1,0:T(8,128)(2,1)S(1)} collective-permute-done((bf16[144,768]{1,0:T(8,128)(2,1)S(1)}, bf16[144,768]{1,0:T(8,128)(2,1)S(1)}, u32[]{:S(2)}, u32[]{:S(2)}) %collective-permute-start.18) | collective-permute-done | bytes 221216 | tf_op jit(solution)/shard_map/ppermute | solution.py:251
  75.6 3.7 %collective-permute-done.14.refs_2_ = bf16[288,768]{1,0:T(8,128)(2,1)S(1)} collective-permute-done((bf16[288,768]{1,0:T(8,128)(2,1)S(1)}, bf16[288,768]{1,0:T(8,128)(2,1)S(1)}, u32[]{:S(2)}, u32[]{:S(2)}) %collective-permute-start.14) | collective-permute-done | bytes 442400 | tf_op jit(solution)/shard_map/ppermute | solution.py:251
  79.3 3.8 %collective-permute-done.15.refs_3_ = bf16[288,768]{1,0:T(8,128)(2,1)S(1)} collective-permute-done((bf16[288,768]{1,0:T(8,128)(2,1)S(1)}, bf16[288,768]{1,0:T(8,128)(2,1)S(1)}, u32[]{:S(2)}, u32[]{:S(2)}) %collective-permute-start.15) | collective-permute-done | bytes 442400 | tf_op jit(solution)/shard_map/ppermute | solution.py:251
  83.5 2.9 %collective-permute-done.19.refs_2_ = bf16[144,768]{1,0:T(8,128)(2,1)S(1)} collective-permute-done((bf16[144,768]{1,0:T(8,128)(2,1)S(1)}, bf16[144,768]{1,0:T(8,128)(2,1)S(1)}, u32[]{:S(2)}, u32[]{:S(2)}) %collective-permute-start.19) | collective-permute-done | bytes 221216 | tf_op jit(solution)/shard_map/ppermute | solution.py:251
  86.4 6.5 %collective-permute-done.16.got_ref = bf16[144,768]{1,0:T(8,128)(2,1)S(1)} collective-permute-done((bf16[144,768]{1,0:T(8,128)(2,1)S(1)}, bf16[144,768]{1,0:T(8,128)(2,1)S(1)}, u32[]{:S(2)}, u32[]{:S(2)}) %collective-permute-start.16) | collective-permute-done | bytes 221216 | tf_op jit(solution)/shard_map/ppermute | solution.py:358
  93.2 22.9 %all_to_all.10.pk_ref = f32[256,1,128]{2,1,0:T(1,128)S(1)} all-to-all(f32[256,1,128]{2,1,0:T(1,128)S(1)} %get-tuple-element.69), channel_id=1, replica_groups=mesh['x'=4,'zh'=4,'zl'=2,'y'=4,'c'=2] {'x','zh','zl','y','c'}, dimensions={0} | all-to-all | bytes 262144 | tf_op jit(solution)/shard_map/all_to_all | solution.py:366
  116.0 0.9 cast.1
  (26 shorter events, 3.8 us)
Async XLA Ops:
  2.6 22.0 %collective-permute-start.8 = (bf16[144,768]{1,0:T(8,128)(2,1)}, bf16[144,768]{1,0:T(8,128)(2,1)S(1)}, u32[]{:S(2)}, u32[]{:S(2)}) collective-permute-start(bf16[144,768]{1,0:T(8,128)(2,1)} %get-tuple-element.38.refs_4_), channel_id=1, source_target_pairs={{0,48},{1,17},{16,0},{17,33},{32,16},{33,49},{48,32},{49,1},{2,50}... | collective-permute-start | bytes 663560 | tf_op jit(solution)/shard_map/ppermute | solution.py:251
  6.5 21.1 %collective-permute-start.4 = (bf16[144,768]{1,0:T(8,128)(2,1)}, bf16[144,768]{1,0:T(8,128)(2,1)S(1)}, u32[]{:S(2)}, u32[]{:S(2)}) collective-permute-start(bf16[144,768]{1,0:T(8,128)(2,1)} %get-tuple-element.38.refs_4_), channel_id=1, source_target_pairs={{0,16},{1,49},{16,32},{17,1},{32,48},{33,17},{48,0},{49,33},{2,18}... | collective-permute-start | bytes 663560 | tf_op jit(solution)/shard_map/ppermute | solution.py:251
  9.6 22.8 %collective-permute-start = (bf16[144,768]{1,0:T(8,128)(2,1)}, bf16[144,768]{1,0:T(8,128)(2,1)S(1)}, u32[]{:S(2)}, u32[]{:S(2)}) collective-permute-start(bf16[144,768]{1,0:T(8,128)(2,1)} %get-tuple-element.37.refs_0_), channel_id=1, source_target_pairs={{0,8},{8,0},{1,9},{9,1},{2,10},{10,2},{3,11},{11,3},{4,12},{12,4},... | collective-permute-start | bytes 663560 | tf_op jit(solution)/shard_map/ppermute | solution.py:288
  10.4 22.4 %collective-permute-start.7 = (bf16[144,768]{1,0:T(8,128)(2,1)}, bf16[144,768]{1,0:T(8,128)(2,1)S(1)}, u32[]{:S(2)}, u32[]{:S(2)}) collective-permute-start(bf16[144,768]{1,0:T(8,128)(2,1)} %get-tuple-element.37.refs_0_), channel_id=1, source_target_pairs={{0,64},{1,193},{64,128},{65,1},{128,192},{129,65},{192,0},{193,129... | collective-permute-start | bytes 663560 | tf_op jit(solution)/shard_map/ppermute | solution.py:251
  12.8 21.7 %collective-permute-start.6 = (bf16[144,768]{1,0:T(8,128)(2,1)}, bf16[144,768]{1,0:T(8,128)(2,1)S(1)}, u32[]{:S(2)}, u32[]{:S(2)}) collective-permute-start(bf16[144,768]{1,0:T(8,128)(2,1)} %get-tuple-element.37.refs_0_), channel_id=1, source_target_pairs={{0,192},{1,65},{64,0},{65,129},{128,64},{129,193},{192,128},{193,1... | collective-permute-start | bytes 663560 | tf_op jit(solution)/shard_map/ppermute | solution.py:251
  12.9 24.6 %all-to-all-start = ((f32[256,1,128]{2,1,0:T(1,128)}), f32[256,1,128]{2,1,0:T(1,128)S(1)}, u32[]{:S(2)}, u32[]{:S(2)}) async-start(f32[256,1,128]{2,1,0:T(1,128)} %get-tuple-element.39), calls=%async_computation | async-start | bytes 262144 | tf_op jit(solution)/shard_map/all_to_all | solution.py:295
  24.7 10.8 %collective-permute-start.5 = (bf16[144,768]{1,0:T(8,128)(2,1)}, bf16[144,768]{1,0:T(8,128)(2,1)S(1)}, u32[]{:S(2)}, u32[]{:S(2)}) collective-permute-start(bf16[144,768]{1,0:T(8,128)(2,1)} %get-tuple-element.37.refs_0_), channel_id=1, source_target_pairs={{0,128},{1,129},{64,192},{65,193},{128,0},{129,1},{192,64},{193,65... | collective-permute-start | bytes 663560 | tf_op jit(solution)/shard_map/ppermute | solution.py:251
  27.6 10.0 %collective-permute-start.9 = (bf16[144,768]{1,0:T(8,128)(2,1)S(1)}, bf16[144,768]{1,0:T(8,128)(2,1)S(1)}, u32[]{:S(2)}, u32[]{:S(2)}) collective-permute-start(bf16[144,768]{1,0:T(8,128)(2,1)S(1)} %collective-permute-done.4.refs_1_), channel_id=1, source_target_pairs={{0,16},{1,49},{16,32},{17,1},{32,48},{33,17},{48,0},{49,33},{2,18}... | collective-permute-start | bytes 663560 | tf_op jit(solution)/shard_map/ppermute | solution.py:251
  32.4 12.2 %collective-permute-start.3 = (bf16[144,768]{1,0:T(8,128)(2,1)S(1)}, bf16[144,768]{1,0:T(8,128)(2,1)S(1)}, u32[]{:S(2)}, u32[]{:S(2)}) collective-permute-start(bf16[144,768]{1,0:T(8,128)(2,1)S(1)} %collective-permute-done.refs_0_), channel_id=1, source_target_pairs={{0,192},{1,65},{64,0},{65,129},{128,64},{129,193},{192,128},{193,1... | collective-permute-start | bytes 663560 | tf_op jit(solution)/shard_map/ppermute | solution.py:251
  32.7 11.9 %collective-permute-start.2 = (bf16[144,768]{1,0:T(8,128)(2,1)S(1)}, bf16[144,768]{1,0:T(8,128)(2,1)S(1)}, u32[]{:S(2)}, u32[]{:S(2)}) collective-permute-start(bf16[144,768]{1,0:T(8,128)(2,1)S(1)} %collective-permute-done.refs_0_), channel_id=1, source_target_pairs={{0,128},{1,129},{64,192},{65,193},{128,0},{129,1},{192,64},{193,65... | collective-permute-start | bytes 663560 | tf_op jit(solution)/shard_map/ppermute | solution.py:251
  34.5 10.1 %collective-permute-start.1 = (bf16[144,768]{1,0:T(8,128)(2,1)S(1)}, bf16[144,768]{1,0:T(8,128)(2,1)S(1)}, u32[]{:S(2)}, u32[]{:S(2)}) collective-permute-start(bf16[144,768]{1,0:T(8,128)(2,1)S(1)} %collective-permute-done.refs_0_), channel_id=1, source_target_pairs={{0,64},{1,193},{64,128},{65,1},{128,192},{129,65},{192,0},{193,129... | collective-permute-start | bytes 663560 | tf_op jit(solution)/shard_map/ppermute | solution.py:251
  37.7 0.9 copy-start
  38.6 0.9 copy-start.1
  47.0 9.3 %collective-permute-start.12 = (f32[8,576]{1,0:T(8,128)S(1)}, f32[8,576]{1,0:T(8,128)S(1)}, u32[]{:S(2)}, u32[]{:S(2)}) collective-permute-start(f32[8,576]{1,0:T(8,128)S(1)} %get-tuple-element.44.refs_0_), channel_id=1, source_target_pairs={{0,16},{16,32},{32,48},{48,0},{1,17},{17,33},{33,49},{49,1},{2,18}... | collective-permute-start | bytes 55304 | tf_op jit(solution)/shard_map/ppermute | solution.py:256
  48.5 7.8 %collective-permute-start.11 = (f32[8,576]{1,0:T(8,128)S(1)}, f32[8,576]{1,0:T(8,128)S(1)}, u32[]{:S(2)}, u32[]{:S(2)}) collective-permute-start(f32[8,576]{1,0:T(8,128)S(1)} %get-tuple-element.44.refs_0_), channel_id=1, source_target_pairs={{0,32},{16,48},{32,0},{48,16},{1,33},{17,49},{33,1},{49,17},{2,34}... | collective-permute-start | bytes 55304 | tf_op jit(solution)/shard_map/ppermute | solution.py:256
  52.6 4.5 %collective-permute-start.10 = (f32[8,576]{1,0:T(8,128)S(1)}, f32[8,576]{1,0:T(8,128)S(1)}, u32[]{:S(2)}, u32[]{:S(2)}) collective-permute-start(f32[8,576]{1,0:T(8,128)S(1)} %get-tuple-element.44.refs_0_), channel_id=1, source_target_pairs={{0,48},{16,0},{32,16},{48,32},{1,49},{17,1},{33,17},{49,33},{2,50}... | collective-permute-start | bytes 55304 | tf_op jit(solution)/shard_map/ppermute | solution.py:256
  60.2 15.4 %collective-permute-start.13 = (bf16[288,768]{1,0:T(8,128)(2,1)S(1)}, bf16[288,768]{1,0:T(8,128)(2,1)S(1)}, u32[]{:S(2)}, u32[]{:S(2)}) collective-permute-start(bf16[288,768]{1,0:T(8,128)(2,1)S(1)} %get-tuple-element.53), channel_id=1, source_target_pairs={{0,192},{1,65},{64,0},{65,129},{128,64},{129,193},{192,128},{193,1... | collective-permute-start | bytes 1327112 | tf_op jit(solution)/shard_map/ppermute | solution.py:251
  61.1 18.3 %collective-permute-start.14 = (bf16[288,768]{1,0:T(8,128)(2,1)S(1)}, bf16[288,768]{1,0:T(8,128)(2,1)S(1)}, u32[]{:S(2)}, u32[]{:S(2)}) collective-permute-start(bf16[288,768]{1,0:T(8,128)(2,1)S(1)} %get-tuple-element.54), channel_id=1, source_target_pairs={{0,128},{1,129},{64,192},{65,193},{128,0},{129,1},{192,64},{193,65... | collective-permute-start | bytes 1327112 | tf_op jit(solution)/shard_map/ppermute | solution.py:251
  63.6 19.6 %collective-permute-start.15 = (bf16[288,768]{1,0:T(8,128)(2,1)S(1)}, bf16[288,768]{1,0:T(8,128)(2,1)S(1)}, u32[]{:S(2)}, u32[]{:S(2)}) collective-permute-start(bf16[288,768]{1,0:T(8,128)(2,1)S(1)} %get-tuple-element.55), channel_id=1, source_target_pairs={{0,64},{1,193},{64,128},{65,1},{128,192},{129,65},{192,0},{193,129... | collective-permute-start | bytes 1327112 | tf_op jit(solution)/shard_map/ppermute | solution.py:251
  66.6 8.9 %collective-permute-start.18 = (bf16[144,768]{1,0:T(8,128)(2,1)S(1)}, bf16[144,768]{1,0:T(8,128)(2,1)S(1)}, u32[]{:S(2)}, u32[]{:S(2)}) collective-permute-start(bf16[144,768]{1,0:T(8,128)(2,1)S(1)} %get-tuple-element.66), channel_id=1, source_target_pairs={{0,48},{1,17},{16,0},{17,33},{32,16},{33,49},{48,32},{49,1},{2,50}... | collective-permute-start | bytes 663560 | tf_op jit(solution)/shard_map/ppermute | solution.py:251
  67.9 15.6 %collective-permute-start.17 = (bf16[144,768]{1,0:T(8,128)(2,1)S(1)}, bf16[144,768]{1,0:T(8,128)(2,1)S(1)}, u32[]{:S(2)}, u32[]{:S(2)}) collective-permute-start(bf16[144,768]{1,0:T(8,128)(2,1)S(1)} %get-tuple-element.64), channel_id=1, source_target_pairs={{0,16},{1,49},{16,32},{17,1},{32,48},{33,17},{48,0},{49,33},{2,18}... | collective-permute-start | bytes 663560 | tf_op jit(solution)/shard_map/ppermute | solution.py:251
  75.5 10.8 %collective-permute-start.19 = (bf16[144,768]{1,0:T(8,128)(2,1)S(1)}, bf16[144,768]{1,0:T(8,128)(2,1)S(1)}, u32[]{:S(2)}, u32[]{:S(2)}) collective-permute-start(bf16[144,768]{1,0:T(8,128)(2,1)S(1)} %relay.1), channel_id=1, source_target_pairs={{0,48},{1,17},{16,0},{17,33},{32,16},{33,49},{48,32},{49,1},{2,50}... | collective-permute-start | bytes 663560 | tf_op jit(solution)/shard_map/ppermute | solution.py:251
  83.3 9.5 %collective-permute-start.16 = (bf16[144,768]{1,0:T(8,128)(2,1)S(1)}, bf16[144,768]{1,0:T(8,128)(2,1)S(1)}, u32[]{:S(2)}, u32[]{:S(2)}) collective-permute-start(bf16[144,768]{1,0:T(8,128)(2,1)S(1)} %get-tuple-element.57), channel_id=1, source_target_pairs={{0,8},{8,0},{1,9},{9,1},{2,10},{10,2},{3,11},{11,3},{4,12},{12,4},... | collective-permute-start | bytes 663560 | tf_op jit(solution)/shard_map/ppermute | solution.py:358

commit v8 on v7

--- a/solution.py
+++ b/solution.py
@@ -319,7 +319,7 @@
         exps=pairs // 2,
         limit=FORWARD_LIMIT,
     )
-    sts = home([stats] * groups, "zh")
+    sts = [stats] + [turn(stats, groups, -s) for s in range(1, groups)]
     dp1, dp2 = call(
         functools.partial(middle_kernel, heads),
         "middle",

time: 117 us -> 118 us (level)
  starting transfers between devices: 49 us -> 53 us
  waiting for transfers between devices: 27 us -> 23.2 us
    ppermute x15 -> x18, starting transfers between devices: 28.4 us -> 39.7 us  [turn(): return lax.ppermute(x, (axis, 'c'), pairs)]
    ppermute x3 -> x0, starting transfers between devices: 7.94 us -> none  [home(): lax.ppermute(parts[s], axis, shift(n, n - s))]
    ppermute x15 -> x18, waiting for transfers between devices: 17.7 us -> 14.8 us  [turn(): return lax.ppermute(x, (axis, 'c'), pairs)]
where the time goes in v8:
time: 118 us
  starting transfers between devices  53 us (45%)
  blocking collectives  23.8 us (20%)
  waiting for transfers between devices  23.2 us (20%)
  Pallas kernels  15.5 us (13%)
  local copies, waits for them, and re-layouts  1.87 us (2%)
    ppermute x18, starting transfers between devices, turn(): return lax.ppermute(x, (axis, 'c'), pairs)  39.7 us
    all_to_all x1, blocking collectives, on_device(): tops = lax.all_to_all(tops, axes, 0, 0, tiled=True)  23.8 us
    pallas_call x10, Pallas kernels, call(): pl.pallas_call(body, name=name, out_shape=out_shape, scratch_shapes=list(...  15.5 us
    ppermute x18, waiting for transfers between devices, turn(): return lax.ppermute(x, (axis, 'c'), pairs)  14.8 us
    all_to_all x1, starting transfers between devices, on_device(): pk = lax.all_to_all(pk, axes, 0, 0, tiled=True)  11.8 us
    ppermute x1, waiting for transfers between devices, on_device(): got = lax.ppermute(send, 'zl', shift(2, 1))  6.39 us
  transfers between devices with their start and end apart: 21, of which 9 were waited for; matrix products, arithmetic and copies ran while one was open for 0% of the time, Pallas kernels for 6%

profile of v8, /device:TPU:1, one launch (start us, length us, event | category | flops | bytes accessed | tf_op | source)
XLA Modules:
  0.0 118.2 jit_solution(7867486782980638193)
XLA Ops:
  0.6 2.0 %prep.1 = (bf16[144,768]{1,0:T(8,128)(2,1)}, bf16[144,768]{1,0:T(8,128)(2,1)}, f32[256,1,128]{2,1,0:T(1,128)}) custom-call(bf16[144,384]{1,0:T(8,128)(2,1)} %q_ref.1, bf16[144,384]{1,0:T(8,128)(2,1)} %k_ref.1, bf16[144,384]{1,0:T(8,128)(2,1)} %v_ref.1, bf16[144,384]{1,0:T(8,128)(2,1)} %g_ref.1), custom_call_target="tpu_custom_call" | custom-call | bytes 1048576 | tf_op jit(solution)/shard_map/prep/pallas_call | solution.py:32
  2.6 3.9 %collective-permute-start.8 = (bf16[144,768]{1,0:T(8,128)(2,1)}, bf16[144,768]{1,0:T(8,128)(2,1)S(1)}, u32[]{:S(2)}, u32[]{:S(2)}) collective-permute-start(bf16[144,768]{1,0:T(8,128)(2,1)} %get-tuple-element.38.refs_4_), channel_id=1, source_target_pairs={{0,48},{1,17},{16,0},{17,33},{32,16},{33,49},{48,32},{49,1},{2,50}... | collective-permute-start | bytes 663560 | tf_op jit(solution)/shard_map/ppermute | solution.py:251
  6.5 3.1 %collective-permute-start.4 = (bf16[144,768]{1,0:T(8,128)(2,1)}, bf16[144,768]{1,0:T(8,128)(2,1)S(1)}, u32[]{:S(2)}, u32[]{:S(2)}) collective-permute-start(bf16[144,768]{1,0:T(8,128)(2,1)} %get-tuple-element.38.refs_4_), channel_id=1, source_target_pairs={{0,16},{1,49},{16,32},{17,1},{32,48},{33,17},{48,0},{49,33},{2,18}... | collective-permute-start | bytes 663560 | tf_op jit(solution)/shard_map/ppermute | solution.py:251
  10.4 2.5 %collective-permute-start.7 = (bf16[144,768]{1,0:T(8,128)(2,1)}, bf16[144,768]{1,0:T(8,128)(2,1)S(1)}, u32[]{:S(2)}, u32[]{:S(2)}) collective-permute-start(bf16[144,768]{1,0:T(8,128)(2,1)} %get-tuple-element.37.refs_0_), channel_id=1, source_target_pairs={{0,64},{1,193},{64,128},{65,1},{128,192},{129,65},{192,0},{193,129... | collective-permute-start | bytes 663560 | tf_op jit(solution)/shard_map/ppermute | solution.py:251
  12.9 11.8 %all-to-all-start = ((f32[256,1,128]{2,1,0:T(1,128)}), f32[256,1,128]{2,1,0:T(1,128)S(1)}, u32[]{:S(2)}, u32[]{:S(2)}) async-start(f32[256,1,128]{2,1,0:T(1,128)} %get-tuple-element.39), calls=%async_computation | async-start | bytes 262144 | tf_op jit(solution)/shard_map/all_to_all | solution.py:295
  24.7 3.0 %collective-permute-start.5 = (bf16[144,768]{1,0:T(8,128)(2,1)}, bf16[144,768]{1,0:T(8,128)(2,1)S(1)}, u32[]{:S(2)}, u32[]{:S(2)}) collective-permute-start(bf16[144,768]{1,0:T(8,128)(2,1)} %get-tuple-element.37.refs_0_), channel_id=1, source_target_pairs={{0,128},{1,129},{64,192},{65,193},{128,0},{129,1},{192,64},{193,65... | collective-permute-start | bytes 663560 | tf_op jit(solution)/shard_map/ppermute | solution.py:251
  27.6 4.8 %collective-permute-start.9 = (bf16[144,768]{1,0:T(8,128)(2,1)S(1)}, bf16[144,768]{1,0:T(8,128)(2,1)S(1)}, u32[]{:S(2)}, u32[]{:S(2)}) collective-permute-start(bf16[144,768]{1,0:T(8,128)(2,1)S(1)} %collective-permute-done.4.refs_1_), channel_id=1, source_target_pairs={{0,16},{1,49},{16,32},{17,1},{32,48},{33,17},{48,0},{49,33},{2,18}... | collective-permute-start | bytes 663560 | tf_op jit(solution)/shard_map/ppermute | solution.py:251
  32.7 1.8 %collective-permute-start.2 = (bf16[144,768]{1,0:T(8,128)(2,1)S(1)}, bf16[144,768]{1,0:T(8,128)(2,1)S(1)}, u32[]{:S(2)}, u32[]{:S(2)}) collective-permute-start(bf16[144,768]{1,0:T(8,128)(2,1)S(1)} %collective-permute-done.refs_0_), channel_id=1, source_target_pairs={{0,128},{1,129},{64,192},{65,193},{128,0},{129,1},{192,64},{193,65... | collective-permute-start | bytes 663560 | tf_op jit(solution)/shard_map/ppermute | solution.py:251
  35.5 2.0 %all-to-all-done.refs_8_ = f32[256,1,128]{2,1,0:T(1,128)S(1)} async-done(((f32[256,1,128]{2,1,0:T(1,128)}), f32[256,1,128]{2,1,0:T(1,128)S(1)}, u32[]{:S(2)}, u32[]{:S(2)}) %all-to-all-start) | async-done | bytes 131104 | tf_op jit(solution)/shard_map/all_to_all | solution.py:295
  37.7 0.9 copy-done
  38.6 0.9 copy-done.1
  39.6 3.2 %near.1 = (bf16[576,384]{1,0:T(8,128)(2,1)S(1)}, bf16[576,384]{1,0:T(8,128)(2,1)S(1)}, bf16[576,384]{1,0:T(8,128)(2,1)S(1)}, bf16[576,384]{1,0:T(8,128)(2,1)S(1)...) custom-call(s32[2]{0:T(128)S(1)} %pad_add_fusion.at_ref, ...), custom_call_target="tpu_custom_call" | custom-call | flops 509607936 | bytes 4194304 | tf_op jit(solution)/shard_map/near/pallas_call | solution.py:32
  42.8 1.8 %collective-permute-done.3.refs_3_ = bf16[144,768]{1,0:T(8,128)(2,1)S(1)} collective-permute-done((bf16[144,768]{1,0:T(8,128)(2,1)S(1)}, bf16[144,768]{1,0:T(8,128)(2,1)S(1)}, u32[]{:S(2)}, u32[]{:S(2)}) %collective-permute-start.3) | collective-permute-done | bytes 221216 | tf_op jit(solution)/shard_map/ppermute | solution.py:251
  44.6 2.4 %far.1 = (bf16[576,384]{1,0:T(8,128)(2,1)S(1)}, bf16[576,384]{1,0:T(8,128)(2,1)S(1)}, bf16[3,576,576]{2,1,0:T(8,128)(2,1)S(1)}, f32[384,576]{1,0:T(8,128)S(1)}, ...) custom-call(bf16[144,768]{1,0:T(8,128)(2,1)S(1)} %collective-permute-done.refs_0_, ...), custom_call_target="tpu_custom_call" | custom-call | flops 509607936 | bytes 4194304 | tf_op jit(solution)/shard_map/far/pallas_call | solution.py:32
  47.0 3.5 %collective-permute-start.12 = (f32[8,576]{1,0:T(8,128)S(1)}, f32[8,576]{1,0:T(8,128)S(1)}, u32[]{:S(2)}, u32[]{:S(2)}) collective-permute-start(f32[8,576]{1,0:T(8,128)S(1)} %get-tuple-element.44.refs_0_), channel_id=1, source_target_pairs={{0,16},{1,49},{16,32},{17,1},{32,48},{33,17},{48,0},{49,33},{2,18}... | collective-permute-start | bytes 55304 | tf_op jit(solution)/shard_map/ppermute | solution.py:251
  50.5 1.2 %collective-permute-start.11 = (f32[8,576]{1,0:T(8,128)S(1)}, f32[8,576]{1,0:T(8,128)S(1)}, u32[]{:S(2)}, u32[]{:S(2)}) collective-permute-start(f32[8,576]{1,0:T(8,128)S(1)} %get-tuple-element.44.refs_0_), channel_id=1, source_target_pairs={{0,32},{1,33},{16,48},{17,49},{32,0},{33,1},{48,16},{49,17},{2,34}... | collective-permute-start | bytes 55304 | tf_op jit(solution)/shard_map/ppermute | solution.py:251
  51.8 2.0 %collective-permute-start.10 = (f32[8,576]{1,0:T(8,128)S(1)}, f32[8,576]{1,0:T(8,128)S(1)}, u32[]{:S(2)}, u32[]{:S(2)}) collective-permute-start(f32[8,576]{1,0:T(8,128)S(1)} %get-tuple-element.44.refs_0_), channel_id=1, source_target_pairs={{0,48},{1,17},{16,0},{17,33},{32,16},{33,49},{48,32},{49,1},{2,50}... | collective-permute-start | bytes 55304 | tf_op jit(solution)/shard_map/ppermute | solution.py:251
  53.8 1.3 %middle.1 = (f32[3,576,576]{2,1,0:T(8,128)S(1)}, f32[3,576,576]{2,1,0:T(8,128)S(1)}) custom-call(bf16[576,384]{1,0:T(8,128)(2,1)S(1)} %get-tuple-element.41.refs_5_.gs, bf16[576,384]{1,0:T(8,128)(2,1)S(1)} %get-tuple-element.48.vb1, bf16[576,384]{1,0:T(8,128)(2,1)S(1)} %get-tuple-element.49.vb2), custom_call_target="tpu_custom_call" | custom-call | flops 509607936 | bytes 8388608 | tf_op jit(solution)/shard_map/middle/pallas_call | solution.py:32
  55.1 2.7 %collective-permute-done.11.refs_2_ = f32[8,576]{1,0:T(8,128)S(1)} collective-permute-done((f32[8,576]{1,0:T(8,128)S(1)}, f32[8,576]{1,0:T(8,128)S(1)}, u32[]{:S(2)}, u32[]{:S(2)}) %collective-permute-start.11) | collective-permute-done | bytes 18464 | tf_op jit(solution)/shard_map/ppermute | solution.py:251
  57.7 3.1 %keys.1 = (bf16[3,576,576]{2,1,0:T(8,128)(2,1)S(1)}, bf16[3,576,576]{2,1,0:T(8,128)(2,1)S(1)}, bf16[288,768]{1,0:T(8,128)(2,1)S(1)}, bf16[288,768]{1,0:T(8,128)(...) custom-call(f32[8,576]{1,0:T(8,128)S(1)} %get-tuple-element.44.refs_0_, ...), custom_call_target="tpu_custom_call" | custom-call | flops 1019215872 | bytes 6291456 | tf_op jit(solution)/shard_map/keys/pallas_call | solution.py:32
  60.9 0.9 collective-permute-start.13
  61.8 2.6 %collective-permute-start.14 = (bf16[288,768]{1,0:T(8,128)(2,1)S(1)}, bf16[288,768]{1,0:T(8,128)(2,1)S(1)}, u32[]{:S(2)}, u32[]{:S(2)}) collective-permute-start(bf16[288,768]{1,0:T(8,128)(2,1)S(1)} %get-tuple-element.54), channel_id=1, source_target_pairs={{0,128},{1,129},{64,192},{65,193},{128,0},{129,1},{192,64},{193,65... | collective-permute-start | bytes 1327112 | tf_op jit(solution)/shard_map/ppermute | solution.py:251
  65.3 1.9 %queries.1 = (bf16[144,768]{1,0:T(8,128)(2,1)S(1)}, bf16[144,768]{1,0:T(8,128)(2,1)S(1)}, bf16[144,768]{1,0:T(8,128)(2,1)S(1)}, bf16[144,768]{1,0:T(8,128)(2,1)S(1)}) custom-call(s32[2]{0:T(128)S(1)} %pad_add_fusion.at_ref, f32[8,576]{1,0:T(8,128)S(1)} %get-tuple-element.44.refs_0_, f32[8,576]{1,0:T(8,128)S(1)} %collective-permute-done.10.refs_1_, ...), custom_call_target="tpu_custom_call" | custom-call | flops 509607936 | bytes 6291456 | tf_op jit(solution)/shard_map/queries/pallas_call | solution.py:32
  67.8 3.1 %collective-permute-start.17 = (bf16[144,768]{1,0:T(8,128)(2,1)S(1)}, bf16[144,768]{1,0:T(8,128)(2,1)S(1)}, u32[]{:S(2)}, u32[]{:S(2)}) collective-permute-start(bf16[144,768]{1,0:T(8,128)(2,1)S(1)} %get-tuple-element.64), channel_id=1, source_target_pairs={{0,16},{1,49},{16,32},{17,1},{32,48},{33,17},{48,0},{49,33},{2,18}... | collective-permute-start | bytes 663560 | tf_op jit(solution)/shard_map/ppermute | solution.py:251
  70.9 3.7 %collective-permute-done.18.b_ref = bf16[144,768]{1,0:T(8,128)(2,1)S(1)} collective-permute-done((bf16[144,768]{1,0:T(8,128)(2,1)S(1)}, bf16[144,768]{1,0:T(8,128)(2,1)S(1)}, u32[]{:S(2)}, u32[]{:S(2)}) %collective-permute-start.18) | collective-permute-done | bytes 221216 | tf_op jit(solution)/shard_map/ppermute | solution.py:251
  74.7 4.6 %collective-permute-start.19 = (bf16[144,768]{1,0:T(8,128)(2,1)S(1)}, bf16[144,768]{1,0:T(8,128)(2,1)S(1)}, u32[]{:S(2)}, u32[]{:S(2)}) collective-permute-start(bf16[144,768]{1,0:T(8,128)(2,1)S(1)} %relay.1), channel_id=1, source_target_pairs={{0,48},{1,17},{16,0},{17,33},{32,16},{33,49},{48,32},{49,1},{2,50}... | collective-permute-start | bytes 663560 | tf_op jit(solution)/shard_map/ppermute | solution.py:251
  79.3 1.3 %collective-permute-done.14.refs_2_ = bf16[288,768]{1,0:T(8,128)(2,1)S(1)} collective-permute-done((bf16[288,768]{1,0:T(8,128)(2,1)S(1)}, bf16[288,768]{1,0:T(8,128)(2,1)S(1)}, u32[]{:S(2)}, u32[]{:S(2)}) %collective-permute-start.14) | collective-permute-done | bytes 442400 | tf_op jit(solution)/shard_map/ppermute | solution.py:251
  80.6 3.6 %collective-permute-done.15.refs_3_ = bf16[288,768]{1,0:T(8,128)(2,1)S(1)} collective-permute-done((bf16[288,768]{1,0:T(8,128)(2,1)S(1)}, bf16[288,768]{1,0:T(8,128)(2,1)S(1)}, u32[]{:S(2)}, u32[]{:S(2)}) %collective-permute-start.15) | collective-permute-done | bytes 442400 | tf_op jit(solution)/shard_map/ppermute | solution.py:251
  85.2 1.5 %collective-permute-done.19.refs_2_ = bf16[144,768]{1,0:T(8,128)(2,1)S(1)} collective-permute-done((bf16[144,768]{1,0:T(8,128)(2,1)S(1)}, bf16[144,768]{1,0:T(8,128)(2,1)S(1)}, u32[]{:S(2)}, u32[]{:S(2)}) %collective-permute-start.19) | collective-permute-done | bytes 221216 | tf_op jit(solution)/shard_map/ppermute | solution.py:251
  86.7 6.4 %collective-permute-done.16.got_ref = bf16[144,768]{1,0:T(8,128)(2,1)S(1)} collective-permute-done((bf16[144,768]{1,0:T(8,128)(2,1)S(1)}, bf16[144,768]{1,0:T(8,128)(2,1)S(1)}, u32[]{:S(2)}, u32[]{:S(2)}) %collective-permute-start.16) | collective-permute-done | bytes 221216 | tf_op jit(solution)/shard_map/ppermute | solution.py:358
  93.4 23.8 %all_to_all.10.pk_ref = f32[256,1,128]{2,1,0:T(1,128)S(1)} all-to-all(f32[256,1,128]{2,1,0:T(1,128)S(1)} %get-tuple-element.69), channel_id=1, replica_groups=mesh['x'=4,'zh'=4,'zl'=2,'y'=4,'c'=2] {'x','zh','zl','y','c'}, dimensions={0} | all-to-all | bytes 262144 | tf_op jit(solution)/shard_map/all_to_all | solution.py:366
  117.3 0.9 cast.1
  (26 shorter events, 5.1 us)
Async XLA Ops:
  2.6 22.0 %collective-permute-start.8 = (bf16[144,768]{1,0:T(8,128)(2,1)}, bf16[144,768]{1,0:T(8,128)(2,1)S(1)}, u32[]{:S(2)}, u32[]{:S(2)}) collective-permute-start(bf16[144,768]{1,0:T(8,128)(2,1)} %get-tuple-element.38.refs_4_), channel_id=1, source_target_pairs={{0,48},{1,17},{16,0},{17,33},{32,16},{33,49},{48,32},{49,1},{2,50}... | collective-permute-start | bytes 663560 | tf_op jit(solution)/shard_map/ppermute | solution.py:251
  6.5 21.1 %collective-permute-start.4 = (bf16[144,768]{1,0:T(8,128)(2,1)}, bf16[144,768]{1,0:T(8,128)(2,1)S(1)}, u32[]{:S(2)}, u32[]{:S(2)}) collective-permute-start(bf16[144,768]{1,0:T(8,128)(2,1)} %get-tuple-element.38.refs_4_), channel_id=1, source_target_pairs={{0,16},{1,49},{16,32},{17,1},{32,48},{33,17},{48,0},{49,33},{2,18}... | collective-permute-start | bytes 663560 | tf_op jit(solution)/shard_map/ppermute | solution.py:251
  9.6 22.8 %collective-permute-start = (bf16[144,768]{1,0:T(8,128)(2,1)}, bf16[144,768]{1,0:T(8,128)(2,1)S(1)}, u32[]{:S(2)}, u32[]{:S(2)}) collective-permute-start(bf16[144,768]{1,0:T(8,128)(2,1)} %get-tuple-element.37.refs_0_), channel_id=1, source_target_pairs={{0,8},{8,0},{1,9},{9,1},{2,10},{10,2},{3,11},{11,3},{4,12},{12,4},... | collective-permute-start | bytes 663560 | tf_op jit(solution)/shard_map/ppermute | solution.py:288
  10.4 22.4 %collective-permute-start.7 = (bf16[144,768]{1,0:T(8,128)(2,1)}, bf16[144,768]{1,0:T(8,128)(2,1)S(1)}, u32[]{:S(2)}, u32[]{:S(2)}) collective-permute-start(bf16[144,768]{1,0:T(8,128)(2,1)} %get-tuple-element.37.refs_0_), channel_id=1, source_target_pairs={{0,64},{1,193},{64,128},{65,1},{128,192},{129,65},{192,0},{193,129... | collective-permute-start | bytes 663560 | tf_op jit(solution)/shard_map/ppermute | solution.py:251
  12.8 21.7 %collective-permute-start.6 = (bf16[144,768]{1,0:T(8,128)(2,1)}, bf16[144,768]{1,0:T(8,128)(2,1)S(1)}, u32[]{:S(2)}, u32[]{:S(2)}) collective-permute-start(bf16[144,768]{1,0:T(8,128)(2,1)} %get-tuple-element.37.refs_0_), channel_id=1, source_target_pairs={{0,192},{1,65},{64,0},{65,129},{128,64},{129,193},{192,128},{193,1... | collective-permute-start | bytes 663560 | tf_op jit(solution)/shard_map/ppermute | solution.py:251
  12.9 24.6 %all-to-all-start = ((f32[256,1,128]{2,1,0:T(1,128)}), f32[256,1,128]{2,1,0:T(1,128)S(1)}, u32[]{:S(2)}, u32[]{:S(2)}) async-start(f32[256,1,128]{2,1,0:T(1,128)} %get-tuple-element.39), calls=%async_computation | async-start | bytes 262144 | tf_op jit(solution)/shard_map/all_to_all | solution.py:295
  24.7 10.8 %collective-permute-start.5 = (bf16[144,768]{1,0:T(8,128)(2,1)}, bf16[144,768]{1,0:T(8,128)(2,1)S(1)}, u32[]{:S(2)}, u32[]{:S(2)}) collective-permute-start(bf16[144,768]{1,0:T(8,128)(2,1)} %get-tuple-element.37.refs_0_), channel_id=1, source_target_pairs={{0,128},{1,129},{64,192},{65,193},{128,0},{129,1},{192,64},{193,65... | collective-permute-start | bytes 663560 | tf_op jit(solution)/shard_map/ppermute | solution.py:251
  27.6 10.0 %collective-permute-start.9 = (bf16[144,768]{1,0:T(8,128)(2,1)S(1)}, bf16[144,768]{1,0:T(8,128)(2,1)S(1)}, u32[]{:S(2)}, u32[]{:S(2)}) collective-permute-start(bf16[144,768]{1,0:T(8,128)(2,1)S(1)} %collective-permute-done.4.refs_1_), channel_id=1, source_target_pairs={{0,16},{1,49},{16,32},{17,1},{32,48},{33,17},{48,0},{49,33},{2,18}... | collective-permute-start | bytes 663560 | tf_op jit(solution)/shard_map/ppermute | solution.py:251
  32.4 12.2 %collective-permute-start.3 = (bf16[144,768]{1,0:T(8,128)(2,1)S(1)}, bf16[144,768]{1,0:T(8,128)(2,1)S(1)}, u32[]{:S(2)}, u32[]{:S(2)}) collective-permute-start(bf16[144,768]{1,0:T(8,128)(2,1)S(1)} %collective-permute-done.refs_0_), channel_id=1, source_target_pairs={{0,192},{1,65},{64,0},{65,129},{128,64},{129,193},{192,128},{193,1... | collective-permute-start | bytes 663560 | tf_op jit(solution)/shard_map/ppermute | solution.py:251
  32.7 11.9 %collective-permute-start.2 = (bf16[144,768]{1,0:T(8,128)(2,1)S(1)}, bf16[144,768]{1,0:T(8,128)(2,1)S(1)}, u32[]{:S(2)}, u32[]{:S(2)}) collective-permute-start(bf16[144,768]{1,0:T(8,128)(2,1)S(1)} %collective-permute-done.refs_0_), channel_id=1, source_target_pairs={{0,128},{1,129},{64,192},{65,193},{128,0},{129,1},{192,64},{193,65... | collective-permute-start | bytes 663560 | tf_op jit(solution)/shard_map/ppermute | solution.py:251
  34.5 10.1 %collective-permute-start.1 = (bf16[144,768]{1,0:T(8,128)(2,1)S(1)}, bf16[144,768]{1,0:T(8,128)(2,1)S(1)}, u32[]{:S(2)}, u32[]{:S(2)}) collective-permute-start(bf16[144,768]{1,0:T(8,128)(2,1)S(1)} %collective-permute-done.refs_0_), channel_id=1, source_target_pairs={{0,64},{1,193},{64,128},{65,1},{128,192},{129,65},{192,0},{193,129... | collective-permute-start | bytes 663560 | tf_op jit(solution)/shard_map/ppermute | solution.py:251
  37.7 0.9 copy-start
  38.6 0.9 copy-start.1
  47.0 8.1 %collective-permute-start.12 = (f32[8,576]{1,0:T(8,128)S(1)}, f32[8,576]{1,0:T(8,128)S(1)}, u32[]{:S(2)}, u32[]{:S(2)}) collective-permute-start(f32[8,576]{1,0:T(8,128)S(1)} %get-tuple-element.44.refs_0_), channel_id=1, source_target_pairs={{0,16},{1,49},{16,32},{17,1},{32,48},{33,17},{48,0},{49,33},{2,18}... | collective-permute-start | bytes 55304 | tf_op jit(solution)/shard_map/ppermute | solution.py:251
  50.5 7.2 %collective-permute-start.11 = (f32[8,576]{1,0:T(8,128)S(1)}, f32[8,576]{1,0:T(8,128)S(1)}, u32[]{:S(2)}, u32[]{:S(2)}) collective-permute-start(f32[8,576]{1,0:T(8,128)S(1)} %get-tuple-element.44.refs_0_), channel_id=1, source_target_pairs={{0,32},{1,33},{16,48},{17,49},{32,0},{33,1},{48,16},{49,17},{2,34}... | collective-permute-start | bytes 55304 | tf_op jit(solution)/shard_map/ppermute | solution.py:251
  51.8 6.0 %collective-permute-start.10 = (f32[8,576]{1,0:T(8,128)S(1)}, f32[8,576]{1,0:T(8,128)S(1)}, u32[]{:S(2)}, u32[]{:S(2)}) collective-permute-start(f32[8,576]{1,0:T(8,128)S(1)} %get-tuple-element.44.refs_0_), channel_id=1, source_target_pairs={{0,48},{1,17},{16,0},{17,33},{32,16},{33,49},{48,32},{49,1},{2,50}... | collective-permute-start | bytes 55304 | tf_op jit(solution)/shard_map/ppermute | solution.py:251
  60.9 18.5 %collective-permute-start.13 = (bf16[288,768]{1,0:T(8,128)(2,1)S(1)}, bf16[288,768]{1,0:T(8,128)(2,1)S(1)}, u32[]{:S(2)}, u32[]{:S(2)}) collective-permute-start(bf16[288,768]{1,0:T(8,128)(2,1)S(1)} %get-tuple-element.53), channel_id=1, source_target_pairs={{0,192},{1,65},{64,0},{65,129},{128,64},{129,193},{192,128},{193,1... | collective-permute-start | bytes 1327112 | tf_op jit(solution)/shard_map/ppermute | solution.py:251
  61.8 18.8 %collective-permute-start.14 = (bf16[288,768]{1,0:T(8,128)(2,1)S(1)}, bf16[288,768]{1,0:T(8,128)(2,1)S(1)}, u32[]{:S(2)}, u32[]{:S(2)}) collective-permute-start(bf16[288,768]{1,0:T(8,128)(2,1)S(1)} %get-tuple-element.54), channel_id=1, source_target_pairs={{0,128},{1,129},{64,192},{65,193},{128,0},{129,1},{192,64},{193,65... | collective-permute-start | bytes 1327112 | tf_op jit(solution)/shard_map/ppermute | solution.py:251
  64.4 19.8 %collective-permute-start.15 = (bf16[288,768]{1,0:T(8,128)(2,1)S(1)}, bf16[288,768]{1,0:T(8,128)(2,1)S(1)}, u32[]{:S(2)}, u32[]{:S(2)}) collective-permute-start(bf16[288,768]{1,0:T(8,128)(2,1)S(1)} %get-tuple-element.55), channel_id=1, source_target_pairs={{0,64},{1,193},{64,128},{65,1},{128,192},{129,65},{192,0},{193,129... | collective-permute-start | bytes 1327112 | tf_op jit(solution)/shard_map/ppermute | solution.py:251
  67.2 7.4 %collective-permute-start.18 = (bf16[144,768]{1,0:T(8,128)(2,1)S(1)}, bf16[144,768]{1,0:T(8,128)(2,1)S(1)}, u32[]{:S(2)}, u32[]{:S(2)}) collective-permute-start(bf16[144,768]{1,0:T(8,128)(2,1)S(1)} %get-tuple-element.66), channel_id=1, source_target_pairs={{0,48},{1,17},{16,0},{17,33},{32,16},{33,49},{48,32},{49,1},{2,50}... | collective-permute-start | bytes 663560 | tf_op jit(solution)/shard_map/ppermute | solution.py:251
  67.8 17.5 %collective-permute-start.17 = (bf16[144,768]{1,0:T(8,128)(2,1)S(1)}, bf16[144,768]{1,0:T(8,128)(2,1)S(1)}, u32[]{:S(2)}, u32[]{:S(2)}) collective-permute-start(bf16[144,768]{1,0:T(8,128)(2,1)S(1)} %get-tuple-element.64), channel_id=1, source_target_pairs={{0,16},{1,49},{16,32},{17,1},{32,48},{33,17},{48,0},{49,33},{2,18}... | collective-permute-start | bytes 663560 | tf_op jit(solution)/shard_map/ppermute | solution.py:251
  74.7 12.1 %collective-permute-start.19 = (bf16[144,768]{1,0:T(8,128)(2,1)S(1)}, bf16[144,768]{1,0:T(8,128)(2,1)S(1)}, u32[]{:S(2)}, u32[]{:S(2)}) collective-permute-start(bf16[144,768]{1,0:T(8,128)(2,1)S(1)} %relay.1), channel_id=1, source_target_pairs={{0,48},{1,17},{16,0},{17,33},{32,16},{33,49},{48,32},{49,1},{2,50}... | collective-permute-start | bytes 663560 | tf_op jit(solution)/shard_map/ppermute | solution.py:251
  84.4 8.7 %collective-permute-start.16 = (bf16[144,768]{1,0:T(8,128)(2,1)S(1)}, bf16[144,768]{1,0:T(8,128)(2,1)S(1)}, u32[]{:S(2)}, u32[]{:S(2)}) collective-permute-start(bf16[144,768]{1,0:T(8,128)(2,1)S(1)} %get-tuple-element.57), channel_id=1, source_target_pairs={{0,8},{8,0},{1,9},{9,1},{2,10},{10,2},{3,11},{11,3},{4,12},{12,4},... | collective-permute-start | bytes 663560 | tf_op jit(solution)/shard_map/ppermute | solution.py:358
